TPU v7x, 512 devices: a whole 4x8x8 slice. The times are simulated.
512 devices in a mesh: tile: 128 (over y, z, core), mem: 4 (over x).
Axes of the slice: x: 4, y: 8, z: 8, core: 2. Of those that a mesh axis runs over, the one named last changes fastest.
Arguments:
- background: bfloat16 [1792, 80, 512], P('tile', 'mem'), may hold values from -6 to 6
- obs_ens: bfloat16 [1792, 80, 128], P('tile', 'mem'), may hold values from -6 to 6
- innovation: float32 [1792, 128], P('tile'), may hold values from -6 to 6
- precision: float32 [1792, 128], P('tile'), may hold values from 0.1 to 2
- loc_weight: float32 [1792, 7], P('tile'), may hold values from 0.1 to 1
- old_split: int32 [129], replicated, may hold values from 0 to 1024, as said below
- new_split: int32 [129], replicated, may hold values from 0 to 1024, as said below
- obs_count: int32 [1792], P('tile'), may hold values from 32 to 128
- halo_tiles: int32 [128, 12], replicated, may hold values from 0 to 1023, as said below
- region_list: int32 [1792, 7], P('tile'), may hold values from 0 to 25, as said below
Outputs:
- analysis: bfloat16 [1792, 80, 512], P('tile', 'mem')
Inputs may be any that keep to these rules, and one draw needn't show every extreme that they name: old_split[0] = 0 and old_split[128] = 1024; each device holds between 2 and 14 old tiles, exactly 14 on some device. new_split[0] = 0 and new_split[128] = 1024; each device holds between 6 and 10 new tiles; every new_split[d] differs from old_split[d] by at most 2, by exactly 2 for some d. `halo_tiles`: row d is 3 groups of 4 entries; a group holds distinct tiles in rising order that one device p other than d holds under new_split, with p within 3 of d, and the 3 devices of a row are distinct. `region_list`: for a slot of device d, an entry r < 14 names d's slot r, which is live; an entry r >= 14 names the tile halo_tiles[d, r - 14].
All inputs are finite; a program needn't handle non-finite values.
Results may differ from a plain program's by a relative error of at most 0.0057.
Values may be sent and summed in bfloat16 or wider, within the bound.
No kernel may reach another device: no remote copies, remote signals or barrier semaphores. Data moves between devices by JAX's collectives and lax.ppermute only.
A program may use at most 64 MiB of HBM per device.

v0:
```python
import math

import jax
import jax.numpy as jnp
from jax import lax
from jax.sharding import PartitionSpec as P

TILE_MEAN = 8
MOVE = 2
REACH = 3
HPEER = 3
HCAP = 4
NS_ITERS = 6


inflation = 1.1
exact = lax.Precision.HIGHEST


def from_behind(value, axis, steps):
    count = lax.axis_size(axis)
    first, last = (max(0, -steps), min(count, count - steps))
    return lax.ppermute(value, axis, [(source, source + steps) for source in range(first, last)])


def joined_along(parts, dim):
    shape = list(parts.shape[1:])
    shape[dim] *= parts.shape[0]
    return jnp.moveaxis(parts, 0, dim).reshape(shape)


def sent_to_all(x, axis):
    count = lax.axis_size(axis)
    return lax.all_to_all(jnp.broadcast_to(x[None], (count, *x.shape)), axis, 0, 0, tiled=True)


def collect(x, axis, dim):
    return joined_along(sent_to_all(x, axis), dim)


def owner_of(split_points, position):
    bounds = split_points[1:]
    return jnp.sum((bounds[None, :] <= position[:, None]).astype(jnp.int32), axis=1)


def pick_slots(wanted, range_start, range_end, capacity):
    leading = wanted[..., 0]
    owned_flag = ((leading >= range_start) & (leading < range_end)).astype(jnp.int32)
    rows_here = jnp.sum(owned_flag[..., None] * (wanted - range_start), axis=-2)
    return jnp.clip(rows_here, 0, capacity - 1)


def inverse_root(system, repeats):
    identity = jnp.eye(system.shape[-1], dtype=system.dtype)
    frobenius = jnp.sqrt(jnp.sum(system * system, axis=(1, 2)))
    root_part = system / frobenius[:, None, None]
    inverse_part = jnp.broadcast_to(identity, system.shape)
    for repeat in range(repeats):
        middle = 0.5 * (
            3.0 * identity - jnp.einsum("pij,pjk->pik", inverse_part, root_part, precision=exact)
        )
        root_part = jnp.einsum("pij,pjk->pik", root_part, middle, precision=exact)
        inverse_part = jnp.einsum("pij,pjk->pik", middle, inverse_part, precision=exact)
    return (inverse_part, frobenius)


def weighted_gram(region, region_pulled, row_weights):
    products = jnp.einsum("pekn,pejn->pekj", region, region, preferred_element_type=jnp.float32)
    gram_matrix = jnp.sum(row_weights[:, :, None, None] * products, axis=1)
    pull_terms = jnp.einsum(
        "pekn,pen->pek", region, region_pulled, preferred_element_type=jnp.float32
    )
    return (gram_matrix, jnp.sum(row_weights[:, :, None] * pull_terms, axis=1))


def shards(
    background,
    obs_ens,
    innovation,
    precision,
    loc_weight,
    old_split,
    new_split,
    obs_count,
    halo_tiles,
    region_list,
):
    capacity = background.shape[0]
    members_here = background.shape[1]
    state_width = background.shape[2]
    obs_slots = obs_ens.shape[2]
    devices = lax.axis_size("tile")
    ensemble = members_here * lax.axis_size("mem")
    myself = lax.axis_index("tile")
    member_rank = lax.axis_index("mem")
    old_start = old_split[myself]
    old_end = old_split[myself + 1]
    new_start = new_split[myself]
    new_end = new_split[myself + 1]
    slot_index = jnp.arange(capacity, dtype=jnp.int32)
    position = new_start + slot_index
    going_right = lax.dynamic_slice_in_dim(background, old_end - old_start - MOVE, MOVE, 0)
    going_left = background[:MOVE]
    from_left = from_behind(going_right, "tile", 1)
    from_right = from_behind(going_left, "tile", -1)
    left_index = position - old_start + MOVE
    right_index = MOVE + capacity + position - old_end
    left_size = MOVE
    combined = jnp.concatenate([from_left, background, from_right], axis=0)
    own_index = left_size + position - old_start
    source = jnp.where(
        position < old_start, left_index, jnp.where(position < old_end, own_index, right_index)
    )
    source = jnp.clip(source, 0, combined.shape[0] - 1)
    migrated = jnp.take(combined, source, axis=0)
    live_obs = (jnp.arange(obs_slots, dtype=jnp.int32)[None, :] < obs_count[:, None]).astype(
        jnp.float32
    )
    root_weight = jnp.sqrt(precision * live_obs)
    scaled = (obs_ens * root_weight[:, None, :]).astype(jnp.bfloat16)
    pulled = (root_weight * innovation).astype(jnp.bfloat16)
    groups = halo_tiles.reshape(devices, HPEER, HCAP)
    mine_groups = groups[myself]
    source_peer = owner_of(new_split, mine_groups[:, 0])
    halo_scaled = jnp.zeros((HPEER, HCAP, members_here, obs_slots), jnp.bfloat16)
    halo_pulled = jnp.zeros((HPEER, HCAP, obs_slots), jnp.bfloat16)
    for offset in list(range(-REACH, 0)) + list(range(1, REACH + 1)):
        reader = jnp.clip(myself - offset, 0, devices - 1)
        chosen_rows = pick_slots(groups[reader], new_start, new_end, capacity)
        arrived = from_behind((scaled[chosen_rows], pulled[chosen_rows]), "tile", -offset)
        matches = source_peer == myself + offset
        halo_scaled = jnp.where(matches[:, None, None, None], arrived[0][None], halo_scaled)
        halo_pulled = jnp.where(matches[:, None, None], arrived[1][None], halo_pulled)
    halo_count = halo_scaled.shape[0] * halo_scaled.shape[1]
    table_scaled = jnp.concatenate(
        [scaled, halo_scaled.reshape(halo_count, members_here, obs_slots)], axis=0
    )
    table_pulled = jnp.concatenate([pulled, halo_pulled.reshape(halo_count, obs_slots)], axis=0)
    full_table = collect(table_scaled, "mem", 1)
    entries = jnp.concatenate([slot_index[:, None], region_list], axis=1)
    weights = jnp.concatenate([jnp.ones((capacity, 1), jnp.float32), loc_weight], axis=1)
    per_block = capacity * 4 // TILE_MEAN
    live_count = new_end - new_start
    block_count = capacity // per_block
    identity = jnp.eye(ensemble, dtype=jnp.float32)
    column_start = member_rank * members_here

    def analyse(block_index, output):
        first_slot = block_index * per_block
        region_rows = lax.dynamic_slice_in_dim(entries, first_slot, per_block, 0)
        row_weights = lax.dynamic_slice_in_dim(weights, first_slot, per_block, 0)
        region_pulled = table_pulled[region_rows]
        gram_matrix, pull_sum = weighted_gram(full_table[region_rows], region_pulled, row_weights)
        system = gram_matrix + (ensemble - 1) / inflation * identity
        inverse, frobenius = inverse_root(system, NS_ITERS)
        spread = (math.sqrt(ensemble - 1) / jnp.sqrt(frobenius))[:, None, None] * inverse
        half_way = jnp.einsum("pij,pj->pi", inverse, pull_sum, precision=exact)
        mean_weight = (
            jnp.einsum("pij,pj->pi", inverse, half_way, precision=exact) / frobenius[:, None]
        )
        transform = (spread + mean_weight[:, :, None]).astype(jnp.bfloat16)
        columns = lax.dynamic_slice_in_dim(transform, column_start, members_here, 2)
        keep_share = 1.0 - jnp.sum(columns.astype(jnp.float32), axis=1)
        state_block = lax.dynamic_slice_in_dim(migrated, first_slot, per_block, 0)
        member_piece = collect(state_block, "mem", 1)
        blended = jnp.einsum(
            "pij,pis->pjs", columns, member_piece, preferred_element_type=jnp.float32
        )
        member_total = jnp.sum(member_piece.astype(jnp.float32), axis=1)
        blended, member_total = (blended, member_total)
        mean_state = member_total / ensemble
        analysis_block = blended + keep_share[:, :, None] * mean_state[:, None, :]
        live_rows = (first_slot + jnp.arange(per_block, dtype=jnp.int32) < live_count)[
            :, None, None
        ]
        result = jnp.where(live_rows, analysis_block, 0.0).astype(jnp.bfloat16)
        return lax.dynamic_update_slice_in_dim(output, result, first_slot, 0)

    output = jnp.zeros((capacity, members_here, state_width), jnp.bfloat16)
    return lax.fori_loop(0, block_count, analyse, output)


def solution(mesh):
    in_specs = (
        P("tile", "mem", None),
        P("tile", "mem", None),
        P("tile", None),
        P("tile", None),
        P("tile", None),
        P(),
        P(),
        P("tile"),
        P(),
        P("tile", None),
    )
    out_specs = P("tile", "mem", None)
    return jax.shard_map(shards, mesh=mesh, in_specs=in_specs, out_specs=out_specs, check_vma=False)
```

profile of v0, /device:TPU:34, one launch (start us, length us, event | category | flops | bytes accessed | tf_op | source)
XLA Modules:
  0.0 146.8 jit_solution(2811899100397912589)
XLA Ops:
  0.9 1.4 fusion.42
  2.3 1.4 convert_reduce_fusion.4
  3.7 0.7 multiply_reduce_fusion.5
  4.5 1.4 convert_reduce_fusion.5
  5.9 0.7 multiply_reduce_fusion.6
  6.7 0.8 multiply_convert_fusion.1
  8.0 1.9 %collective-permute-start.9 = (bf16[4,128]{1,0:T(4,128)(2,1)S(1)}, bf16[4,128]{1,0:T(4,128)(2,1)S(1)}, u32[]{:S(2)}, u32[]{:S(2)}) collective-permute-start(bf16[4,128]{1,0:T(4,128)(2,1)S(1)} %gather_fusion.11), channel_id=1, source_target_pairs={{0,4},{4,8},{8,12},{12,16},{16,20},{20,24},{24,28},{28,32},{32,36}... | collective-permute-start | bytes 3080 | tf_op jit(solution)/shard_map/ppermute | solution.py:23
  10.1 1.4 convert_reduce_fusion.7
  12.3 1.4 convert_reduce_fusion.6
  13.7 0.7 multiply_reduce_fusion.7
  15.0 10.8 %collective-permute-start.7 = (bf16[4,128]{1,0:T(4,128)(2,1)S(1)}, bf16[4,128]{1,0:T(4,128)(2,1)S(1)}, u32[]{:S(2)}, u32[]{:S(2)}) collective-permute-start(bf16[4,128]{1,0:T(4,128)(2,1)S(1)} %gather_fusion.9), channel_id=1, source_target_pairs={{8,0},{12,4},{16,8},{20,12},{24,16},{28,20},{32,24},{36,28},{40,32... | collective-permute-start | bytes 3080 | tf_op jit(solution)/shard_map/ppermute | solution.py:23
  25.9 1.4 convert_reduce_fusion.3
  28.2 1.4 convert_reduce_fusion.2
  29.5 0.7 multiply_reduce_fusion.3
  30.9 1.9 %collective-permute-start.11 = (bf16[4,128]{1,0:T(4,128)(2,1)S(1)}, bf16[4,128]{1,0:T(4,128)(2,1)S(1)}, u32[]{:S(2)}, u32[]{:S(2)}) collective-permute-start(bf16[4,128]{1,0:T(4,128)(2,1)S(1)} %gather_fusion.13), channel_id=1, source_target_pairs={{0,12},{4,16},{8,20},{12,24},{16,28},{20,32},{24,36},{28,40},{32,4... | collective-permute-start | bytes 3080 | tf_op jit(solution)/shard_map/ppermute | solution.py:23
  33.4 3.4 %collective-permute-start.8 = (bf16[4,128]{1,0:T(4,128)(2,1)S(1)}, bf16[4,128]{1,0:T(4,128)(2,1)S(1)}, u32[]{:S(2)}, u32[]{:S(2)}) collective-permute-start(bf16[4,128]{1,0:T(4,128)(2,1)S(1)} %gather_fusion.10), channel_id=1, source_target_pairs={{4,0},{8,4},{12,8},{16,12},{20,16},{24,20},{28,24},{32,28},{36,32}... | collective-permute-start | bytes 3080 | tf_op jit(solution)/shard_map/ppermute | solution.py:23
  36.7 0.9 multiply_convert_fusion
  38.2 6.4 %collective-permute-start = (bf16[4,20,128]{2,1,0:T(8,128)(2,1)S(1)}, bf16[4,20,128]{2,1,0:T(8,128)(2,1)S(1)}, u32[]{:S(2)}, u32[]{:S(2)}) collective-permute-start(bf16[4,20,128]{2,1,0:T(8,128)(2,1)S(1)} %gather_fusion.2), channel_id=1, source_target_pairs={{12,0},{16,4},{20,8},{24,12},{28,16},{32,20},{36,24},{40,28},{44,3... | collective-permute-start | bytes 61448 | tf_op jit(solution)/shard_map/ppermute | solution.py:23
  44.7 0.8 slice.27
  45.4 1.4 fusion.41
  48.1 1.9 %fusion.40 = s32[14]{0:T(128)S(1)} fusion(s32[]{:T(128)} %bitcast.29, s32[]{:T(128)} %bitcast.28, s32[]{:T(128)} %bitcast.1), kind=kLoop, calls=%fused_computation.131 | loop fusion | flops 210 | bytes 68 | tf_op jit(solution)/shard_map/jit(_take)/jit(_where)/select_n | solution.py:115
  50.0 0.8 copy.59
  51.2 1.1 copy.69
  52.5 1.9 %compare_and_fusion = pred[14]{0:T(512)(128)(4,1)S(1)} fusion(s32[]{:T(128)} %bitcast.29, s32[]{:T(128)} %bitcast.28, s32[]{:T(128)} %bitcast.1), kind=kLoop, calls=%fused_computation.120 | loop fusion | flops 252 | bytes 26 | tf_op jit(solution)/shard_map/jit(_take)/and | solution.py:115
  60.5 1.9 %collective-permute-start.6 = (bf16[4,128]{1,0:T(4,128)(2,1)S(1)}, bf16[4,128]{1,0:T(4,128)(2,1)S(1)}, u32[]{:S(2)}, u32[]{:S(2)}) collective-permute-start(bf16[4,128]{1,0:T(4,128)(2,1)S(1)} %gather_fusion.8), channel_id=1, source_target_pairs={{12,0},{16,4},{20,8},{24,12},{28,16},{32,20},{36,24},{40,28},{44,3... | collective-permute-start | bytes 3080 | tf_op jit(solution)/shard_map/ppermute | solution.py:23
  62.5 2.0 %collective-permute-start.10 = (bf16[4,128]{1,0:T(4,128)(2,1)S(1)}, bf16[4,128]{1,0:T(4,128)(2,1)S(1)}, u32[]{:S(2)}, u32[]{:S(2)}) collective-permute-start(bf16[4,128]{1,0:T(4,128)(2,1)S(1)} %gather_fusion.12), channel_id=1, source_target_pairs={{0,8},{4,12},{8,16},{12,20},{16,24},{20,28},{24,32},{28,36},{32,40... | collective-permute-start | bytes 3080 | tf_op jit(solution)/shard_map/ppermute | solution.py:23
  64.8 7.2 %collective-permute-start.1 = (bf16[4,20,128]{2,1,0:T(8,128)(2,1)S(1)}, bf16[4,20,128]{2,1,0:T(8,128)(2,1)S(1)}, u32[]{:S(2)}, u32[]{:S(2)}) collective-permute-start(bf16[4,20,128]{2,1,0:T(8,128)(2,1)S(1)} %gather_fusion.3), channel_id=1, source_target_pairs={{8,0},{12,4},{16,8},{20,12},{24,16},{28,20},{32,24},{36,28},{40,32... | collective-permute-start | bytes 61448 | tf_op jit(solution)/shard_map/ppermute | solution.py:23
  72.0 1.9 %collective-permute-start.2 = (bf16[4,20,128]{2,1,0:T(8,128)(2,1)S(1)}, bf16[4,20,128]{2,1,0:T(8,128)(2,1)S(1)}, u32[]{:S(2)}, u32[]{:S(2)}) collective-permute-start(bf16[4,20,128]{2,1,0:T(8,128)(2,1)S(1)} %gather_fusion.4), channel_id=1, source_target_pairs={{4,0},{8,4},{12,8},{16,12},{20,16},{24,20},{28,24},{32,28},{36,32}... | collective-permute-start | bytes 61448 | tf_op jit(solution)/shard_map/ppermute | solution.py:23
  73.9 2.4 %collective-permute-start.3 = (bf16[4,20,128]{2,1,0:T(8,128)(2,1)S(1)}, bf16[4,20,128]{2,1,0:T(8,128)(2,1)S(1)}, u32[]{:S(2)}, u32[]{:S(2)}) collective-permute-start(bf16[4,20,128]{2,1,0:T(8,128)(2,1)S(1)} %gather_fusion.5), channel_id=1, source_target_pairs={{0,4},{4,8},{8,12},{12,16},{16,20},{20,24},{24,28},{28,32},{32,36}... | collective-permute-start | bytes 61448 | tf_op jit(solution)/shard_map/ppermute | solution.py:23
  76.4 3.1 %collective-permute-start.4 = (bf16[4,20,128]{2,1,0:T(8,128)(2,1)S(1)}, bf16[4,20,128]{2,1,0:T(8,128)(2,1)S(1)}, u32[]{:S(2)}, u32[]{:S(2)}) collective-permute-start(bf16[4,20,128]{2,1,0:T(8,128)(2,1)S(1)} %gather_fusion.6), channel_id=1, source_target_pairs={{0,8},{4,12},{8,16},{12,20},{16,24},{20,28},{24,32},{28,36},{32,40... | collective-permute-start | bytes 61448 | tf_op jit(solution)/shard_map/ppermute | solution.py:23
  79.6 1.9 %collective-permute-start.5 = (bf16[4,20,128]{2,1,0:T(8,128)(2,1)S(1)}, bf16[4,20,128]{2,1,0:T(8,128)(2,1)S(1)}, u32[]{:S(2)}, u32[]{:S(2)}) collective-permute-start(bf16[4,20,128]{2,1,0:T(8,128)(2,1)S(1)} %gather_fusion.7), channel_id=1, source_target_pairs={{0,12},{4,16},{8,20},{12,24},{16,28},{20,32},{24,36},{28,40},{32,4... | collective-permute-start | bytes 61448 | tf_op jit(solution)/shard_map/ppermute | solution.py:23
  81.6 2.0 %collective-permute-start.12 = (bf16[2,20,512]{2,1,0:T(8,128)(2,1)S(1)}, bf16[2,20,512]{2,1,0:T(8,128)(2,1)S(1)}, u32[]{:S(2)}, u32[]{:S(2)}) collective-permute-start(bf16[2,20,512]{2,1,0:T(8,128)(2,1)S(1)} %get-tuple-element.303), channel_id=1, source_target_pairs={{0,4},{4,8},{8,12},{12,16},{16,20},{20,24},{24,28},{28,32},{32,36}... | collective-permute-start | bytes 122888 | tf_op jit(solution)/shard_map/ppermute | solution.py:23
  83.6 6.9 %collective-permute-start.13 = (bf16[2,20,512]{2,1,0:T(8,128)(2,1)S(1)}, bf16[2,20,512]{2,1,0:T(8,128)(2,1)S(1)}, u32[]{:S(2)}, u32[]{:S(2)}) collective-permute-start(bf16[2,20,512]{2,1,0:T(8,128)(2,1)S(1)} %get-tuple-element.304), channel_id=1, source_target_pairs={{4,0},{8,4},{12,8},{16,12},{20,16},{24,20},{28,24},{32,28},{36,32}... | collective-permute-start | bytes 122888 | tf_op jit(solution)/shard_map/ppermute | solution.py:23
  90.7 0.9 broadcast_in_dim.392
  91.6 4.8 %all-to-all-start.1 = ((bf16[4,26,20,128]{3,2,1,0:T(8,128)(2,1)}), bf16[4,26,20,128]{3,2,1,0:T(8,128)(2,1)S(1)}, u32[]{:S(2)}, u32[]{:S(2)}) async-start(bf16[4,26,20,128]{3,2,1,0:T(8,128)(2,1)} %broadcast_in_dim.392), calls=%async_computation.1 | async-start | bytes 1277952 | tf_op jit(solution)/shard_map/all_to_all | solution.py:34
  97.3 6.4 %all-to-all-done.1 = bf16[4,26,20,128]{3,2,1,0:T(8,128)(2,1)S(1)} async-done(((bf16[4,26,20,128]{3,2,1,0:T(8,128)(2,1)}), bf16[4,26,20,128]{3,2,1,0:T(8,128)(2,1)S(1)}, u32[]{:S(2)}, u32[]{:S(2)}) %all-to-all-start.1) | async-done | bytes 532512 | tf_op jit(solution)/shard_map/all_to_all | solution.py:34
  103.9 0.8 broadcast_in_dim.360.clone
  104.7 42.2 %while.16 = (s32[]{:T(128)}, bf16[14,20,512]{2,0,1:T(8,128)(2,1)}, s32[]{:T(128)}, f32[14,8]{1,0:T(8,128)S(1)}, s32[14,8]{1,0:T(8,128)S(1)}, /*index=5*/bf16[26,...) while((s32[]{:T(128)}, bf16[14,20,512]{2,0,1:T(8,128)(2,1)}, ...), condition=%wide.region_13.14_spmd.clone, body=%wide.region_7.13_spmd.clone.sunk | while | flops 839092416 | bytes 21879992 | solution.py:180
  104.7 0.9 broadcast_in_dim.455
  105.6 4.9 %all-to-all-start = ((bf16[4,7,20,512]{3,1,2,0:T(8,128)(2,1)}), bf16[4,7,20,512]{3,1,2,0:T(8,128)(2,1)S(1)}, u32[]{:S(2)}, u32[]{:S(2)}) async-start(bf16[4,7,20,512]{3,1,2,0:T(8,128)(2,1)} %broadcast_in_dim.455), calls=%async_computation | async-start | bytes 1310720 | tf_op jit(solution)/shard_map/while/body/eval_jaxpr/all_to_all | solution.py:34
  110.7 0.8 gather_fusion
  111.4 0.8 multiply_reduce_fusion.12
  123.0 2.0 %dynamic_update_slice.11 = bf16[14,20,512]{2,0,1:T(8,128)(2,1)S(1)} dynamic-update-slice(bf16[14,20,512]{2,0,1:T(8,128)(2,1)S(1)} %copy-done, bf16[7,20,512]{2,0,1:T(8,128)(2,1)S(1)} %copy.116, s32[]{:T(128)S(6)} %select_n.354, s32[]{:T(128)} %constant.172.clone.1..sunk, s32[]{:T(128)} %constant.172.clone.1..sunk) | dynamic-update-slice | bytes 286724 | tf_op jit(solution)/shard_map/while/body/eval_jaxpr/dynamic_update_slice | solution.py:177
  125.9 0.9 broadcast_in_dim.455
  126.7 4.8 %all-to-all-start = ((bf16[4,7,20,512]{3,1,2,0:T(8,128)(2,1)}), bf16[4,7,20,512]{3,1,2,0:T(8,128)(2,1)S(1)}, u32[]{:S(2)}, u32[]{:S(2)}) async-start(bf16[4,7,20,512]{3,1,2,0:T(8,128)(2,1)} %broadcast_in_dim.455), calls=%async_computation | async-start | bytes 1310720 | tf_op jit(solution)/shard_map/while/body/eval_jaxpr/all_to_all | solution.py:34
  131.7 0.8 gather_fusion
  132.5 0.7 multiply_reduce_fusion.12
  144.0 2.0 %dynamic_update_slice.11 = bf16[14,20,512]{2,0,1:T(8,128)(2,1)S(1)} dynamic-update-slice(bf16[14,20,512]{2,0,1:T(8,128)(2,1)S(1)} %copy-done, bf16[7,20,512]{2,0,1:T(8,128)(2,1)S(1)} %copy.116, s32[]{:T(128)S(6)} %select_n.354, s32[]{:T(128)} %constant.172.clone.1..sunk, s32[]{:T(128)} %constant.172.clone.1..sunk) | dynamic-update-slice | bytes 286724 | tf_op jit(solution)/shard_map/while/body/eval_jaxpr/dynamic_update_slice | solution.py:177
  (181 shorter events, 35.9 us)
Async XLA Ops:
  0.0 59.6 %copy-start.2 = (f32[14,7]{0,1:T(8,128)S(1)}, f32[14,7]{0,1:T(8,128)}, u32[]{:S(2)}) copy-start(f32[14,7]{0,1:T(8,128)} %param.16) | copy-start | bytes 1180
  8.0 52.5 %collective-permute-start.9 = (bf16[4,128]{1,0:T(4,128)(2,1)S(1)}, bf16[4,128]{1,0:T(4,128)(2,1)S(1)}, u32[]{:S(2)}, u32[]{:S(2)}) collective-permute-start(bf16[4,128]{1,0:T(4,128)(2,1)S(1)} %gather_fusion.11), channel_id=1, source_target_pairs={{0,4},{4,8},{8,12},{12,16},{16,20},{20,24},{24,28},{28,32},{32,36}... | collective-permute-start | bytes 3080 | tf_op jit(solution)/shard_map/ppermute | solution.py:23
  15.0 47.5 %collective-permute-start.7 = (bf16[4,128]{1,0:T(4,128)(2,1)S(1)}, bf16[4,128]{1,0:T(4,128)(2,1)S(1)}, u32[]{:S(2)}, u32[]{:S(2)}) collective-permute-start(bf16[4,128]{1,0:T(4,128)(2,1)S(1)} %gather_fusion.9), channel_id=1, source_target_pairs={{8,0},{12,4},{16,8},{20,12},{24,16},{28,20},{32,24},{36,28},{40,32... | collective-permute-start | bytes 3080 | tf_op jit(solution)/shard_map/ppermute | solution.py:23
  30.9 33.9 %collective-permute-start.11 = (bf16[4,128]{1,0:T(4,128)(2,1)S(1)}, bf16[4,128]{1,0:T(4,128)(2,1)S(1)}, u32[]{:S(2)}, u32[]{:S(2)}) collective-permute-start(bf16[4,128]{1,0:T(4,128)(2,1)S(1)} %gather_fusion.13), channel_id=1, source_target_pairs={{0,12},{4,16},{8,20},{12,24},{16,28},{20,32},{24,36},{28,40},{32,4... | collective-permute-start | bytes 3080 | tf_op jit(solution)/shard_map/ppermute | solution.py:23
  33.4 38.6 %collective-permute-start.8 = (bf16[4,128]{1,0:T(4,128)(2,1)S(1)}, bf16[4,128]{1,0:T(4,128)(2,1)S(1)}, u32[]{:S(2)}, u32[]{:S(2)}) collective-permute-start(bf16[4,128]{1,0:T(4,128)(2,1)S(1)} %gather_fusion.10), channel_id=1, source_target_pairs={{4,0},{8,4},{12,8},{16,12},{20,16},{24,20},{28,24},{32,28},{36,32}... | collective-permute-start | bytes 3080 | tf_op jit(solution)/shard_map/ppermute | solution.py:23
  38.2 41.3 %collective-permute-start = (bf16[4,20,128]{2,1,0:T(8,128)(2,1)S(1)}, bf16[4,20,128]{2,1,0:T(8,128)(2,1)S(1)}, u32[]{:S(2)}, u32[]{:S(2)}) collective-permute-start(bf16[4,20,128]{2,1,0:T(8,128)(2,1)S(1)} %gather_fusion.2), channel_id=1, source_target_pairs={{12,0},{16,4},{20,8},{24,12},{28,16},{32,20},{36,24},{40,28},{44,3... | collective-permute-start | bytes 61448 | tf_op jit(solution)/shard_map/ppermute | solution.py:23
  60.5 13.4 %collective-permute-start.6 = (bf16[4,128]{1,0:T(4,128)(2,1)S(1)}, bf16[4,128]{1,0:T(4,128)(2,1)S(1)}, u32[]{:S(2)}, u32[]{:S(2)}) collective-permute-start(bf16[4,128]{1,0:T(4,128)(2,1)S(1)} %gather_fusion.8), channel_id=1, source_target_pairs={{12,0},{16,4},{20,8},{24,12},{28,16},{32,20},{36,24},{40,28},{44,3... | collective-permute-start | bytes 3080 | tf_op jit(solution)/shard_map/ppermute | solution.py:23
  62.5 13.9 %collective-permute-start.10 = (bf16[4,128]{1,0:T(4,128)(2,1)S(1)}, bf16[4,128]{1,0:T(4,128)(2,1)S(1)}, u32[]{:S(2)}, u32[]{:S(2)}) collective-permute-start(bf16[4,128]{1,0:T(4,128)(2,1)S(1)} %gather_fusion.12), channel_id=1, source_target_pairs={{0,8},{4,12},{8,16},{12,20},{16,24},{20,28},{24,32},{28,36},{32,40... | collective-permute-start | bytes 3080 | tf_op jit(solution)/shard_map/ppermute | solution.py:23
  64.8 16.8 %collective-permute-start.1 = (bf16[4,20,128]{2,1,0:T(8,128)(2,1)S(1)}, bf16[4,20,128]{2,1,0:T(8,128)(2,1)S(1)}, u32[]{:S(2)}, u32[]{:S(2)}) collective-permute-start(bf16[4,20,128]{2,1,0:T(8,128)(2,1)S(1)} %gather_fusion.3), channel_id=1, source_target_pairs={{8,0},{12,4},{16,8},{20,12},{24,16},{28,20},{32,24},{36,28},{40,32... | collective-permute-start | bytes 61448 | tf_op jit(solution)/shard_map/ppermute | solution.py:23
  72.0 11.6 %collective-permute-start.2 = (bf16[4,20,128]{2,1,0:T(8,128)(2,1)S(1)}, bf16[4,20,128]{2,1,0:T(8,128)(2,1)S(1)}, u32[]{:S(2)}, u32[]{:S(2)}) collective-permute-start(bf16[4,20,128]{2,1,0:T(8,128)(2,1)S(1)} %gather_fusion.4), channel_id=1, source_target_pairs={{4,0},{8,4},{12,8},{16,12},{20,16},{24,20},{28,24},{32,28},{36,32}... | collective-permute-start | bytes 61448 | tf_op jit(solution)/shard_map/ppermute | solution.py:23
  73.9 16.6 %collective-permute-start.3 = (bf16[4,20,128]{2,1,0:T(8,128)(2,1)S(1)}, bf16[4,20,128]{2,1,0:T(8,128)(2,1)S(1)}, u32[]{:S(2)}, u32[]{:S(2)}) collective-permute-start(bf16[4,20,128]{2,1,0:T(8,128)(2,1)S(1)} %gather_fusion.5), channel_id=1, source_target_pairs={{0,4},{4,8},{8,12},{12,16},{16,20},{20,24},{24,28},{28,32},{32,36}... | collective-permute-start | bytes 61448 | tf_op jit(solution)/shard_map/ppermute | solution.py:23
  76.4 14.1 %collective-permute-start.4 = (bf16[4,20,128]{2,1,0:T(8,128)(2,1)S(1)}, bf16[4,20,128]{2,1,0:T(8,128)(2,1)S(1)}, u32[]{:S(2)}, u32[]{:S(2)}) collective-permute-start(bf16[4,20,128]{2,1,0:T(8,128)(2,1)S(1)} %gather_fusion.6), channel_id=1, source_target_pairs={{0,8},{4,12},{8,16},{12,20},{16,24},{20,28},{24,32},{28,36},{32,40... | collective-permute-start | bytes 61448 | tf_op jit(solution)/shard_map/ppermute | solution.py:23
  79.6 11.0 %collective-permute-start.5 = (bf16[4,20,128]{2,1,0:T(8,128)(2,1)S(1)}, bf16[4,20,128]{2,1,0:T(8,128)(2,1)S(1)}, u32[]{:S(2)}, u32[]{:S(2)}) collective-permute-start(bf16[4,20,128]{2,1,0:T(8,128)(2,1)S(1)} %gather_fusion.7), channel_id=1, source_target_pairs={{0,12},{4,16},{8,20},{12,24},{16,28},{20,32},{24,36},{28,40},{32,4... | collective-permute-start | bytes 61448 | tf_op jit(solution)/shard_map/ppermute | solution.py:23
  81.6 14.9 %collective-permute-start.12 = (bf16[2,20,512]{2,1,0:T(8,128)(2,1)S(1)}, bf16[2,20,512]{2,1,0:T(8,128)(2,1)S(1)}, u32[]{:S(2)}, u32[]{:S(2)}) collective-permute-start(bf16[2,20,512]{2,1,0:T(8,128)(2,1)S(1)} %get-tuple-element.303), channel_id=1, source_target_pairs={{0,4},{4,8},{8,12},{12,16},{16,20},{20,24},{24,28},{28,32},{32,36}... | collective-permute-start | bytes 122888 | tf_op jit(solution)/shard_map/ppermute | solution.py:23
  83.6 12.8 %collective-permute-start.13 = (bf16[2,20,512]{2,1,0:T(8,128)(2,1)S(1)}, bf16[2,20,512]{2,1,0:T(8,128)(2,1)S(1)}, u32[]{:S(2)}, u32[]{:S(2)}) collective-permute-start(bf16[2,20,512]{2,1,0:T(8,128)(2,1)S(1)} %get-tuple-element.304), channel_id=1, source_target_pairs={{4,0},{8,4},{12,8},{16,12},{20,16},{24,20},{28,24},{32,28},{36,32}... | collective-permute-start | bytes 122888 | tf_op jit(solution)/shard_map/ppermute | solution.py:23
  91.6 12.1 %all-to-all-start.1 = ((bf16[4,26,20,128]{3,2,1,0:T(8,128)(2,1)}), bf16[4,26,20,128]{3,2,1,0:T(8,128)(2,1)S(1)}, u32[]{:S(2)}, u32[]{:S(2)}) async-start(bf16[4,26,20,128]{3,2,1,0:T(8,128)(2,1)} %broadcast_in_dim.392), calls=%async_computation.1 | async-start | bytes 1277952 | tf_op jit(solution)/shard_map/all_to_all | solution.py:34
  105.6 16.7 %all-to-all-start = ((bf16[4,7,20,512]{3,1,2,0:T(8,128)(2,1)}), bf16[4,7,20,512]{3,1,2,0:T(8,128)(2,1)S(1)}, u32[]{:S(2)}, u32[]{:S(2)}) async-start(bf16[4,7,20,512]{3,1,2,0:T(8,128)(2,1)} %broadcast_in_dim.455), calls=%async_computation | async-start | bytes 1310720 | tf_op jit(solution)/shard_map/while/body/eval_jaxpr/all_to_all | solution.py:34
  122.0 1.0 copy-start
  125.1 0.7 copy-start.1
  126.7 16.6 %all-to-all-start = ((bf16[4,7,20,512]{3,1,2,0:T(8,128)(2,1)}), bf16[4,7,20,512]{3,1,2,0:T(8,128)(2,1)S(1)}, u32[]{:S(2)}, u32[]{:S(2)}) async-start(bf16[4,7,20,512]{3,1,2,0:T(8,128)(2,1)} %broadcast_in_dim.455), calls=%async_computation | async-start | bytes 1310720 | tf_op jit(solution)/shard_map/while/body/eval_jaxpr/all_to_all | solution.py:34
  143.1 1.0 copy-start
  146.1 0.7 copy-start.1
where the time goes:
time: 148 us; the launch traced here: 147 us
  starting transfers between devices  68.3 us (46%)
  local copies, waits for them, and re-layouts  28.4 us (19%)
  other arithmetic  20.4 us (14%)
  matrix products  19.7 us (13%)
  waiting for transfers between devices  6.4 us (4%)
  between operations  2.97 us (2%)
    ppermute x14, starting transfers between devices, from_behind(): lax.ppermute(value, axis, [(source, source + steps) for source in range(f...  53.8 us
    all_to_all x3, starting transfers between devices, sent_to_all(): lax.all_to_all(jnp.broadcast_to(x[None], (count, *x.shape)), axis, 0, 0,...  14.5 us
    mul x6, other arithmetic, pick_slots(): rows_here = jnp.sum(owned_flag[..., None] * (wanted - range_start), axis=-2)  8.29 us
    all_to_all x3, waiting for transfers between devices, sent_to_all(): lax.all_to_all(jnp.broadcast_to(x[None], (count, *x.shape)), axis, 0, 0,...  6.36 us
    dot_general x12, matrix products, inverse_root(): jnp.einsum('pij,pjk->pik', middle, inverse_part, precision=exact)  5.37 us
    dot_general x12, matrix products, inverse_root(): jnp.einsum('pij,pjk->pik', inverse_part, root_part, precision=exact)  5.14 us
    reduce_sum x6, other arithmetic, pick_slots(): rows_here = jnp.sum(owned_flag[..., None] * (wanted - range_start), axis=-2)  4.39 us
    dot_general x10, matrix products, inverse_root(): root_part = jnp.einsum('pij,pjk->pik', root_part, middle, precision=exact)  4.28 us
  transfers between devices with their start and end apart: 17, of which 1 were waited for; matrix products, arithmetic and copies ran while one was open for 35% of the time, Pallas kernels for 0%

commit v1 on v0

v1 whole, which is shorter than its diff:
```python
import functools
import math

import jax
import jax.numpy as jnp
from jax import lax
from jax.experimental import pallas as pl
from jax.experimental.pallas import tpu as pltpu
from jax.sharding import PartitionSpec as P

MOVE = 2
REACH = 3
HPEER = 3
HCAP = 4
NS_ITERS = 6
LIVE = 10
BLOCK = 4
PADDED = 24
INFLATION = 1.1

SWAPS = ((-3, 3, -3, 3), (-2, -2, 2, 2), (-1, -3, 3, 1))

SMEM = pltpu.SMEM
VMEM = pltpu.VMEM
F32 = jnp.float32
BF16 = jnp.bfloat16


def chosen(place, values):
    result = values[0]
    for k in range(1, len(values)):
        result = jnp.where(place == k, values[k], result)
    return result


def padded_rows(x, extra=()):
    rows = x.shape[0] + len(extra)
    zeros = jnp.zeros((PADDED - rows, x.shape[1]), x.dtype)
    return jnp.concatenate([x, *extra, zeros], axis=0)


def pack_kernel(
    count_ref, old_ref, new_ref, halo_ref,
    obs_ref, innovation_ref, precision_ref, background_ref,
    own_ref, block_ref, *swap_refs,
):
    devices = new_ref.shape[0] - 1
    me = lax.axis_index("tile")
    place = lax.rem(me, BLOCK)
    new_start, new_end = new_ref[me], new_ref[me + 1]
    members, obs_slots = obs_ref.shape[1:]
    lane = lax.broadcasted_iota(jnp.int32, (1, obs_slots), 1)
    for i in range(LIVE):
        live = (lane < count_ref[i]).astype(F32)
        root = jnp.sqrt(precision_ref[i : i + 1, :] * live)
        scaled = obs_ref[i].astype(F32) * root
        pulled = root * innovation_ref[i : i + 1, :]
        own_ref[i] = padded_rows(scaled, (pulled,)).astype(BF16)

    def pack(reader, put):
        reader = jnp.clip(reader, 0, devices - 1)
        group = 0
        for g in range(1, HPEER):
            first = halo_ref[reader, g * HCAP]
            group = jnp.where((first >= new_start) & (first < new_end), g, group)
        for k in range(HCAP):
            row = jnp.clip(halo_ref[reader, group * HCAP + k] - new_start, 0, LIVE - 1)
            put(k, own_ref[row])

    for j in range(BLOCK):
        def put(k, value, j=j):
            block_ref[j, k] = value
        pack(me - place + j, put)
    for swap, swap_ref in zip(SWAPS, swap_refs):
        def put(k, value, swap_ref=swap_ref):
            swap_ref[k] = value
        pack(me + chosen(place, swap), put)

    old_count = old_ref[me + 1] - old_ref[me]
    pieces = background_ref.shape[2] // obs_slots
    for first, inside, slot in (
        (old_count - MOVE, place < BLOCK - 1, place + 1),
        (0, place > 0, place - 1),
    ):
        for t in range(MOVE):
            value = padded_rows(background_ref[first + t].astype(F32)).astype(BF16)
            for c in range(pieces):
                piece = value[:, c * obs_slots : (c + 1) * obs_slots]
                at = HCAP + t * pieces + c

                @pl.when(inside)
                def _():
                    block_ref[slot, at] = piece

                @pl.when(jnp.logical_not(inside))
                def _():
                    swap_refs[-1][at] = piece


def table_kernel(new_ref, halo_ref, own_ref, block_ref, *refs):
    swap_refs, out_ref = refs[:-1], refs[-1]
    devices = new_ref.shape[0] - 1
    me = lax.axis_index("tile")
    place = lax.rem(me, BLOCK)
    copies = out_ref.shape[0]
    moved = block_ref.shape[1] - HCAP

    def put(at, value):
        for r in range(copies):
            out_ref[r, at] = value

    for i in range(LIVE):
        put(i, own_ref[i])
    for g in range(HPEER):
        first = halo_ref[me, g * HCAP]
        peer = me - REACH
        for o in range(1 - REACH, REACH + 1):
            bound = new_ref[jnp.clip(me + o, 0, devices)]
            peer = peer + (bound <= first).astype(jnp.int32)
        at = LIVE + g * HCAP
        base = me - place

        @pl.when((peer >= base) & (peer < base + BLOCK))
        def _():
            slot = jnp.clip(peer - base, 0, BLOCK - 1)
            for k in range(HCAP):
                put(at + k, block_ref[slot, k])

        for swap, swap_ref in zip(SWAPS, swap_refs):
            @pl.when(peer == me + chosen(place, swap))
            def _():
                for k in range(HCAP):
                    put(at + k, swap_ref[k])

    for at, inside, slot in (
        (LIVE + HPEER * HCAP, place > 0, place - 1),
        (LIVE + HPEER * HCAP + moved, place < BLOCK - 1, place + 1),
    ):
        @pl.when(inside)
        def _():
            for k in range(moved):
                put(at + k, block_ref[slot, HCAP + k])

        @pl.when(jnp.logical_not(inside))
        def _():
            for k in range(moved):
                put(at + k, swap_refs[-1][HCAP + k])


def split(x):
    high = x.astype(BF16)
    return high, (x - high.astype(F32)).astype(BF16)


def dot(a, b):
    return jnp.dot(a, b, preferred_element_type=F32)


def dot3(a, b):
    return dot(a[0], b[0]) + (dot(a[0], b[1]) + dot(a[1], b[0]))


def analysis_kernel(
    region_ref, weight_ref, old_ref, new_ref,
    table_ref, background_ref, out_ref,
    gram_ref, system_ref, inverse_ref, state_ref,
):
    me = lax.axis_index("tile")
    rank = lax.axis_index("mem")
    ranks, tiles = table_ref.shape[0], LIVE + HPEER * HCAP
    capacity, members, width = out_ref.shape
    obs_slots = table_ref.shape[3]
    side = ranks * PADDED
    ensemble = ranks * members
    old_start, old_end = old_ref[me], old_ref[me + 1]
    new_start, new_end = new_ref[me], new_ref[me + 1]

    row = lax.broadcasted_iota(jnp.int32, (side, side), 0)
    column = lax.broadcasted_iota(jnp.int32, (side, side), 1)
    real = (lax.rem(row, PADDED) < members) & (lax.rem(column, PADDED) < members)
    diagonal = (row == column).astype(F32)
    shift = jnp.where(real, diagonal * ((ensemble - 1) / INFLATION), 0.0)
    lane = lax.broadcasted_iota(jnp.int32, (1, side), 1)
    real_lane = lax.rem(lane, PADDED) < members

    for t in range(tiles):
        rows = [table_ref[r, t].astype(F32) for r in range(ranks)]
        block = jnp.concatenate(rows, axis=0).astype(BF16)
        gram_ref[t] = lax.dot_general(
            block, block, (((1,), (1,)), ((), ())), preferred_element_type=F32
        )

    pieces = width // obs_slots
    for i in range(LIVE):
        tile = new_start + i
        stays = (tile >= old_start) & (tile < old_end)

        @pl.when(stays)
        def _():
            at = jnp.clip(tile - old_start, 0, capacity - 1)
            rows = [padded_rows(background_ref[r * capacity + at].astype(F32)) for r in range(ranks)]
            state_ref[i] = jnp.concatenate(rows, axis=0).astype(BF16)

        @pl.when(jnp.logical_not(stays))
        def _():
            left = jnp.clip(tile - old_start + MOVE, 0, MOVE - 1) * pieces
            right = (jnp.clip(tile - old_end, 0, MOVE - 1) + MOVE) * pieces
            at = tiles + jnp.where(tile < old_start, left, right)
            for c in range(pieces):
                rows = [table_ref[r, at + c].astype(F32) for r in range(ranks)]
                state_ref[i, :, c * obs_slots : (c + 1) * obs_slots] = jnp.concatenate(
                    rows, axis=0
                ).astype(BF16)

    frobenius, pull = [], []
    for i in range(LIVE):
        total = gram_ref[i]
        for e in range(region_ref.shape[1]):
            r = region_ref[i, e]
            at = jnp.where(r < capacity, jnp.minimum(r, LIVE - 1), r - capacity + LIVE)
            total = total + weight_ref[i, e] * gram_ref[at]
        pull.append(jnp.where(real_lane, total[members : members + 1, :], 0.0))
        system = jnp.where(real, total, 0.0) + shift
        squared = jnp.sum(jnp.sum(system * system, axis=0, keepdims=True), axis=1, keepdims=True)
        norm = jnp.sqrt(squared)
        frobenius.append(norm)
        root = system * (1.0 / norm)
        middle = 1.5 * diagonal - 0.5 * root
        inverse_ref[i] = middle
        system_ref[i] = dot3(split(root), split(middle))

    for step in range(1, NS_ITERS):
        for i in range(LIVE):
            root, inverse = split(system_ref[i]), split(inverse_ref[i])
            middle = split(1.5 * diagonal - 0.5 * dot3(inverse, root))
            if step < NS_ITERS - 1:
                system_ref[i] = dot3(root, middle)
            inverse_ref[i] = dot3(middle, inverse)

    own_row = lax.broadcasted_iota(jnp.int32, (PADDED, side), 0)
    for i in range(LIVE):
        inverse = split(inverse_ref[i])
        pulled = jnp.broadcast_to(pull[i], (8, side))
        half_way = dot3(split(pulled), inverse)
        mean_weight = dot3(split(half_way), inverse)[0:1, :] / frobenius[i]
        own = inverse_ref[i, pl.ds(pl.multiple_of(rank * PADDED, 8), PADDED), :]
        spread = (math.sqrt(ensemble - 1) / jnp.sqrt(frobenius[i])) * own
        transform = jnp.where((own_row < members) & real_lane, spread + mean_weight, 0.0)
        transform = transform.astype(BF16)
        keep_share = 1.0 - jnp.sum(transform.astype(F32), axis=1, keepdims=True)
        ones = jnp.where((own_row == members) & real_lane, 1.0, 0.0).astype(BF16)
        blended = dot(transform + ones, state_ref[i])
        mean_state = blended[members : members + 1, :] / ensemble
        analysis = blended[:members] + keep_share[:members] * mean_state
        out_ref[i] = jnp.where(new_start + i < new_end, analysis, 0.0).astype(BF16)
    for i in range(LIVE, capacity):
        out_ref[i] = jnp.zeros((members, width), BF16)


def shards(
    background, obs_ens, innovation, precision, loc_weight,
    old_split, new_split, obs_count, halo_tiles, region_list,
):
    capacity, members, width = background.shape
    obs_slots = obs_ens.shape[2]
    devices = lax.axis_size("tile")
    ranks = lax.axis_size("mem")
    moved = MOVE * width // obs_slots
    tiles = LIVE + HPEER * HCAP
    smem = pl.BlockSpec(memory_space=SMEM)
    vmem = pl.BlockSpec(memory_space=VMEM)

    def tile_blocks(*leading):
        return jax.ShapeDtypeStruct((*leading, PADDED, obs_slots), BF16)

    gathered = lax.all_gather(background, "mem", axis=0, tiled=True)

    own, block, *swaps = pl.pallas_call(
        pack_kernel,
        out_shape=(
            tile_blocks(LIVE),
            tile_blocks(BLOCK, HCAP + moved),
            tile_blocks(HCAP),
            tile_blocks(HCAP),
            tile_blocks(HCAP + moved),
        ),
        in_specs=[smem] * 4 + [vmem] * 4,
        out_specs=[vmem] * 5,
        compiler_params=pltpu.CompilerParams(vmem_limit_bytes=16 << 20),
    )(obs_count, old_split, new_split, halo_tiles, obs_ens, innovation, precision, background)

    groups = [list(range(b, b + BLOCK)) for b in range(0, devices, BLOCK)]
    block = lax.all_to_all(block, "tile", 0, 0, axis_index_groups=groups, tiled=True)
    arrived = []
    for swap, value in zip(SWAPS, swaps):
        pairs = [(d, d + swap[d % BLOCK]) for d in range(devices)]
        pairs = [(d, e) for d, e in pairs if 0 <= e < devices]
        arrived.append(lax.ppermute(value, "tile", pairs))

    table = pl.pallas_call(
        table_kernel,
        out_shape=tile_blocks(ranks, tiles + 2 * moved),
        in_specs=[smem] * 2 + [vmem] * 5,
        out_specs=vmem,
        compiler_params=pltpu.CompilerParams(vmem_limit_bytes=16 << 20),
    )(new_split, halo_tiles, own, block, *arrived)
    table = lax.all_to_all(table, "mem", 0, 0, tiled=True)

    side = ranks * PADDED
    return pl.pallas_call(
        analysis_kernel,
        out_shape=jax.ShapeDtypeStruct((capacity, members, width), BF16),
        in_specs=[smem] * 4 + [vmem] * 2,
        out_specs=vmem,
        scratch_shapes=[
            VMEM((tiles, side, side), F32),
            VMEM((LIVE, side, side), F32),
            VMEM((LIVE, side, side), F32),
            VMEM((LIVE, side, width), BF16),
        ],
        compiler_params=pltpu.CompilerParams(vmem_limit_bytes=28 << 20),
    )(region_list, loc_weight, old_split, new_split, table, gathered)


def solution(mesh):
    in_specs = (
        P("tile", "mem", None),
        P("tile", "mem", None),
        P("tile", None),
        P("tile", None),
        P("tile", None),
        P(),
        P(),
        P("tile"),
        P(),
        P("tile", None),
    )
    out_specs = P("tile", "mem", None)
    return jax.shard_map(shards, mesh=mesh, in_specs=in_specs, out_specs=out_specs, check_vma=False)
```

time: 148 us -> 87 us (0.59)
  the two profiles are of different devices: /device:TPU:34 before, /device:TPU:56 now
where the time goes in v1:
time: 87 us; the launch traced here: 86.1 us
  starting transfers between devices  25 us (29%)
  Pallas kernels  19.7 us (23%)
  waiting for transfers between devices  17.5 us (20%)
  between operations  13.5 us (16%)
  local copies, waits for them, and re-layouts  10.3 us (12%)
    ppermute x3, starting transfers between devices, shards(): arrived.append(lax.ppermute(value, 'tile', pairs))  17.1 us
    pallas_call x1, Pallas kernels, shards(): pl.pallas_call(analysis_kernel, out_shape=jax.ShapeDtypeStruct((capacity,...  14.3 us
    all_to_all x1, waiting for transfers between devices, shards(): table = lax.all_to_all(table, 'mem', 0, 0, tiled=True)  12.6 us
    unnamed x27, local copies, waits for them, and re-layouts  9.51 us
    ppermute x3, waiting for transfers between devices, shards(): arrived.append(lax.ppermute(value, 'tile', pairs))  4.95 us
    all_to_all x1, starting transfers between devices, shards(): table = lax.all_to_all(table, 'mem', 0, 0, tiled=True)  4.29 us
    all_to_all x1, starting transfers between devices, shards(): lax.all_to_all(block, 'tile', 0, 0, axis_index_groups=groups, tiled=True)  3.64 us
    pallas_call x1, Pallas kernels, shards(): pl.pallas_call(table_kernel, out_shape=tile_blocks(ranks, tiles + 2 * mov...  2.8 us
  transfers between devices with their start and end apart: 6, of which 3 were waited for; matrix products, arithmetic and copies ran while one was open for 2% of the time, Pallas kernels for 6%

profile of v1, /device:TPU:56, one launch (start us, length us, event | category | flops | bytes accessed | tf_op | source)
XLA Modules:
  0.0 86.1 jit_solution(16373374351008283028)
XLA Ops:
  6.5 0.0 copy-start.3
  6.5 0.0 all-gather.2.cloned.1.call-start
  6.5 1.9 %copy.21.background_ref = bf16[14,20,512]{2,1,0:T(8,128)(2,1)} copy(bf16[14,20,512]{2,0,1:T(8,128)(2,1)} %param.10) | data formatting | bytes 573440 | tf_op args[0]
  8.4 0.0 all-gather.2.cloned.1.call-update
  8.4 0.8 copy.22.halo_ref
  9.2 0.9 %copy.20.obs_ref = bf16[14,20,128]{2,1,0:T(8,128)(2,1)S(1)} copy(bf16[14,20,128]{2,0,1:T(8,128)(2,1)} %param.11) | data formatting | bytes 143360 | tf_op args[1]
  10.2 0.0 copy-start
  10.2 1.0 %copy-done = bf16[14,20,512]{2,1,0:T(8,128)(2,1)S(1)} copy-done((bf16[14,20,512]{2,1,0:T(8,128)(2,1)S(1)}, bf16[14,20,512]{2,1,0:T(8,128)(2,1)}, u32[]{:S(2)}) %copy-start) | copy-done | bytes 286744
  11.1 0.0 copy-start.2
  11.1 0.7 copy-done.2
  11.8 0.0 copy-start.4
  11.8 0.7 copy-done.4
  12.5 0.0 copy-start.5
  12.5 0.7 copy-done.5
  13.2 0.0 copy-start.6
  13.2 0.7 copy-done.6
  13.9 0.0 copy-start.8
  13.9 0.7 copy-done.8
  14.5 2.7 %shard_map.100 = (bf16[10,24,128]{2,1,0:T(8,128)(2,1)S(1)}, bf16[4,12,24,128]{3,2,1,0:T(8,128)(2,1)}, bf16[4,24,128]{2,1,0:T(8,128)(2,1)S(1)}, bf16[4,24,128]{2,1,0:T(8,128)(2,1)S(1)}, bf16[12,24,128]{2,1,0:T(8,128)(2,1)S(1)}) custom-call(s32[14]{0:T(128)S(1)} %copy-done.8, s32[129]{0:T(256)S(1)} %copy-done.6, s32[129]{0:T(256)S(1)} %copy-done.2, ...), custom_call_target="tpu_custom_call" | custom-call | tf_op jit(solution)/shard_map/pallas_call | solution.py:278
  17.2 3.6 %all-to-all-start = ((bf16[4,12,24,128]{3,2,1,0:T(8,128)(2,1)}), bf16[4,12,24,128]{3,2,1,0:T(8,128)(2,1)S(1)}, u32[]{:S(2)}, u32[]{:S(2)}) async-start(bf16[4,12,24,128]{3,2,1,0:T(8,128)(2,1)} %get-tuple-element.11), calls=%async_computation | async-start | bytes 589824 | tf_op jit(solution)/shard_map/all_to_all | solution.py:293
  20.8 11.8 %collective-permute-start.2 = (bf16[12,24,128]{2,1,0:T(8,128)(2,1)S(1)}, bf16[12,24,128]{2,1,0:T(8,128)(2,1)S(1)}, u32[]{:S(2)}, u32[]{:S(2)}) collective-permute-start(bf16[12,24,128]{2,1,0:T(8,128)(2,1)S(1)} %get-tuple-element.14), channel_id=1, source_target_pairs={{8,20},{12,16},{16,12},{20,8},{24,36},{28,32},{32,28},{36,24},{40,... | collective-permute-start | bytes 221192 | tf_op jit(solution)/shard_map/ppermute | solution.py:298
  32.7 2.4 %collective-permute-start = (bf16[4,24,128]{2,1,0:T(8,128)(2,1)S(1)}, bf16[4,24,128]{2,1,0:T(8,128)(2,1)S(1)}, u32[]{:S(2)}, u32[]{:S(2)}) collective-permute-start(bf16[4,24,128]{2,1,0:T(8,128)(2,1)S(1)} %get-tuple-element.12), channel_id=1, source_target_pairs={{4,16},{12,24},{16,4},{20,32},{24,12},{28,40},{32,20},{36,48},{40,... | collective-permute-start | bytes 73736 | tf_op jit(solution)/shard_map/ppermute | solution.py:298
  35.1 2.9 %collective-permute-start.1 = (bf16[4,24,128]{2,1,0:T(8,128)(2,1)S(1)}, bf16[4,24,128]{2,1,0:T(8,128)(2,1)S(1)}, u32[]{:S(2)}, u32[]{:S(2)}) collective-permute-start(bf16[4,24,128]{2,1,0:T(8,128)(2,1)S(1)} %get-tuple-element.13), channel_id=1, source_target_pairs={{8,16},{12,20},{16,8},{20,12},{24,32},{28,36},{32,24},{36,28},{40,... | collective-permute-start | bytes 73736 | tf_op jit(solution)/shard_map/ppermute | solution.py:298
  38.0 2.8 %collective-permute-done.refs_0_ = bf16[4,24,128]{2,1,0:T(8,128)(2,1)S(1)} collective-permute-done((bf16[4,24,128]{2,1,0:T(8,128)(2,1)S(1)}, bf16[4,24,128]{2,1,0:T(8,128)(2,1)S(1)}, u32[]{:S(2)}, u32[]{:S(2)}) %collective-permute-start) | collective-permute-done | bytes 24608 | tf_op jit(solution)/shard_map/ppermute | solution.py:298
  40.8 2.1 %collective-permute-done.1.refs_1_ = bf16[4,24,128]{2,1,0:T(8,128)(2,1)S(1)} collective-permute-done((bf16[4,24,128]{2,1,0:T(8,128)(2,1)S(1)}, bf16[4,24,128]{2,1,0:T(8,128)(2,1)S(1)}, u32[]{:S(2)}, u32[]{:S(2)}) %collective-permute-start.1) | collective-permute-done | bytes 24608 | tf_op jit(solution)/shard_map/ppermute | solution.py:298
  42.9 0.0 collective-permute-done.2.refs_2_
  42.9 0.0 all-to-all-done.block_ref
  42.9 0.0 copy-done.3
  42.9 0.0 copy-start.9
  42.9 0.0 copy-start.10
  43.0 0.0 copy-start.7
  43.0 2.8 %shard_map.101 = bf16[4,38,24,128]{3,2,1,0:T(8,128)(2,1)} custom-call(s32[129]{0:T(256)S(1)} %copy-done.3, s32[128,12]{1,0:T(8,128)S(1)} %copy.22.halo_ref, bf16[10,24,128]{2,1,0:T(8,128)(2,1)S(1)} %get-tuple-element.10.own_ref, bf16[4,12,24,128]{3,2,1,0:T(8,128)(2,1)S(1)} %all-to-all-done.block_ref, bf16[4,24,128]{2,1,0:T(8,128)(2,1)S(1)} %collective-permute-done.refs_0_, ...), custom_call_target="tpu_custom_call" | custom-call | tf_op jit(solution)/shard_map/pallas_call | solution.py:300
  45.8 4.3 %all-to-all-start.1 = ((bf16[4,38,24,128]{3,2,1,0:T(8,128)(2,1)}), bf16[4,38,24,128]{3,2,1,0:T(8,128)(2,1)S(1)}, u32[]{:S(2)}, u32[]{:S(2)}) async-start(bf16[4,38,24,128]{3,2,1,0:T(8,128)(2,1)} %shard_map.101), calls=%async_computation.1 | async-start | bytes 1867776 | tf_op jit(solution)/shard_map/all_to_all | solution.py:307
  50.1 0.0 copy-done.9
  50.1 0.1 copy.24.region_ref
  50.2 0.0 copy-done.10
  50.2 0.1 copy.25.weight_ref
  50.3 12.6 %all-to-all-done.1.table_ref = bf16[4,38,24,128]{3,2,1,0:T(8,128)(2,1)S(1)} async-done(((bf16[4,38,24,128]{3,2,1,0:T(8,128)(2,1)}), bf16[4,38,24,128]{3,2,1,0:T(8,128)(2,1)S(1)}, u32[]{:S(2)}, u32[]{:S(2)}) %all-to-all-start.1) | async-done | bytes 933920 | tf_op jit(solution)/shard_map/all_to_all | solution.py:307
  62.8 0.0 all-gather.2.cloned.1.call-done.background_ref
  62.8 0.0 copy-done.7
  62.8 0.0 copy-start.1
  62.8 1.3 %copy-done.1 = bf16[56,20,512]{2,1,0:T(8,128)(2,1)S(1)} copy-done((bf16[56,20,512]{2,1,0:T(8,128)(2,1)S(1)}, bf16[56,20,512]{2,1,0:T(8,128)(2,1)}, u32[]{:S(2)}) %copy-start.1) | copy-done | bytes 1146904
  64.2 14.3 %shard_map.102 = bf16[14,20,512]{2,1,0:T(8,128)(2,1)S(1)} custom-call(s32[14,7]{1,0:T(8,128)S(1)} %copy.24.region_ref, f32[14,7]{1,0:T(8,128)S(1)} %copy.25.weight_ref, s32[129]{0:T(256)S(1)} %copy-done.7, s32[129]{0:T(256)S(1)} %copy-done.3, bf16[4,38,24,128]{3,2,1,0:T(8,128)(2,1)S(1)} %all-to-all-done.1.table_ref, bf16[56,20,512]{2,1,0:T(8,128)(2,1)S(1)} %copy-done.1), custom_call_target="tpu_custom_call" | custom-call | tf_op jit(solution)/shard_map/pallas_call | solution.py:310
  78.4 0.8 copy.26
Async XLA Ops:
  6.5 36.4 %copy-start.3 = (s32[129]{0:T(256)S(1)}, s32[129]{0:T(256)}, u32[]{:S(2)}) copy-start(s32[129]{0:T(256)} %new_ref.5) | copy-start | bytes 1552
  6.5 56.3 %all-gather.2.cloned.1.call-start = ((), (), s32[]{:S(2)}) async-start(), calls=%async_computation.2 | async-start | bytes 1720320 | tf_op jit(solution)/shard_map/all_gather | solution.py:276
  10.2 1.0 %copy-start = (bf16[14,20,512]{2,1,0:T(8,128)(2,1)S(1)}, bf16[14,20,512]{2,1,0:T(8,128)(2,1)}, u32[]{:S(2)}) copy-start(bf16[14,20,512]{2,1,0:T(8,128)(2,1)} %copy.21.background_ref) | copy-start | bytes 860164
  11.1 0.7 copy-start.2
  11.8 0.7 copy-start.4
  12.5 0.7 copy-start.5
  13.2 0.7 copy-start.6
  13.9 0.7 copy-start.8
  17.2 25.7 %all-to-all-start = ((bf16[4,12,24,128]{3,2,1,0:T(8,128)(2,1)}), bf16[4,12,24,128]{3,2,1,0:T(8,128)(2,1)S(1)}, u32[]{:S(2)}, u32[]{:S(2)}) async-start(bf16[4,12,24,128]{3,2,1,0:T(8,128)(2,1)} %get-tuple-element.11), calls=%async_computation | async-start | bytes 589824 | tf_op jit(solution)/shard_map/all_to_all | solution.py:293
  20.8 22.1 %collective-permute-start.2 = (bf16[12,24,128]{2,1,0:T(8,128)(2,1)S(1)}, bf16[12,24,128]{2,1,0:T(8,128)(2,1)S(1)}, u32[]{:S(2)}, u32[]{:S(2)}) collective-permute-start(bf16[12,24,128]{2,1,0:T(8,128)(2,1)S(1)} %get-tuple-element.14), channel_id=1, source_target_pairs={{8,20},{12,16},{16,12},{20,8},{24,36},{28,32},{32,28},{36,24},{40,... | collective-permute-start | bytes 221192 | tf_op jit(solution)/shard_map/ppermute | solution.py:298
  32.7 8.2 %collective-permute-start = (bf16[4,24,128]{2,1,0:T(8,128)(2,1)S(1)}, bf16[4,24,128]{2,1,0:T(8,128)(2,1)S(1)}, u32[]{:S(2)}, u32[]{:S(2)}) collective-permute-start(bf16[4,24,128]{2,1,0:T(8,128)(2,1)S(1)} %get-tuple-element.12), channel_id=1, source_target_pairs={{4,16},{12,24},{16,4},{20,32},{24,12},{28,40},{32,20},{36,48},{40,... | collective-permute-start | bytes 73736 | tf_op jit(solution)/shard_map/ppermute | solution.py:298
  35.1 7.8 %collective-permute-start.1 = (bf16[4,24,128]{2,1,0:T(8,128)(2,1)S(1)}, bf16[4,24,128]{2,1,0:T(8,128)(2,1)S(1)}, u32[]{:S(2)}, u32[]{:S(2)}) collective-permute-start(bf16[4,24,128]{2,1,0:T(8,128)(2,1)S(1)} %get-tuple-element.13), channel_id=1, source_target_pairs={{8,16},{12,20},{16,8},{20,12},{24,32},{28,36},{32,24},{36,28},{40,... | collective-permute-start | bytes 73736 | tf_op jit(solution)/shard_map/ppermute | solution.py:298
  42.9 7.1 %copy-start.9 = (s32[14,7]{0,1:T(8,128)S(1)}, s32[14,7]{0,1:T(8,128)}, u32[]{:S(2)}) copy-start(s32[14,7]{0,1:T(8,128)} %param.19) | copy-start | bytes 1180
  42.9 7.2 %copy-start.10 = (f32[14,7]{0,1:T(8,128)S(1)}, f32[14,7]{0,1:T(8,128)}, u32[]{:S(2)}) copy-start(f32[14,7]{0,1:T(8,128)} %param.14) | copy-start | bytes 1180
  43.0 19.9 %copy-start.7 = (s32[129]{0:T(256)S(1)}, s32[129]{0:T(256)}, u32[]{:S(2)}) copy-start(s32[129]{0:T(256)} %old_ref.3) | copy-start | bytes 1552
  45.8 17.0 %all-to-all-start.1 = ((bf16[4,38,24,128]{3,2,1,0:T(8,128)(2,1)}), bf16[4,38,24,128]{3,2,1,0:T(8,128)(2,1)S(1)}, u32[]{:S(2)}, u32[]{:S(2)}) async-start(bf16[4,38,24,128]{3,2,1,0:T(8,128)(2,1)} %shard_map.101), calls=%async_computation.1 | async-start | bytes 1867776 | tf_op jit(solution)/shard_map/all_to_all | solution.py:307
  62.8 1.3 %copy-start.1 = (bf16[56,20,512]{2,1,0:T(8,128)(2,1)S(1)}, bf16[56,20,512]{2,1,0:T(8,128)(2,1)}, u32[]{:S(2)}) copy-start(bf16[56,20,512]{2,1,0:T(8,128)(2,1)} %all-gather.2.cloned.1.call-done.background_ref) | copy-start | bytes 3440644
Sparse Core Ops, SparseCore 0:
  9.5 34.4 all-gather.1

commit v2 on v1

v2 whole, which is shorter than its diff:
```python
import functools
import math

import jax
import jax.numpy as jnp
from jax import lax
from jax.experimental import pallas as pl
from jax.experimental.pallas import tpu as pltpu
from jax.sharding import PartitionSpec as P

MOVE = 2
REACH = 3
HPEER = 3
HCAP = 4
NS_ITERS = 6
LIVE = 10
BLOCK = 4
PADDED = 24
INFLATION = 1.1
PITCH = 16

SWAPS = ((-3, 3, -3, 3), (-2, -2, 2, 2), (-1, -3, 3, 1))

SMEM = pltpu.SMEM
VMEM = pltpu.VMEM
F32 = jnp.float32
BF16 = jnp.bfloat16


def chosen(place, values):
    result = values[0]
    for k in range(1, len(values)):
        result = jnp.where(place == k, values[k], result)
    return result


def padded_rows(x, extra=()):
    rows = x.shape[0] + len(extra)
    zeros = jnp.zeros((PADDED - rows, x.shape[1]), x.dtype)
    return jnp.concatenate([x, *extra, zeros], axis=0)


def pack_kernel(
    count_ref, old_ref, new_ref, halo_ref,
    obs_ref, innovation_ref, precision_ref, background_ref,
    own_ref, state_ref, block_ref, *refs,
):
    swap_refs, (obs_rows, state_rows) = refs[:-2], refs[-2:]
    devices = new_ref.shape[0] - 1
    me = lax.axis_index("tile")
    place = lax.rem(me, BLOCK)
    new_start, new_end = new_ref[me], new_ref[me + 1]
    members, capacity, obs_slots = obs_ref.shape
    pieces = background_ref.shape[2] // obs_slots

    lane = lax.broadcasted_iota(jnp.int32, (1, obs_slots), 1)
    live = [(lane < count_ref[i]).astype(F32) for i in range(capacity)]
    root = jnp.sqrt(precision_ref[...] * jnp.concatenate(live, axis=0))
    pulled = root * innovation_ref[...]
    for m in range(members):
        obs_rows[m * PITCH : m * PITCH + capacity, :] = obs_ref[m].astype(F32) * root
        for c in range(pieces):
            span = slice(c * obs_slots, (c + 1) * obs_slots)
            state_rows[c, m * PITCH : m * PITCH + capacity, :] = background_ref[m, :, span].astype(F32)
    for i in range(LIVE):
        scaled = obs_rows[pl.ds(i, members, stride=PITCH), :]
        own_ref[i] = padded_rows(scaled, (pulled[i : i + 1, :],)).astype(BF16)
    for i in range(capacity):
        for c in range(pieces):
            rows = state_rows[c, pl.ds(i, members, stride=PITCH), :]
            state_ref[i, c] = padded_rows(rows).astype(BF16)

    def pack(reader, put):
        reader = jnp.clip(reader, 0, devices - 1)
        group = 0
        for g in range(1, HPEER):
            first = halo_ref[g * HCAP, reader]
            group = jnp.where((first >= new_start) & (first < new_end), g, group)
        for k in range(HCAP):
            row = jnp.clip(halo_ref[group * HCAP + k, reader] - new_start, 0, LIVE - 1)
            put(k, own_ref[row])

    for j in range(BLOCK):
        def put(k, value, j=j):
            block_ref[j, k] = value
        pack(me - place + j, put)
    for swap, swap_ref in zip(SWAPS, swap_refs):
        def put(k, value, swap_ref=swap_ref):
            swap_ref[k] = value
        pack(me + chosen(place, swap), put)

    old_count = old_ref[me + 1] - old_ref[me]
    for first, inside, slot in (
        (old_count - MOVE, place < BLOCK - 1, place + 1),
        (0, place > 0, place - 1),
    ):
        for t in range(MOVE):
            for c in range(pieces):
                piece = state_ref[first + t, c]
                at = HCAP + t * pieces + c

                @pl.when(inside)
                def _():
                    block_ref[slot, at] = piece

                @pl.when(jnp.logical_not(inside))
                def _():
                    swap_refs[-1][at] = piece


def table_kernel(
    old_hbm, new_hbm, halo_hbm, own_hbm, state_hbm, block_ref, *refs
):
    swap_refs, (out_ref, table_ref, state_ref, old_ref, new_ref, halo_ref, sems) = refs[:-7], refs[-7:]
    fetches = [
        pltpu.make_async_copy(source, target, sems.at[k])
        for k, (source, target) in enumerate((
            (old_hbm, old_ref),
            (new_hbm, new_ref),
            (halo_hbm, halo_ref),
            (own_hbm, table_ref.at[pl.ds(0, LIVE)]),
            (state_hbm, state_ref),
        ))
    ]
    for fetch in fetches:
        fetch.start()
    for fetch in fetches:
        fetch.wait()
    devices = new_ref.shape[0] - 1
    me = lax.axis_index("tile")
    place = lax.rem(me, BLOCK)
    base = me - place
    old_start, old_end, new_start = old_ref[me], old_ref[me + 1], new_ref[me]
    pieces = state_ref.shape[1]

    for g in range(HPEER):
        first = halo_ref[g * HCAP, me]
        peer = me - REACH
        for o in range(1 - REACH, REACH + 1):
            bound = new_ref[jnp.clip(me + o, 0, devices)]
            peer = peer + (bound <= first).astype(jnp.int32)
        at = LIVE + g * HCAP

        @pl.when((peer >= base) & (peer < base + BLOCK))
        def _():
            slot = jnp.clip(peer - base, 0, BLOCK - 1)
            for k in range(HCAP):
                table_ref[at + k] = block_ref[slot, k]

        for swap, swap_ref in zip(SWAPS, swap_refs):
            @pl.when(peer == me + chosen(place, swap))
            def _():
                for k in range(HCAP):
                    table_ref[at + k] = swap_ref[k]

    for i in range(LIVE):
        tile = new_start + i
        at = LIVE + HPEER * HCAP + i * pieces
        stays = (tile >= old_start) & (tile < old_end)
        from_left = tile < old_start
        inside = jnp.where(from_left, place > 0, place < BLOCK - 1)
        left = jnp.clip(tile - old_start + MOVE, 0, MOVE - 1)
        right = jnp.clip(tile - old_end, 0, MOVE - 1)
        begin = HCAP + jnp.where(from_left, left, right) * pieces
        slot = jnp.clip(jnp.where(from_left, place - 1, place + 1), 0, BLOCK - 1)

        @pl.when(stays)
        def _():
            own = jnp.clip(tile - old_start, 0, state_ref.shape[0] - 1)
            for c in range(pieces):
                table_ref[at + c] = state_ref[own, c]

        @pl.when(jnp.logical_not(stays) & inside)
        def _():
            for c in range(pieces):
                table_ref[at + c] = block_ref[slot, begin + c]

        @pl.when(jnp.logical_not(stays) & jnp.logical_not(inside))
        def _():
            for c in range(pieces):
                table_ref[at + c] = swap_refs[-1][begin + c]

    copies = [
        pltpu.make_async_copy(table_ref, out_ref.at[r], sems.at[r])
        for r in range(out_ref.shape[0])
    ]
    for copy in copies:
        copy.start()
    for copy in copies:
        copy.wait()


def split(x):
    high = x.astype(BF16)
    return high, (x - high.astype(F32)).astype(BF16)


def dot(a, b):
    return jnp.dot(a, b, preferred_element_type=F32)


def dot3(a, b):
    return dot(a[0], b[0]) + (dot(a[0], b[1]) + dot(a[1], b[0]))


def analysis_kernel(
    region_ref, weight_ref, new_ref, table_ref, out_ref,
    gram_ref, system_ref, inverse_ref, rows_ref,
):
    me = lax.axis_index("tile")
    rank = lax.axis_index("mem")
    ranks, tiles = table_ref.shape[0], LIVE + HPEER * HCAP
    members, capacity, width = out_ref.shape
    obs_slots = table_ref.shape[3]
    pieces = width // obs_slots
    side = ranks * PADDED
    ensemble = ranks * members
    live_count = new_ref[me + 1] - new_ref[me]

    row = lax.broadcasted_iota(jnp.int32, (side, side), 0)
    column = lax.broadcasted_iota(jnp.int32, (side, side), 1)
    real = (lax.rem(row, PADDED) < members) & (lax.rem(column, PADDED) < members)
    diagonal = (row == column).astype(F32)
    shift = jnp.where(real, diagonal * ((ensemble - 1) / INFLATION), 0.0)
    lane = lax.broadcasted_iota(jnp.int32, (1, side), 1)
    real_lane = lax.rem(lane, PADDED) < members

    def all_members(at):
        rows = [table_ref[r, at].astype(F32) for r in range(ranks)]
        return jnp.concatenate(rows, axis=0).astype(BF16)

    for t in range(tiles):
        block = all_members(t)
        gram_ref[t] = lax.dot_general(
            block, block, (((1,), (1,)), ((), ())), preferred_element_type=F32
        )

    frobenius, pull = [], []
    for i in range(LIVE):
        total = gram_ref[i]
        for e in range(region_ref.shape[0]):
            r = region_ref[e, i]
            at = jnp.where(r < capacity, jnp.minimum(r, LIVE - 1), r - capacity + LIVE)
            total = total + weight_ref[e, i] * gram_ref[at]
        pull.append(jnp.where(real_lane, total[members : members + 1, :], 0.0))
        system = jnp.where(real, total, 0.0) + shift
        squared = jnp.sum(jnp.sum(system * system, axis=0, keepdims=True), axis=1, keepdims=True)
        norm = jnp.sqrt(squared)
        frobenius.append(norm)
        root = system * (1.0 / norm)
        middle = 1.5 * diagonal - 0.5 * root
        inverse_ref[i] = middle
        system_ref[i] = dot3(split(root), split(middle))

    for step in range(1, NS_ITERS):
        for i in range(LIVE):
            root, inverse = split(system_ref[i]), split(inverse_ref[i])
            middle = split(1.5 * diagonal - 0.5 * dot3(inverse, root))
            if step < NS_ITERS - 1:
                system_ref[i] = dot3(root, middle)
            inverse_ref[i] = dot3(middle, inverse)

    own_row = lax.broadcasted_iota(jnp.int32, (PADDED, side), 0)
    for i in range(LIVE):
        inverse = split(inverse_ref[i])
        pulled = jnp.broadcast_to(pull[i], (8, side))
        half_way = dot3(split(pulled), inverse)
        mean_weight = dot3(split(half_way), inverse)[0:1, :] / frobenius[i]
        own = inverse_ref[i, pl.ds(pl.multiple_of(rank * PADDED, 8), PADDED), :]
        spread = (math.sqrt(ensemble - 1) / jnp.sqrt(frobenius[i])) * own
        transform = jnp.where((own_row < members) & real_lane, spread + mean_weight, 0.0)
        transform = transform.astype(BF16)
        keep_share = 1.0 - jnp.sum(transform.astype(F32), axis=1, keepdims=True)
        ones = jnp.where((own_row == members) & real_lane, 1.0, 0.0).astype(BF16)
        weights = transform + ones
        for c in range(pieces):
            blended = dot(weights, all_members(tiles + i * pieces + c))
            mean_state = blended[members : members + 1, :] / ensemble
            analysis = blended[:members] + keep_share[:members] * mean_state
            rows_ref[c, pl.ds(i, members, stride=PITCH), :] = jnp.where(i < live_count, analysis, 0.0)
    for i in range(LIVE, capacity):
        for c in range(pieces):
            rows_ref[c, pl.ds(i, members, stride=PITCH), :] = jnp.zeros((members, obs_slots), F32)
    for m in range(members):
        for c in range(pieces):
            span = slice(c * obs_slots, (c + 1) * obs_slots)
            out_ref[m, :, span] = rows_ref[c, m * PITCH : m * PITCH + capacity, :].astype(BF16)


def shards(
    background, obs_ens, innovation, precision, loc_weight,
    old_split, new_split, obs_count, halo_tiles, region_list,
):
    capacity, members, width = background.shape
    obs_slots = obs_ens.shape[2]
    devices = lax.axis_size("tile")
    ranks = lax.axis_size("mem")
    pieces = width // obs_slots
    tiles = LIVE + HPEER * HCAP
    smem = pl.BlockSpec(memory_space=SMEM)
    vmem = pl.BlockSpec(memory_space=VMEM)
    hbm = pl.BlockSpec(memory_space=pltpu.HBM)

    def params(mebibytes):
        return pltpu.CompilerParams(vmem_limit_bytes=mebibytes << 20)

    def tile_blocks(*leading):
        return jax.ShapeDtypeStruct((*leading, PADDED, obs_slots), BF16)

    background, obs_ens = background.transpose(1, 0, 2), obs_ens.transpose(1, 0, 2)
    halo_tiles, region_list, loc_weight = halo_tiles.T, region_list.T, loc_weight.T

    own, state, block, *swaps = pl.pallas_call(
        pack_kernel,
        out_shape=(
            tile_blocks(LIVE),
            tile_blocks(capacity, pieces),
            tile_blocks(BLOCK, HCAP + MOVE * pieces),
            tile_blocks(HCAP),
            tile_blocks(HCAP),
            tile_blocks(HCAP + MOVE * pieces),
        ),
        in_specs=[smem] * 4 + [vmem] * 4,
        out_specs=[vmem] * 6,
        scratch_shapes=[
            VMEM((members * PITCH, obs_slots), F32),
            VMEM((pieces, members * PITCH, obs_slots), F32),
        ],
        compiler_params=params(56),
    )(obs_count, old_split, new_split, halo_tiles, obs_ens, innovation, precision, background)

    groups = [list(range(b, b + BLOCK)) for b in range(0, devices, BLOCK)]
    block = lax.all_to_all(block, "tile", 0, 0, axis_index_groups=groups, tiled=True)
    arrived = []
    for swap, value in zip(SWAPS, swaps):
        pairs = [(d, d + swap[d % BLOCK]) for d in range(devices)]
        pairs = [(d, e) for d, e in pairs if 0 <= e < devices]
        arrived.append(lax.ppermute(value, "tile", pairs))

    entries = tiles + LIVE * pieces
    table = pl.pallas_call(
        table_kernel,
        out_shape=tile_blocks(ranks, entries),
        in_specs=[hbm] * 5 + [vmem] * 4,
        out_specs=pl.BlockSpec(memory_space=pl.ANY),
        scratch_shapes=[
            VMEM((entries, PADDED, obs_slots), BF16),
            VMEM((capacity, pieces, PADDED, obs_slots), BF16),
            SMEM(old_split.shape, jnp.int32),
            SMEM(new_split.shape, jnp.int32),
            SMEM(halo_tiles.shape, jnp.int32),
            pltpu.SemaphoreType.DMA((max(ranks, 5),)),
        ],
        compiler_params=params(56),
    )(old_split, new_split, halo_tiles, own, state, block, *arrived)
    table = lax.all_to_all(table, "mem", 0, 0, tiled=True)

    side = ranks * PADDED
    analysis = pl.pallas_call(
        analysis_kernel,
        out_shape=jax.ShapeDtypeStruct((members, capacity, width), BF16),
        in_specs=[smem] * 3 + [vmem],
        out_specs=vmem,
        scratch_shapes=[
            VMEM((tiles, side, side), F32),
            VMEM((LIVE, side, side), F32),
            VMEM((LIVE, side, side), F32),
            VMEM((pieces, members * PITCH, obs_slots), F32),
        ],
        compiler_params=params(28),
    )(region_list, loc_weight, new_split, table)
    return analysis.transpose(1, 0, 2)


def solution(mesh):
    in_specs = (
        P("tile", "mem", None),
        P("tile", "mem", None),
        P("tile", None),
        P("tile", None),
        P("tile", None),
        P(),
        P(),
        P("tile"),
        P(),
        P("tile", None),
    )
    out_specs = P("tile", "mem", None)
    return jax.shard_map(shards, mesh=mesh, in_specs=in_specs, out_specs=out_specs, check_vma=False)
```

time: 87 us -> 71.5 us (0.82)
  blocking collectives: 0 us -> 23.5 us
  between operations: 13.5 us -> 0.09 us
  waiting for transfers between devices: 17.5 us -> 5.16 us
  local copies, waits for them, and re-layouts: 10.3 us -> 0.74 us
  starting transfers between devices: 25 us -> 20.7 us
  Pallas kernels: 19.7 us -> 20.6 us
    all_to_all x0 -> x1, blocking collectives: none -> 23.5 us  [shards(): table = lax.all_to_all(table, 'mem', 0, 0, tiled=True)]
    all_to_all x1 -> x0, waiting for transfers between devices: 12.6 us -> none  [shards(): table = lax.all_to_all(table, 'mem', 0, 0, tiled=True)]
    unnamed x27 -> x14, local copies, waits for them, and re-layouts: 9.51 us -> 0.74 us
    all_to_all x1 -> x0, starting transfers between devices: 4.29 us -> none  [shards(): table = lax.all_to_all(table, 'mem', 0, 0, tiled=True)]
    pallas_call x3, Pallas kernels: 19.7 us -> 20.6 us  [the longest x1 14.7 us: shards(): pl.pallas_call(analysis_kernel, out_shape=jax.ShapeDtypeStruct((members,...]
  transfers between devices with their start and end apart: 6 -> 4, of which waited for: 3 -> 2; matrix products, arithmetic and copies ran while one was open for 2% -> 0% of each run, Pallas kernels for 6% -> 0%
where the time goes in v2:
time: 71.5 us; the launch traced here: 70.9 us
  blocking collectives  23.5 us (33%)
  starting transfers between devices  20.7 us (29%)
  Pallas kernels  20.6 us (29%)
  waiting for transfers between devices  5.16 us (7%)
  local copies, waits for them, and re-layouts  0.74 us (1%)
    all_to_all x1, blocking collectives, shards(): table = lax.all_to_all(table, 'mem', 0, 0, tiled=True)  23.5 us
    ppermute x3, starting transfers between devices, shards(): arrived.append(lax.ppermute(value, 'tile', pairs))  17.1 us
    pallas_call x1, Pallas kernels, shards(): pl.pallas_call(analysis_kernel, out_shape=jax.ShapeDtypeStruct((members,...  14.7 us
    ppermute x3, waiting for transfers between devices, shards(): arrived.append(lax.ppermute(value, 'tile', pairs))  5.15 us
    all_to_all x1, starting transfers between devices, shards(): lax.all_to_all(block, 'tile', 0, 0, axis_index_groups=groups, tiled=True)  3.66 us
    pallas_call x1, Pallas kernels, shards(): pl.pallas_call(table_kernel, out_shape=tile_blocks(ranks, entries), in_sp...  3.42 us
    pallas_call x1, Pallas kernels, shards(): pl.pallas_call(pack_kernel, out_shape=(tile_blocks(LIVE), tile_blocks(cap...  2.44 us
  transfers between devices with their start and end apart: 4, of which 2 were waited for; matrix products, arithmetic and copies ran while one was open for 0% of the time, Pallas kernels for 0%

profile of v2, /device:TPU:56, one launch (start us, length us, event | category | flops | bytes accessed | tf_op | source)
XLA Modules:
  0.0 70.9 jit_solution(13920777906474560109)
XLA Ops:
  0.0 2.4 %shard_map.100 = (bf16[10,24,128]{2,1,0:T(8,128)(2,1)}, bf16[14,4,24,128]{3,2,1,0:T(8,128)(2,1)}, bf16[4,12,24,128]{3,2,1,0:T(8,128)(2,1)}, bf16[4,24,128]{2,1,0...) custom-call(s32[14]{0:T(128)} %count_ref.1, s32[129]{0:T(256)} %old_hbm.1, s32[129]{0:T(256)} %new_ref.3, ...), custom_call_target="tpu_custom_call" | custom-call | tf_op jit(solution)/shard_map/pallas_call | solution.py:313
  2.4 3.7 %all-to-all-start = ((bf16[4,12,24,128]{3,2,1,0:T(8,128)(2,1)}), bf16[4,12,24,128]{3,2,1,0:T(8,128)(2,1)S(1)}, u32[]{:S(2)}, u32[]{:S(2)}) async-start(bf16[4,12,24,128]{3,2,1,0:T(8,128)(2,1)} %get-tuple-element.13), calls=%async_computation | async-start | bytes 589824 | tf_op jit(solution)/shard_map/all_to_all | solution.py:333
  6.1 11.8 %collective-permute-start.2 = (bf16[12,24,128]{2,1,0:T(8,128)(2,1)}, bf16[12,24,128]{2,1,0:T(8,128)(2,1)S(1)}, u32[]{:S(2)}, u32[]{:S(2)}) collective-permute-start(bf16[12,24,128]{2,1,0:T(8,128)(2,1)} %get-tuple-element.16), channel_id=1, source_target_pairs={{8,20},{12,16},{16,12},{20,8},{24,36},{28,32},{32,28},{36,24},{40,... | collective-permute-start | bytes 221192 | tf_op jit(solution)/shard_map/ppermute | solution.py:338
  17.9 2.4 %collective-permute-start = (bf16[4,24,128]{2,1,0:T(8,128)(2,1)}, bf16[4,24,128]{2,1,0:T(8,128)(2,1)S(1)}, u32[]{:S(2)}, u32[]{:S(2)}) collective-permute-start(bf16[4,24,128]{2,1,0:T(8,128)(2,1)} %get-tuple-element.14), channel_id=1, source_target_pairs={{4,16},{12,24},{16,4},{20,32},{24,12},{28,40},{32,20},{36,48},{40,... | collective-permute-start | bytes 73736 | tf_op jit(solution)/shard_map/ppermute | solution.py:338
  20.3 2.9 %collective-permute-start.1 = (bf16[4,24,128]{2,1,0:T(8,128)(2,1)}, bf16[4,24,128]{2,1,0:T(8,128)(2,1)S(1)}, u32[]{:S(2)}, u32[]{:S(2)}) collective-permute-start(bf16[4,24,128]{2,1,0:T(8,128)(2,1)} %get-tuple-element.15), channel_id=1, source_target_pairs={{8,16},{12,20},{16,8},{20,12},{24,32},{28,36},{32,24},{36,28},{40,... | collective-permute-start | bytes 73736 | tf_op jit(solution)/shard_map/ppermute | solution.py:338
  23.2 3.1 %collective-permute-done.refs_0_ = bf16[4,24,128]{2,1,0:T(8,128)(2,1)S(1)} collective-permute-done((bf16[4,24,128]{2,1,0:T(8,128)(2,1)}, bf16[4,24,128]{2,1,0:T(8,128)(2,1)S(1)}, u32[]{:S(2)}, u32[]{:S(2)}) %collective-permute-start) | collective-permute-done | bytes 24608 | tf_op jit(solution)/shard_map/ppermute | solution.py:338
  26.3 0.0 copy-start.5
  26.3 2.1 %collective-permute-done.1.refs_1_ = bf16[4,24,128]{2,1,0:T(8,128)(2,1)S(1)} collective-permute-done((bf16[4,24,128]{2,1,0:T(8,128)(2,1)}, bf16[4,24,128]{2,1,0:T(8,128)(2,1)S(1)}, u32[]{:S(2)}, u32[]{:S(2)}) %collective-permute-start.1) | collective-permute-done | bytes 24608 | tf_op jit(solution)/shard_map/ppermute | solution.py:338
  28.4 0.0 copy-start.6
  28.4 0.0 collective-permute-done.2.refs_2_
  28.4 0.0 copy-start.4
  28.4 0.0 all-to-all-done.block_ref
  28.4 0.0 copy-start.3
  28.4 0.0 copy-done.5
  28.4 0.6 copy-done.6
  29.0 0.0 copy-done.4
  29.0 0.1 copy-done.3
  29.1 3.4 %shard_map.101 = bf16[4,62,24,128]{3,2,1,0:T(8,128)(2,1)} custom-call(s32[129]{0:T(256)} %old_hbm.1, s32[129]{0:T(256)} %new_ref.3, s32[12,128]{1,0:T(8,128)} %bitcast.11, bf16[10,24,128]{2,1,0:T(8,128)(2,1)} %get-tuple-element.11.own_hbm, bf16[14,4,24,128]{3,2,1,0:T(8,128)(2,1)} %get-tuple-element.12.state_hbm, bf16[4,12,24,128]{3,2,1,0:T(8,128)(2,1)} %copy-done.3, ...), custom_call_target="tpu_custom_call" | custom-call | tf_op jit(solution)/shard_map/pallas_call | solution.py:341
  32.5 0.0 copy-start
  32.6 0.0 copy-start.1
  32.6 0.0 copy-start.2
  32.6 23.5 %all_to_all.10.table_ref = bf16[4,62,24,128]{3,2,1,0:T(8,128)(2,1)S(1)} all-to-all(bf16[4,62,24,128]{3,2,1,0:T(8,128)(2,1)} %shard_map.101), channel_id=1, replica_groups=mesh['tile'=128,'mem'=4] {'mem'}, dimensions={0} | all-to-all | bytes 3047424 | tf_op jit(solution)/shard_map/all_to_all | solution.py:356
  56.1 0.0 copy-done
  56.1 0.0 copy-done.1
  56.1 0.0 copy-done.2
  56.1 14.7 %shard_map.102 = bf16[20,14,512]{2,1,0:T(8,128)(2,1)} custom-call(s32[7,14]{1,0:T(8,128)S(1)} %bitcast.6, f32[7,14]{1,0:T(8,128)S(1)} %bitcast.7, s32[129]{0:T(256)S(1)} %copy-done, bf16[4,62,24,128]{3,2,1,0:T(8,128)(2,1)S(1)} %all_to_all.10.table_ref), custom_call_target="tpu_custom_call" | custom-call | tf_op jit(solution)/shard_map/pallas_call | solution.py:359
Async XLA Ops:
  2.4 25.9 %all-to-all-start = ((bf16[4,12,24,128]{3,2,1,0:T(8,128)(2,1)}), bf16[4,12,24,128]{3,2,1,0:T(8,128)(2,1)S(1)}, u32[]{:S(2)}, u32[]{:S(2)}) async-start(bf16[4,12,24,128]{3,2,1,0:T(8,128)(2,1)} %get-tuple-element.13), calls=%async_computation | async-start | bytes 589824 | tf_op jit(solution)/shard_map/all_to_all | solution.py:333
  6.1 22.3 %collective-permute-start.2 = (bf16[12,24,128]{2,1,0:T(8,128)(2,1)}, bf16[12,24,128]{2,1,0:T(8,128)(2,1)S(1)}, u32[]{:S(2)}, u32[]{:S(2)}) collective-permute-start(bf16[12,24,128]{2,1,0:T(8,128)(2,1)} %get-tuple-element.16), channel_id=1, source_target_pairs={{8,20},{12,16},{16,12},{20,8},{24,36},{28,32},{32,28},{36,24},{40,... | collective-permute-start | bytes 221192 | tf_op jit(solution)/shard_map/ppermute | solution.py:338
  17.9 8.4 %collective-permute-start = (bf16[4,24,128]{2,1,0:T(8,128)(2,1)}, bf16[4,24,128]{2,1,0:T(8,128)(2,1)S(1)}, u32[]{:S(2)}, u32[]{:S(2)}) collective-permute-start(bf16[4,24,128]{2,1,0:T(8,128)(2,1)} %get-tuple-element.14), channel_id=1, source_target_pairs={{4,16},{12,24},{16,4},{20,32},{24,12},{28,40},{32,20},{36,48},{40,... | collective-permute-start | bytes 73736 | tf_op jit(solution)/shard_map/ppermute | solution.py:338
  20.3 8.0 %collective-permute-start.1 = (bf16[4,24,128]{2,1,0:T(8,128)(2,1)}, bf16[4,24,128]{2,1,0:T(8,128)(2,1)S(1)}, u32[]{:S(2)}, u32[]{:S(2)}) collective-permute-start(bf16[4,24,128]{2,1,0:T(8,128)(2,1)} %get-tuple-element.15), channel_id=1, source_target_pairs={{8,16},{12,20},{16,8},{20,12},{24,32},{28,36},{32,24},{36,28},{40,... | collective-permute-start | bytes 73736 | tf_op jit(solution)/shard_map/ppermute | solution.py:338
  26.3 2.1 %copy-start.5 = (bf16[4,24,128]{2,1,0:T(8,128)(2,1)}, bf16[4,24,128]{2,1,0:T(8,128)(2,1)S(1)}, u32[]{:S(2)}) copy-start(bf16[4,24,128]{2,1,0:T(8,128)(2,1)S(1)} %collective-permute-done.refs_0_) | copy-start | bytes 73732
  28.4 0.6 copy-start.6
  28.4 0.6 copy-start.4
  28.4 0.7 %copy-start.3 = (bf16[4,12,24,128]{3,2,1,0:T(8,128)(2,1)}, bf16[4,12,24,128]{3,2,1,0:T(8,128)(2,1)S(1)}, u32[]{:S(2)}) copy-start(bf16[4,12,24,128]{3,2,1,0:T(8,128)(2,1)S(1)} %all-to-all-done.block_ref) | copy-start | bytes 884740
  32.5 23.6 %copy-start = (s32[129]{0:T(256)S(1)}, s32[129]{0:T(256)}, u32[]{:S(2)}) copy-start(s32[129]{0:T(256)} %new_ref.3) | copy-start | bytes 1552
  32.6 23.5 %copy-start.1 = (s32[14,7]{0,1:T(8,128)S(1)}, s32[14,7]{0,1:T(8,128)}, u32[]{:S(2)}) copy-start(s32[14,7]{0,1:T(8,128)} %param.19) | copy-start | bytes 1180
  32.6 23.5 %copy-start.2 = (f32[14,7]{0,1:T(8,128)S(1)}, f32[14,7]{0,1:T(8,128)}, u32[]{:S(2)}) copy-start(f32[14,7]{0,1:T(8,128)} %param.14) | copy-start | bytes 1180

commit v3 on v2

--- a/solution.py
+++ b/solution.py
@@ -235,7 +235,7 @@
             block, block, (((1,), (1,)), ((), ())), preferred_element_type=F32
         )
 
-    frobenius, pull = [], []
+    frobenius, pull, change = [], [], []
     for i in range(LIVE):
         total = gram_ref[i]
         for e in range(region_ref.shape[0]):
@@ -248,31 +248,39 @@
         norm = jnp.sqrt(squared)
         frobenius.append(norm)
         root = system * (1.0 / norm)
-        middle = 1.5 * diagonal - 0.5 * root
-        inverse_ref[i] = middle
-        system_ref[i] = dot3(split(root), split(middle))
-
-    for step in range(1, NS_ITERS):
+        half = 0.5 * (diagonal - root)
+        system_ref[i] = root
+        inverse_ref[i] = diagonal + half
+        change.append(split(half))
+
+    for step in range(NS_ITERS):
+        if step:
+            change = []
+            for i in range(LIVE):
+                product = dot3(split(inverse_ref[i]), split(system_ref[i]))
+                change.append(split(0.5 * (diagonal - product)))
         for i in range(LIVE):
-            root, inverse = split(system_ref[i]), split(inverse_ref[i])
-            middle = split(1.5 * diagonal - 0.5 * dot3(inverse, root))
+            if step:
+                inverse = inverse_ref[i]
+                inverse_ref[i] = inverse + dot3(change[i], split(inverse))
             if step < NS_ITERS - 1:
-                system_ref[i] = dot3(root, middle)
-            inverse_ref[i] = dot3(middle, inverse)
+                root = system_ref[i]
+                system_ref[i] = root + dot3(split(root), change[i])
 
     own_row = lax.broadcasted_iota(jnp.int32, (PADDED, side), 0)
+    inverses = [split(inverse_ref[i]) for i in range(LIVE)]
+    half_way = [
+        dot3(split(jnp.broadcast_to(pull[i], (8, side))), inverses[i]) for i in range(LIVE)
+    ]
+    mean_weights = [dot3(split(half_way[i]), inverses[i])[0:1, :] for i in range(LIVE)]
     for i in range(LIVE):
-        inverse = split(inverse_ref[i])
-        pulled = jnp.broadcast_to(pull[i], (8, side))
-        half_way = dot3(split(pulled), inverse)
-        mean_weight = dot3(split(half_way), inverse)[0:1, :] / frobenius[i]
+        mean_weight = mean_weights[i] * (1.0 / frobenius[i])
         own = inverse_ref[i, pl.ds(pl.multiple_of(rank * PADDED, 8), PADDED), :]
-        spread = (math.sqrt(ensemble - 1) / jnp.sqrt(frobenius[i])) * own
+        spread = (math.sqrt(ensemble - 1) * lax.rsqrt(frobenius[i])) * own
         transform = jnp.where((own_row < members) & real_lane, spread + mean_weight, 0.0)
         transform = transform.astype(BF16)
         keep_share = 1.0 - jnp.sum(transform.astype(F32), axis=1, keepdims=True)
-        ones = jnp.where((own_row == members) & real_lane, 1.0, 0.0).astype(BF16)
-        weights = transform + ones
+        weights = transform + jnp.where((own_row == members) & real_lane, 1.0, 0.0).astype(BF16)
         for c in range(pieces):
             blended = dot(weights, all_members(tiles + i * pieces + c))
             mean_state = blended[members : members + 1, :] / ensemble

time: 71.5 us -> 62.9 us (0.88)
  Pallas kernels: 20.6 us -> 12 us
    pallas_call x1, Pallas kernels: 14.7 us -> 6.11 us  [shards(): pl.pallas_call(analysis_kernel, out_shape=jax.ShapeDtypeStruct((members,...]
where the time goes in v3:
time: 62.9 us; the launch traced here: 62.2 us
  blocking collectives  23.5 us (37%)
  starting transfers between devices  20.7 us (33%)
  Pallas kernels  12 us (19%)
  waiting for transfers between devices  5.16 us (8%)
  local copies, waits for them, and re-layouts  0.74 us (1%)
    all_to_all x1, blocking collectives, shards(): table = lax.all_to_all(table, 'mem', 0, 0, tiled=True)  23.5 us
    ppermute x3, starting transfers between devices, shards(): arrived.append(lax.ppermute(value, 'tile', pairs))  17.1 us
    pallas_call x1, Pallas kernels, shards(): pl.pallas_call(analysis_kernel, out_shape=jax.ShapeDtypeStruct((members,...  6.11 us
    ppermute x3, waiting for transfers between devices, shards(): arrived.append(lax.ppermute(value, 'tile', pairs))  5.15 us
    all_to_all x1, starting transfers between devices, shards(): lax.all_to_all(block, 'tile', 0, 0, axis_index_groups=groups, tiled=True)  3.66 us
    pallas_call x1, Pallas kernels, shards(): pl.pallas_call(table_kernel, out_shape=tile_blocks(ranks, entries), in_sp...  3.44 us
    pallas_call x1, Pallas kernels, shards(): pl.pallas_call(pack_kernel, out_shape=(tile_blocks(LIVE), tile_blocks(cap...  2.44 us
  transfers between devices with their start and end apart: 4, of which 2 were waited for; matrix products, arithmetic and copies ran while one was open for 0% of the time, Pallas kernels for 0%

profile of v3, /device:TPU:56, one launch (start us, length us, event | category | flops | bytes accessed | tf_op | source)
XLA Modules:
  0.0 62.2 jit_solution(6634973960696765221)
XLA Ops:
  0.0 2.4 %shard_map.100 = (bf16[10,24,128]{2,1,0:T(8,128)(2,1)}, bf16[14,4,24,128]{3,2,1,0:T(8,128)(2,1)}, bf16[4,12,24,128]{3,2,1,0:T(8,128)(2,1)}, bf16[4,24,128]{2,1,0...) custom-call(s32[14]{0:T(128)} %count_ref.1, s32[129]{0:T(256)} %old_hbm.1, s32[129]{0:T(256)} %new_ref.3, ...), custom_call_target="tpu_custom_call" | custom-call | tf_op jit(solution)/shard_map/pallas_call | solution.py:321
  2.4 3.7 %all-to-all-start = ((bf16[4,12,24,128]{3,2,1,0:T(8,128)(2,1)}), bf16[4,12,24,128]{3,2,1,0:T(8,128)(2,1)S(1)}, u32[]{:S(2)}, u32[]{:S(2)}) async-start(bf16[4,12,24,128]{3,2,1,0:T(8,128)(2,1)} %get-tuple-element.13), calls=%async_computation | async-start | bytes 589824 | tf_op jit(solution)/shard_map/all_to_all | solution.py:341
  6.1 11.8 %collective-permute-start.2 = (bf16[12,24,128]{2,1,0:T(8,128)(2,1)}, bf16[12,24,128]{2,1,0:T(8,128)(2,1)S(1)}, u32[]{:S(2)}, u32[]{:S(2)}) collective-permute-start(bf16[12,24,128]{2,1,0:T(8,128)(2,1)} %get-tuple-element.16), channel_id=1, source_target_pairs={{8,20},{12,16},{16,12},{20,8},{24,36},{28,32},{32,28},{36,24},{40,... | collective-permute-start | bytes 221192 | tf_op jit(solution)/shard_map/ppermute | solution.py:346
  17.9 2.4 %collective-permute-start = (bf16[4,24,128]{2,1,0:T(8,128)(2,1)}, bf16[4,24,128]{2,1,0:T(8,128)(2,1)S(1)}, u32[]{:S(2)}, u32[]{:S(2)}) collective-permute-start(bf16[4,24,128]{2,1,0:T(8,128)(2,1)} %get-tuple-element.14), channel_id=1, source_target_pairs={{4,16},{12,24},{16,4},{20,32},{24,12},{28,40},{32,20},{36,48},{40,... | collective-permute-start | bytes 73736 | tf_op jit(solution)/shard_map/ppermute | solution.py:346
  20.3 2.9 %collective-permute-start.1 = (bf16[4,24,128]{2,1,0:T(8,128)(2,1)}, bf16[4,24,128]{2,1,0:T(8,128)(2,1)S(1)}, u32[]{:S(2)}, u32[]{:S(2)}) collective-permute-start(bf16[4,24,128]{2,1,0:T(8,128)(2,1)} %get-tuple-element.15), channel_id=1, source_target_pairs={{8,16},{12,20},{16,8},{20,12},{24,32},{28,36},{32,24},{36,28},{40,... | collective-permute-start | bytes 73736 | tf_op jit(solution)/shard_map/ppermute | solution.py:346
  23.2 3.1 %collective-permute-done.refs_0_ = bf16[4,24,128]{2,1,0:T(8,128)(2,1)S(1)} collective-permute-done((bf16[4,24,128]{2,1,0:T(8,128)(2,1)}, bf16[4,24,128]{2,1,0:T(8,128)(2,1)S(1)}, u32[]{:S(2)}, u32[]{:S(2)}) %collective-permute-start) | collective-permute-done | bytes 24608 | tf_op jit(solution)/shard_map/ppermute | solution.py:346
  26.3 0.0 copy-start.5
  26.3 2.1 %collective-permute-done.1.refs_1_ = bf16[4,24,128]{2,1,0:T(8,128)(2,1)S(1)} collective-permute-done((bf16[4,24,128]{2,1,0:T(8,128)(2,1)}, bf16[4,24,128]{2,1,0:T(8,128)(2,1)S(1)}, u32[]{:S(2)}, u32[]{:S(2)}) %collective-permute-start.1) | collective-permute-done | bytes 24608 | tf_op jit(solution)/shard_map/ppermute | solution.py:346
  28.4 0.0 copy-start.6
  28.4 0.0 collective-permute-done.2.refs_2_
  28.4 0.0 copy-start.4
  28.4 0.0 all-to-all-done.block_ref
  28.4 0.0 copy-start.3
  28.4 0.0 copy-done.5
  28.4 0.6 copy-done.6
  29.0 0.0 copy-done.4
  29.0 0.1 copy-done.3
  29.1 3.4 %shard_map.101 = bf16[4,62,24,128]{3,2,1,0:T(8,128)(2,1)} custom-call(s32[129]{0:T(256)} %old_hbm.1, s32[129]{0:T(256)} %new_ref.3, s32[12,128]{1,0:T(8,128)} %bitcast.11, bf16[10,24,128]{2,1,0:T(8,128)(2,1)} %get-tuple-element.11.own_hbm, bf16[14,4,24,128]{3,2,1,0:T(8,128)(2,1)} %get-tuple-element.12.state_hbm, bf16[4,12,24,128]{3,2,1,0:T(8,128)(2,1)} %copy-done.3, ...), custom_call_target="tpu_custom_call" | custom-call | tf_op jit(solution)/shard_map/pallas_call | solution.py:349
  32.6 0.0 copy-start
  32.6 0.0 copy-start.1
  32.6 0.0 copy-start.2
  32.6 23.5 %all_to_all.10.table_ref = bf16[4,62,24,128]{3,2,1,0:T(8,128)(2,1)S(1)} all-to-all(bf16[4,62,24,128]{3,2,1,0:T(8,128)(2,1)} %shard_map.101), channel_id=1, replica_groups=mesh['tile'=128,'mem'=4] {'mem'}, dimensions={0} | all-to-all | bytes 3047424 | tf_op jit(solution)/shard_map/all_to_all | solution.py:364
  56.1 0.0 copy-done
  56.1 0.0 copy-done.1
  56.1 0.0 copy-done.2
  56.1 6.1 %shard_map.102 = bf16[20,14,512]{2,1,0:T(8,128)(2,1)} custom-call(s32[7,14]{1,0:T(8,128)S(1)} %bitcast.6, f32[7,14]{1,0:T(8,128)S(1)} %bitcast.7, s32[129]{0:T(256)S(1)} %copy-done, bf16[4,62,24,128]{3,2,1,0:T(8,128)(2,1)S(1)} %all_to_all.10.table_ref), custom_call_target="tpu_custom_call" | custom-call | tf_op jit(solution)/shard_map/pallas_call | solution.py:367
Async XLA Ops:
  2.4 25.9 %all-to-all-start = ((bf16[4,12,24,128]{3,2,1,0:T(8,128)(2,1)}), bf16[4,12,24,128]{3,2,1,0:T(8,128)(2,1)S(1)}, u32[]{:S(2)}, u32[]{:S(2)}) async-start(bf16[4,12,24,128]{3,2,1,0:T(8,128)(2,1)} %get-tuple-element.13), calls=%async_computation | async-start | bytes 589824 | tf_op jit(solution)/shard_map/all_to_all | solution.py:341
  6.1 22.3 %collective-permute-start.2 = (bf16[12,24,128]{2,1,0:T(8,128)(2,1)}, bf16[12,24,128]{2,1,0:T(8,128)(2,1)S(1)}, u32[]{:S(2)}, u32[]{:S(2)}) collective-permute-start(bf16[12,24,128]{2,1,0:T(8,128)(2,1)} %get-tuple-element.16), channel_id=1, source_target_pairs={{8,20},{12,16},{16,12},{20,8},{24,36},{28,32},{32,28},{36,24},{40,... | collective-permute-start | bytes 221192 | tf_op jit(solution)/shard_map/ppermute | solution.py:346
  17.9 8.4 %collective-permute-start = (bf16[4,24,128]{2,1,0:T(8,128)(2,1)}, bf16[4,24,128]{2,1,0:T(8,128)(2,1)S(1)}, u32[]{:S(2)}, u32[]{:S(2)}) collective-permute-start(bf16[4,24,128]{2,1,0:T(8,128)(2,1)} %get-tuple-element.14), channel_id=1, source_target_pairs={{4,16},{12,24},{16,4},{20,32},{24,12},{28,40},{32,20},{36,48},{40,... | collective-permute-start | bytes 73736 | tf_op jit(solution)/shard_map/ppermute | solution.py:346
  20.3 8.0 %collective-permute-start.1 = (bf16[4,24,128]{2,1,0:T(8,128)(2,1)}, bf16[4,24,128]{2,1,0:T(8,128)(2,1)S(1)}, u32[]{:S(2)}, u32[]{:S(2)}) collective-permute-start(bf16[4,24,128]{2,1,0:T(8,128)(2,1)} %get-tuple-element.15), channel_id=1, source_target_pairs={{8,16},{12,20},{16,8},{20,12},{24,32},{28,36},{32,24},{36,28},{40,... | collective-permute-start | bytes 73736 | tf_op jit(solution)/shard_map/ppermute | solution.py:346
  26.3 2.1 %copy-start.5 = (bf16[4,24,128]{2,1,0:T(8,128)(2,1)}, bf16[4,24,128]{2,1,0:T(8,128)(2,1)S(1)}, u32[]{:S(2)}) copy-start(bf16[4,24,128]{2,1,0:T(8,128)(2,1)S(1)} %collective-permute-done.refs_0_) | copy-start | bytes 73732
  28.4 0.6 copy-start.6
  28.4 0.6 %copy-start.4 = (bf16[12,24,128]{2,1,0:T(8,128)(2,1)}, bf16[12,24,128]{2,1,0:T(8,128)(2,1)S(1)}, u32[]{:S(2)}) copy-start(bf16[12,24,128]{2,1,0:T(8,128)(2,1)S(1)} %collective-permute-done.2.refs_2_) | copy-start | bytes 221188
  28.4 0.7 %copy-start.3 = (bf16[4,12,24,128]{3,2,1,0:T(8,128)(2,1)}, bf16[4,12,24,128]{3,2,1,0:T(8,128)(2,1)S(1)}, u32[]{:S(2)}) copy-start(bf16[4,12,24,128]{3,2,1,0:T(8,128)(2,1)S(1)} %all-to-all-done.block_ref) | copy-start | bytes 884740
  32.6 23.5 %copy-start = (s32[129]{0:T(256)S(1)}, s32[129]{0:T(256)}, u32[]{:S(2)}) copy-start(s32[129]{0:T(256)} %new_ref.3) | copy-start | bytes 1552
  32.6 23.5 %copy-start.1 = (s32[14,7]{0,1:T(8,128)S(1)}, s32[14,7]{0,1:T(8,128)}, u32[]{:S(2)}) copy-start(s32[14,7]{0,1:T(8,128)} %param.19) | copy-start | bytes 1180
  32.6 23.5 %copy-start.2 = (f32[14,7]{0,1:T(8,128)S(1)}, f32[14,7]{0,1:T(8,128)}, u32[]{:S(2)}) copy-start(f32[14,7]{0,1:T(8,128)} %param.14) | copy-start | bytes 1180

commit v4 on v3

v4 whole, which is shorter than its diff:
```python
import functools
import math

import jax
import jax.numpy as jnp
from jax import lax
from jax.experimental import pallas as pl
from jax.experimental.pallas import tpu as pltpu
from jax.sharding import PartitionSpec as P

MOVE = 2
REACH = 3
HPEER = 3
HCAP = 4
NS_ITERS = 6
LIVE = 10
BLOCK = 4
PADDED = 24
INFLATION = 1.1
COST = pl.CostEstimate(flops=1 << 20, bytes_accessed=4 << 20, transcendentals=0)
PITCH = 16

SWAPS = ((-3, 3, -3, 3), (-2, -2, 2, 2), (-1, -3, 3, 1))

SMEM = pltpu.SMEM
VMEM = pltpu.VMEM
F32 = jnp.float32
BF16 = jnp.bfloat16


def chosen(place, values):
    result = values[0]
    for k in range(1, len(values)):
        result = jnp.where(place == k, values[k], result)
    return result


def padded_to(x, rows):
    return jnp.concatenate([x, jnp.zeros((rows - x.shape[0], x.shape[1]), x.dtype)], axis=0)


def paired(x, y):
    return jnp.concatenate([x.astype(F32), y.astype(F32)], axis=0).astype(BF16)


def pack_kernel(
    count_ref, old_ref, new_ref, halo_ref,
    obs_ref, innovation_ref, precision_ref, background_ref,
    own_ref, pulled_ref, block_ref, *refs,
):
    swap_refs, (obs_rows, state_rows) = refs[:-2], refs[-2:]
    devices = new_ref.shape[0] - 1
    me = lax.axis_index("tile")
    place = lax.rem(me, BLOCK)
    new_start, new_end = new_ref[me], new_ref[me + 1]
    members, capacity, obs_slots = obs_ref.shape
    pieces = background_ref.shape[2] // obs_slots

    lane = lax.broadcasted_iota(jnp.int32, (1, obs_slots), 1)
    live = [(lane < count_ref[i]).astype(F32) for i in range(capacity)]
    root = jnp.sqrt(precision_ref[...] * jnp.concatenate(live, axis=0))
    pulled = root * innovation_ref[...]
    for m in range(members):
        obs_rows[m * PITCH : m * PITCH + capacity, :] = obs_ref[m].astype(F32) * root
        for c in range(pieces):
            span = slice(c * obs_slots, (c + 1) * obs_slots)
            state_rows[c, m * PITCH : m * PITCH + capacity, :] = background_ref[m, :, span].astype(F32)
    pulled_ref[...] = padded_to(pulled, PITCH).astype(BF16).astype(F32)
    for i in range(LIVE):
        scaled = obs_rows[pl.ds(i, members, stride=PITCH), :]
        own_ref[i] = padded_to(jnp.concatenate([scaled, pulled[i : i + 1, :]], axis=0), PADDED).astype(BF16)

    def pack(reader, put):
        reader = jnp.clip(reader, 0, devices - 1)
        group = 0
        for g in range(1, HPEER):
            first = halo_ref[g * HCAP, reader]
            group = jnp.where((first >= new_start) & (first < new_end), g, group)
        for k in range(HCAP):
            row = jnp.clip(halo_ref[group * HCAP + k, reader] - new_start, 0, LIVE - 1)
            put(k, own_ref[row])

    for j in range(BLOCK):
        def put(k, value, j=j):
            block_ref[j, k] = value
        pack(me - place + j, put)
    for swap, swap_ref in zip(SWAPS, swap_refs):
        def put(k, value, swap_ref=swap_ref):
            swap_ref[k] = value
        pack(me + chosen(place, swap), put)

    old_count = old_ref[me + 1] - old_ref[me]
    for first, inside, slot in (
        (old_count - MOVE, place < BLOCK - 1, place + 1),
        (0, place > 0, place - 1),
    ):
        for t in range(MOVE):
            for c in range(pieces):
                piece = state_rows[c, pl.ds(first + t, members, stride=PITCH), :]
                piece = padded_to(piece, PADDED).astype(BF16)
                at = HCAP + t * pieces + c

                @pl.when(inside)
                def _():
                    block_ref[slot, at] = piece

                @pl.when(jnp.logical_not(inside))
                def _():
                    swap_refs[-1][at] = piece


def own_table_kernel(
    old_ref, new_ref, own_ref, background_ref, out_ref, table_ref, state_rows, sems
):
    me = lax.axis_index("tile")
    old_start, old_end, new_start = old_ref[me], old_ref[me + 1], new_ref[me]
    members, capacity, width = background_ref.shape
    obs_slots = own_ref.shape[2]
    pieces = width // obs_slots
    for m in range(members):
        for c in range(pieces):
            span = slice(c * obs_slots, (c + 1) * obs_slots)
            state_rows[c, m * PITCH : m * PITCH + capacity, :] = background_ref[m, :, span].astype(F32)
    for i in range(0, LIVE, 2):
        table_ref[i // 2] = paired(own_ref[i][:members], own_ref[i + 1][:members])
    for i in range(LIVE):
        at = jnp.clip(new_start + i - old_start, 0, capacity - 1)
        rows = [state_rows[c, pl.ds(at, members, stride=PITCH), :] for c in range(pieces)]
        for c in range(0, pieces, 2):
            table_ref[(LIVE + HPEER * HCAP + i * pieces + c) // 2] = paired(rows[c], rows[c + 1])
    copies = [
        pltpu.make_async_copy(table_ref, out_ref.at[r], sems.at[r])
        for r in range(out_ref.shape[0])
    ]
    for copy in copies:
        copy.start()
    for copy in copies:
        copy.wait()


def table_kernel(old_ref, new_ref, halo_ref, table_ref, block_ref, *refs):
    swap_refs, (out_ref, pulled_ref, halo_rows, moved_rows, halo_sems, moved_sems) = refs[:-6], refs[-6:]
    devices = new_ref.shape[0] - 1
    me = lax.axis_index("tile")
    place = lax.rem(me, BLOCK)
    base = me - place
    old_start, old_end = old_ref[me], old_ref[me + 1]
    new_start, new_end = new_ref[me], new_ref[me + 1]
    ranks, _, pair_rows, _ = out_ref.shape
    members = pair_rows // 2
    pieces = (block_ref.shape[1] - HCAP) // MOVE
    pulled_ref[...] = jnp.zeros(pulled_ref.shape, F32)

    moves = []
    for j in range(MOVE):
        tile = new_start + j
        index = jnp.clip(tile - old_start + MOVE, 0, MOVE - 1)
        moves.append((tile < old_start, j, index, place > 0, place - 1))
    for j in range(MOVE):
        tile = old_end + j
        slot = jnp.clip(tile - new_start, 0, LIVE - 1)
        moves.append((tile < new_end, slot, j, place < BLOCK - 1, place + 1))
    copies = []
    for n, (comes, slot, index, inside, source) in enumerate(moves):
        begin = HCAP + index * pieces
        source = jnp.clip(source, 0, BLOCK - 1)
        at = (LIVE + HPEER * HCAP + slot * pieces) // 2
        mine = [
            pltpu.make_async_copy(
                moved_rows.at[n], out_ref.at[r, pl.ds(at, pieces // 2)], moved_sems.at[n, r]
            )
            for r in range(ranks)
        ]
        copies.append((comes, mine))

        def put(read, n=n):
            for c in range(0, pieces, 2):
                moved_rows[n, c // 2] = paired(read(c)[:members], read(c + 1)[:members])

        @pl.when(comes & inside)
        def _():
            put(lambda c: block_ref[source, begin + c])

        @pl.when(comes & jnp.logical_not(inside))
        def _():
            put(lambda c: swap_refs[-1][begin + c])

        @pl.when(comes)
        def _():
            for copy in mine:
                copy.start()

    for g in range(HPEER):
        first = halo_ref[g * HCAP, me]
        peer = me - REACH
        for o in range(1 - REACH, REACH + 1):
            bound = new_ref[jnp.clip(me + o, 0, devices)]
            peer = peer + (bound <= first).astype(jnp.int32)

        def put(read, g=g):
            for k in range(HCAP):
                at = g * HCAP + k
                pulled_ref[at : at + 1, :] = read(k).astype(F32)[members : members + 1]
            for k in range(0, HCAP, 2):
                halo_rows[(g * HCAP + k) // 2] = paired(read(k)[:members], read(k + 1)[:members])

        @pl.when((peer >= base) & (peer < base + BLOCK))
        def _():
            slot = jnp.clip(peer - base, 0, BLOCK - 1)
            put(lambda k: block_ref[slot, k])

        for swap, swap_ref in zip(SWAPS, swap_refs):
            @pl.when(peer == me + chosen(place, swap))
            def _():
                put(lambda k: swap_ref[k])

    halo = [
        pltpu.make_async_copy(
            halo_rows, out_ref.at[r, pl.ds(LIVE // 2, HPEER * HCAP // 2)], halo_sems.at[r]
        )
        for r in range(ranks)
    ]
    for copy in halo:
        copy.start()
    for comes, mine in copies:
        @pl.when(comes)
        def _():
            for copy in mine:
                copy.wait()
    for copy in halo:
        copy.wait()


def split(x):
    high = x.astype(BF16)
    return high, (x - high.astype(F32)).astype(BF16)


def dot(a, b):
    return jnp.dot(a, b, preferred_element_type=F32)


def dot3(a, b):
    return dot(a[0], b[0]) + (dot(a[0], b[1]) + dot(a[1], b[0]))


def analysis_kernel(
    region_ref, weight_ref, new_ref, own_pulled_ref, halo_pulled_ref, table_ref, out_ref,
    gram_ref, system_ref, inverse_ref, rows_ref,
):
    me = lax.axis_index("tile")
    rank = lax.axis_index("mem")
    ranks, tiles = table_ref.shape[0], LIVE + HPEER * HCAP
    members, capacity, width = out_ref.shape
    obs_slots = table_ref.shape[3]
    pieces = width // obs_slots
    side = ranks * members
    live_count = new_ref[me + 1] - new_ref[me]

    row = lax.broadcasted_iota(jnp.int32, (side, side), 0)
    column = lax.broadcasted_iota(jnp.int32, (side, side), 1)
    diagonal = (row == column).astype(F32)
    shift = diagonal * ((side - 1) / INFLATION)

    def all_members(pair):
        rows = [table_ref[r, pair].astype(F32) for r in range(ranks)]
        return [
            jnp.concatenate([x[k * members : (k + 1) * members] for x in rows], axis=0).astype(BF16)
            for k in range(2)
        ]

    for t in range(0, tiles, 2):
        for k, block in enumerate(all_members(t // 2)):
            at = t + k
            pulled_ref, where = (own_pulled_ref, at) if at < LIVE else (halo_pulled_ref, at - LIVE)
            pulled = padded_to(pulled_ref[where : where + 1, :], PITCH).astype(BF16)
            product = lax.dot_general(
                jnp.concatenate([block, pulled], axis=0), block,
                (((1,), (1,)), ((), ())), preferred_element_type=F32,
            )
            gram_ref[at] = product[: side + 8]

    frobenius, pull, change = [], [], []
    for i in range(LIVE):
        total = gram_ref[i]
        for e in range(region_ref.shape[0]):
            r = region_ref[e, i]
            at = jnp.where(r < capacity, jnp.minimum(r, LIVE - 1), r - capacity + LIVE)
            total = total + weight_ref[e, i] * gram_ref[at]
        pull.append(total[side : side + 1, :])
        system = total[:side] + shift
        squared = jnp.sum(jnp.sum(system * system, axis=0, keepdims=True), axis=1, keepdims=True)
        norm = jnp.sqrt(squared)
        frobenius.append(norm)
        root = system * (1.0 / norm)
        half = 0.5 * (diagonal - root)
        system_ref[i] = root
        inverse_ref[i] = diagonal + half
        change.append(split(half))

    for step in range(NS_ITERS):
        if step:
            change = []
            for i in range(LIVE):
                product = dot3(split(inverse_ref[i]), split(system_ref[i]))
                change.append(split(0.5 * (diagonal - product)))
        for i in range(LIVE):
            if step:
                inverse = inverse_ref[i]
                inverse_ref[i] = inverse + dot3(change[i], split(inverse))
            if step < NS_ITERS - 1:
                root = system_ref[i]
                system_ref[i] = root + dot3(split(root), change[i])

    start = pl.multiple_of(rank * members // 8 * 8, 8)
    begins_inside = rank * members > start
    ones = jnp.ones((1, side), F32)
    inverses = [split(inverse_ref[i]) for i in range(LIVE)]
    half_way = [
        dot3(split(jnp.broadcast_to(pull[i], (8, side))), inverses[i]) for i in range(LIVE)
    ]
    mean_weights = [dot3(split(half_way[i]), inverses[i])[0:1, :] for i in range(LIVE)]
    for i in range(LIVE):
        mean_weight = mean_weights[i] * (1.0 / frobenius[i])
        own = inverse_ref[i, pl.ds(start, PADDED), :]
        own = jnp.where(begins_inside, own[PADDED - members :], own[:members])
        transform = (math.sqrt(side - 1) * lax.rsqrt(frobenius[i])) * own + mean_weight
        transform = transform.astype(BF16).astype(F32)
        keep_share = 1.0 - jnp.sum(transform, axis=1, keepdims=True)
        weights = padded_to(jnp.concatenate([transform, ones], axis=0), 2 * PITCH).astype(BF16)
        state = [x for c in range(0, pieces, 2) for x in all_members((tiles + i * pieces + c) // 2)]
        for c in range(pieces):
            blended = dot(weights, state[c])
            mean_state = blended[members : members + 1, :] / side
            analysis = blended[:members] + keep_share * mean_state
            rows_ref[c, pl.ds(i, members, stride=PITCH), :] = jnp.where(i < live_count, analysis, 0.0)
    for i in range(LIVE, capacity):
        for c in range(pieces):
            rows_ref[c, pl.ds(i, members, stride=PITCH), :] = jnp.zeros((members, obs_slots), F32)
    for m in range(members):
        for c in range(pieces):
            span = slice(c * obs_slots, (c + 1) * obs_slots)
            out_ref[m, :, span] = rows_ref[c, m * PITCH : m * PITCH + capacity, :].astype(BF16)


def shards(
    background, obs_ens, innovation, precision, loc_weight,
    old_split, new_split, obs_count, halo_tiles, region_list,
):
    capacity, members, width = background.shape
    obs_slots = obs_ens.shape[2]
    devices = lax.axis_size("tile")
    ranks = lax.axis_size("mem")
    pieces = width // obs_slots
    tiles = LIVE + HPEER * HCAP
    smem = pl.BlockSpec(memory_space=SMEM)
    vmem = pl.BlockSpec(memory_space=VMEM)
    hbm = pl.BlockSpec(memory_space=pltpu.HBM)

    def params(mebibytes):
        return pltpu.CompilerParams(vmem_limit_bytes=mebibytes << 20)

    def tile_blocks(*leading):
        return jax.ShapeDtypeStruct((*leading, PADDED, obs_slots), BF16)

    background, obs_ens = background.transpose(1, 0, 2), obs_ens.transpose(1, 0, 2)
    halo_tiles, region_list, loc_weight = halo_tiles.T, region_list.T, loc_weight.T

    own, own_pulled, block, *swaps = pl.pallas_call(
        pack_kernel,
        out_shape=(
            tile_blocks(LIVE),
            jax.ShapeDtypeStruct((PITCH, obs_slots), F32),
            tile_blocks(BLOCK, HCAP + MOVE * pieces),
            tile_blocks(HCAP),
            tile_blocks(HCAP),
            tile_blocks(HCAP + MOVE * pieces),
        ),
        in_specs=[smem] * 4 + [vmem] * 4,
        out_specs=[vmem] * 6,
        scratch_shapes=[
            VMEM((members * PITCH, obs_slots), F32),
            VMEM((pieces, members * PITCH, obs_slots), F32),
        ],
        compiler_params=params(56),
    )(obs_count, old_split, new_split, halo_tiles, obs_ens, innovation, precision, background)

    groups = [list(range(b, b + BLOCK)) for b in range(0, devices, BLOCK)]
    block = lax.all_to_all(block, "tile", 0, 0, axis_index_groups=groups, tiled=True)
    arrived = []
    for swap, value in zip(SWAPS, swaps):
        pairs = [(d, d + swap[d % BLOCK]) for d in range(devices)]
        pairs = [(d, e) for d, e in pairs if 0 <= e < devices]
        arrived.append(lax.ppermute(value, "tile", pairs))

    table_shape = (ranks, (tiles + LIVE * pieces) // 2, 2 * members, obs_slots)
    table = pl.pallas_call(
        own_table_kernel,
        out_shape=jax.ShapeDtypeStruct(table_shape, BF16),
        in_specs=[smem] * 2 + [vmem] * 2,
        out_specs=pl.BlockSpec(memory_space=pl.ANY),
        scratch_shapes=[
            VMEM(table_shape[1:], BF16),
            VMEM((pieces, members * PITCH, obs_slots), F32),
            pltpu.SemaphoreType.DMA((ranks,)),
        ],
        compiler_params=params(56),
        cost_estimate=COST,
    )(old_split, new_split, own, background)
    table, halo_pulled = pl.pallas_call(
        table_kernel,
        out_shape=(
            jax.ShapeDtypeStruct(table_shape, BF16),
            jax.ShapeDtypeStruct((PITCH, obs_slots), F32),
        ),
        in_specs=[smem] * 3 + [pl.BlockSpec(memory_space=pl.ANY)] + [vmem] * 4,
        out_specs=(pl.BlockSpec(memory_space=pl.ANY), vmem),
        input_output_aliases={3: 0},
        scratch_shapes=[
            VMEM((HPEER * HCAP // 2, 2 * members, obs_slots), BF16),
            VMEM((2 * MOVE, pieces // 2, 2 * members, obs_slots), BF16),
            pltpu.SemaphoreType.DMA((ranks,)),
            pltpu.SemaphoreType.DMA((2 * MOVE, ranks)),
        ],
        compiler_params=params(56),
    )(old_split, new_split, halo_tiles, table, block, *arrived)
    table = lax.all_to_all(table, "mem", 0, 0, tiled=True)

    side = ranks * members
    analysis = pl.pallas_call(
        analysis_kernel,
        out_shape=jax.ShapeDtypeStruct((members, capacity, width), BF16),
        in_specs=[smem] * 3 + [vmem] * 3,
        out_specs=vmem,
        scratch_shapes=[
            VMEM((tiles, side + 8, side), F32),
            VMEM((LIVE, side, side), F32),
            VMEM((LIVE, side, side), F32),
            VMEM((pieces, members * PITCH, obs_slots), F32),
        ],
        compiler_params=params(28),
    )(region_list, loc_weight, new_split, own_pulled, halo_pulled, table)
    return analysis.transpose(1, 0, 2)


def solution(mesh):
    in_specs = (
        P("tile", "mem", None),
        P("tile", "mem", None),
        P("tile", None),
        P("tile", None),
        P("tile", None),
        P(),
        P(),
        P("tile"),
        P(),
        P("tile", None),
    )
    out_specs = P("tile", "mem", None)
    return jax.shard_map(shards, mesh=mesh, in_specs=in_specs, out_specs=out_specs, check_vma=False)
```

time: 62.9 us -> 61.6 us (0.979)
  Pallas kernels: 12 us -> 15.1 us
  blocking collectives: 23.5 us -> 20.8 us
  waiting for transfers between devices: 5.16 us -> 2.76 us
  local copies, waits for them, and re-layouts: 0.74 us -> 1.37 us
    all_to_all x1, blocking collectives: 23.5 us -> 20.8 us  [shards(): table = lax.all_to_all(table, 'mem', 0, 0, tiled=True)]
    ppermute x3, waiting for transfers between devices: 5.15 us -> 2.76 us  [shards(): arrived.append(lax.ppermute(value, 'tile', pairs))]
    pallas_call x1, Pallas kernels: 6.11 us -> 7.8 us  [shards(): pl.pallas_call(analysis_kernel, out_shape=jax.ShapeDtypeStruct((members,...]
    pallas_call x2 -> x3, Pallas kernels: 5.88 us -> 7.3 us  [the longest x1 2.71 us: shards(): pl.pallas_call(table_kernel, out_shape=(jax.ShapeDtypeStruct(table_shape,...]
    unnamed x14 -> x18, local copies, waits for them, and re-layouts: 0.74 us -> 1.37 us
  transfers between devices with their start and end apart: 4 -> 4, of which waited for: 2 -> 2; matrix products, arithmetic and copies ran while one was open for 0% -> 0% of each run, Pallas kernels for 0% -> 4%
where the time goes in v4:
time: 61.6 us; the launch traced here: 60.9 us
  blocking collectives  20.8 us (34%)
  starting transfers between devices  20.7 us (34%)
  Pallas kernels  15.1 us (25%)
  waiting for transfers between devices  2.76 us (4%)
  local copies, waits for them, and re-layouts  1.37 us (2%)
    all_to_all x1, blocking collectives, shards(): table = lax.all_to_all(table, 'mem', 0, 0, tiled=True)  20.8 us
    ppermute x3, starting transfers between devices, shards(): arrived.append(lax.ppermute(value, 'tile', pairs))  17.1 us
    pallas_call x1, Pallas kernels, shards(): pl.pallas_call(analysis_kernel, out_shape=jax.ShapeDtypeStruct((members,...  7.8 us
    all_to_all x1, starting transfers between devices, shards(): lax.all_to_all(block, 'tile', 0, 0, axis_index_groups=groups, tiled=True)  3.66 us
    ppermute x3, waiting for transfers between devices, shards(): arrived.append(lax.ppermute(value, 'tile', pairs))  2.76 us
    pallas_call x1, Pallas kernels, shards(): pl.pallas_call(table_kernel, out_shape=(jax.ShapeDtypeStruct(table_shape,...  2.71 us
    pallas_call x1, Pallas kernels, shards(): pl.pallas_call(own_table_kernel, out_shape=jax.ShapeDtypeStruct(table_sha...  2.39 us
    pallas_call x1, Pallas kernels, shards(): pl.pallas_call(pack_kernel, out_shape=(tile_blocks(LIVE), jax.ShapeDtypeS...  2.2 us
  transfers between devices with their start and end apart: 4, of which 2 were waited for; matrix products, arithmetic and copies ran while one was open for 0% of the time, Pallas kernels for 4%

profile of v4, /device:TPU:56, one launch (start us, length us, event | category | flops | bytes accessed | tf_op | source)
XLA Modules:
  0.0 60.9 jit_solution(7962053058610588023)
XLA Ops:
  0.0 2.2 %shard_map.100 = (bf16[10,24,128]{2,1,0:T(8,128)(2,1)}, f32[16,128]{1,0:T(8,128)}, bf16[4,12,24,128]{3,2,1,0:T(8,128)(2,1)}, bf16[4,24,128]{2,1,0:T(8,128)(2,1)}...) custom-call(s32[14]{0:T(128)} %count_ref.1, s32[129]{0:T(256)} %old_ref.5, s32[129]{0:T(256)} %new_ref.7, ...), custom_call_target="tpu_custom_call" | custom-call | tf_op jit(solution)/shard_map/pallas_call | solution.py:369
  2.2 3.7 %all-to-all-start = ((bf16[4,12,24,128]{3,2,1,0:T(8,128)(2,1)}), bf16[4,12,24,128]{3,2,1,0:T(8,128)(2,1)S(1)}, u32[]{:S(2)}, u32[]{:S(2)}) async-start(bf16[4,12,24,128]{3,2,1,0:T(8,128)(2,1)} %get-tuple-element.15), calls=%async_computation | async-start | bytes 589824 | tf_op jit(solution)/shard_map/all_to_all | solution.py:389
  5.9 11.8 %collective-permute-start.2 = (bf16[12,24,128]{2,1,0:T(8,128)(2,1)}, bf16[12,24,128]{2,1,0:T(8,128)(2,1)S(1)}, u32[]{:S(2)}, u32[]{:S(2)}) collective-permute-start(bf16[12,24,128]{2,1,0:T(8,128)(2,1)} %get-tuple-element.18), channel_id=1, source_target_pairs={{8,20},{12,16},{16,12},{20,8},{24,36},{28,32},{32,28},{36,24},{40,... | collective-permute-start | bytes 221192 | tf_op jit(solution)/shard_map/ppermute | solution.py:394
  17.7 2.4 %collective-permute-start = (bf16[4,24,128]{2,1,0:T(8,128)(2,1)}, bf16[4,24,128]{2,1,0:T(8,128)(2,1)S(1)}, u32[]{:S(2)}, u32[]{:S(2)}) collective-permute-start(bf16[4,24,128]{2,1,0:T(8,128)(2,1)} %get-tuple-element.16), channel_id=1, source_target_pairs={{4,16},{12,24},{16,4},{20,32},{24,12},{28,40},{32,20},{36,48},{40,... | collective-permute-start | bytes 73736 | tf_op jit(solution)/shard_map/ppermute | solution.py:394
  20.1 2.9 %collective-permute-start.1 = (bf16[4,24,128]{2,1,0:T(8,128)(2,1)}, bf16[4,24,128]{2,1,0:T(8,128)(2,1)S(1)}, u32[]{:S(2)}, u32[]{:S(2)}) collective-permute-start(bf16[4,24,128]{2,1,0:T(8,128)(2,1)} %get-tuple-element.17), channel_id=1, source_target_pairs={{8,16},{12,20},{16,8},{20,12},{24,32},{28,36},{32,24},{36,28},{40,... | collective-permute-start | bytes 73736 | tf_op jit(solution)/shard_map/ppermute | solution.py:394
  23.0 2.4 %shard_map.101.table_ref = bf16[4,31,40,128]{3,2,1,0:T(8,128)(2,1)} custom-call(s32[129]{0:T(256)} %old_ref.5, s32[129]{0:T(256)} %new_ref.7, bf16[10,24,128]{2,1,0:T(8,128)(2,1)} %get-tuple-element.14.own_ref, bf16[20,14,512]{2,1,0:T(8,128)(2,1)} %bitcast.9), custom_call_target="tpu_custom_call" | custom-call | flops 1048576 | bytes 4194304 | tf_op jit(solution)/shard_map/pallas_call | solution.py:397
  25.4 0.7 %collective-permute-done.refs_0_ = bf16[4,24,128]{2,1,0:T(8,128)(2,1)S(1)} collective-permute-done((bf16[4,24,128]{2,1,0:T(8,128)(2,1)}, bf16[4,24,128]{2,1,0:T(8,128)(2,1)S(1)}, u32[]{:S(2)}, u32[]{:S(2)}) %collective-permute-start) | collective-permute-done | bytes 24608 | tf_op jit(solution)/shard_map/ppermute | solution.py:394
  26.0 0.0 copy-start.7
  26.0 2.1 %collective-permute-done.1.refs_1_ = bf16[4,24,128]{2,1,0:T(8,128)(2,1)S(1)} collective-permute-done((bf16[4,24,128]{2,1,0:T(8,128)(2,1)}, bf16[4,24,128]{2,1,0:T(8,128)(2,1)S(1)}, u32[]{:S(2)}, u32[]{:S(2)}) %collective-permute-start.1) | collective-permute-done | bytes 24608 | tf_op jit(solution)/shard_map/ppermute | solution.py:394
  28.1 0.0 copy-start.8
  28.1 0.0 collective-permute-done.2.refs_2_
  28.1 0.0 copy-start.6
  28.1 0.0 all-to-all-done.block_ref
  28.1 0.0 copy-done.7
  28.1 0.6 copy-done.8
  28.7 0.0 copy-done.6
  28.8 0.0 copy-start.5
  28.8 0.7 %copy-done.5 = bf16[4,12,24,128]{3,2,1,0:T(8,128)(2,1)} copy-done((bf16[4,12,24,128]{3,2,1,0:T(8,128)(2,1)}, bf16[4,12,24,128]{3,2,1,0:T(8,128)(2,1)S(1)}, u32[]{:S(2)}) %copy-start.5) | copy-done | bytes 294936
  29.5 2.7 %shard_map.102 = (bf16[4,31,40,128]{3,2,1,0:T(8,128)(2,1)}, f32[16,128]{1,0:T(8,128)}) custom-call(s32[129]{0:T(256)} %old_ref.5, s32[129]{0:T(256)} %new_ref.7, s32[12,128]{1,0:T(8,128)} %bitcast.12, bf16[4,31,40,128]{3,2,1,0:T(8,128)(2,1)} %shard_map.101.table_ref, bf16[4,12,24,128]{3,2,1,0:T(8,128)(2,1)} %copy-done.5, ...), custom_call_target="tpu_custom_call", output_to_operand_aliasing={{0}: (3, {})} | custom-call | tf_op jit(solution)/shard_map/pallas_call | solution.py:410
  32.2 0.0 copy-start
  32.2 0.0 copy-start.1
  32.2 0.0 copy-start.2
  32.2 0.0 copy-start.3
  32.3 0.0 copy-start.4
  32.3 20.8 %all_to_all.10.table_ref = bf16[4,31,40,128]{3,2,1,0:T(8,128)(2,1)S(1)} all-to-all(bf16[4,31,40,128]{3,2,1,0:T(8,128)(2,1)} %get-tuple-element.20), channel_id=1, replica_groups=mesh['tile'=128,'mem'=4] {'mem'}, dimensions={0} | all-to-all | bytes 2539520 | tf_op jit(solution)/shard_map/all_to_all | solution.py:427
  53.0 0.0 copy-done
  53.0 0.0 copy-done.1
  53.0 0.0 copy-done.2
  53.0 0.0 copy-done.3
  53.1 0.0 copy-done.4
  53.1 7.8 %shard_map.103 = bf16[20,14,512]{2,1,0:T(8,128)(2,1)} custom-call(s32[7,14]{1,0:T(8,128)S(1)} %bitcast.6, f32[7,14]{1,0:T(8,128)S(1)} %bitcast.7, s32[129]{0:T(256)S(1)} %copy-done, f32[16,128]{1,0:T(8,128)S(1)} %copy-done.1, f32[16,128]{1,0:T(8,128)S(1)} %copy-done.2, bf16[4,31,40,128]{3,2,1,0:T(8,128)(2,1)S(1)} %all_to_all.10.table_ref), custom_call_target="tpu_custom_call" | custom-call | tf_op jit(solution)/shard_map/pallas_call | solution.py:430
Async XLA Ops:
  2.2 25.9 %all-to-all-start = ((bf16[4,12,24,128]{3,2,1,0:T(8,128)(2,1)}), bf16[4,12,24,128]{3,2,1,0:T(8,128)(2,1)S(1)}, u32[]{:S(2)}, u32[]{:S(2)}) async-start(bf16[4,12,24,128]{3,2,1,0:T(8,128)(2,1)} %get-tuple-element.15), calls=%async_computation | async-start | bytes 589824 | tf_op jit(solution)/shard_map/all_to_all | solution.py:389
  5.9 22.3 %collective-permute-start.2 = (bf16[12,24,128]{2,1,0:T(8,128)(2,1)}, bf16[12,24,128]{2,1,0:T(8,128)(2,1)S(1)}, u32[]{:S(2)}, u32[]{:S(2)}) collective-permute-start(bf16[12,24,128]{2,1,0:T(8,128)(2,1)} %get-tuple-element.18), channel_id=1, source_target_pairs={{8,20},{12,16},{16,12},{20,8},{24,36},{28,32},{32,28},{36,24},{40,... | collective-permute-start | bytes 221192 | tf_op jit(solution)/shard_map/ppermute | solution.py:394
  17.7 8.4 %collective-permute-start = (bf16[4,24,128]{2,1,0:T(8,128)(2,1)}, bf16[4,24,128]{2,1,0:T(8,128)(2,1)S(1)}, u32[]{:S(2)}, u32[]{:S(2)}) collective-permute-start(bf16[4,24,128]{2,1,0:T(8,128)(2,1)} %get-tuple-element.16), channel_id=1, source_target_pairs={{4,16},{12,24},{16,4},{20,32},{24,12},{28,40},{32,20},{36,48},{40,... | collective-permute-start | bytes 73736 | tf_op jit(solution)/shard_map/ppermute | solution.py:394
  20.1 8.0 %collective-permute-start.1 = (bf16[4,24,128]{2,1,0:T(8,128)(2,1)}, bf16[4,24,128]{2,1,0:T(8,128)(2,1)S(1)}, u32[]{:S(2)}, u32[]{:S(2)}) collective-permute-start(bf16[4,24,128]{2,1,0:T(8,128)(2,1)} %get-tuple-element.17), channel_id=1, source_target_pairs={{8,16},{12,20},{16,8},{20,12},{24,32},{28,36},{32,24},{36,28},{40,... | collective-permute-start | bytes 73736 | tf_op jit(solution)/shard_map/ppermute | solution.py:394
  26.0 2.1 %copy-start.7 = (bf16[4,24,128]{2,1,0:T(8,128)(2,1)}, bf16[4,24,128]{2,1,0:T(8,128)(2,1)S(1)}, u32[]{:S(2)}) copy-start(bf16[4,24,128]{2,1,0:T(8,128)(2,1)S(1)} %collective-permute-done.refs_0_) | copy-start | bytes 73732
  28.1 0.6 %copy-start.8 = (bf16[4,24,128]{2,1,0:T(8,128)(2,1)}, bf16[4,24,128]{2,1,0:T(8,128)(2,1)S(1)}, u32[]{:S(2)}) copy-start(bf16[4,24,128]{2,1,0:T(8,128)(2,1)S(1)} %collective-permute-done.1.refs_1_) | copy-start | bytes 73732
  28.1 0.6 %copy-start.6 = (bf16[12,24,128]{2,1,0:T(8,128)(2,1)}, bf16[12,24,128]{2,1,0:T(8,128)(2,1)S(1)}, u32[]{:S(2)}) copy-start(bf16[12,24,128]{2,1,0:T(8,128)(2,1)S(1)} %collective-permute-done.2.refs_2_) | copy-start | bytes 221188
  28.8 0.7 %copy-start.5 = (bf16[4,12,24,128]{3,2,1,0:T(8,128)(2,1)}, bf16[4,12,24,128]{3,2,1,0:T(8,128)(2,1)S(1)}, u32[]{:S(2)}) copy-start(bf16[4,12,24,128]{3,2,1,0:T(8,128)(2,1)S(1)} %all-to-all-done.block_ref) | copy-start | bytes 884740
  32.2 20.8 %copy-start = (s32[129]{0:T(256)S(1)}, s32[129]{0:T(256)}, u32[]{:S(2)}) copy-start(s32[129]{0:T(256)} %new_ref.7) | copy-start | bytes 1552
  32.2 20.8 %copy-start.1 = (f32[16,128]{1,0:T(8,128)S(1)}, f32[16,128]{1,0:T(8,128)}, u32[]{:S(2)}) copy-start(f32[16,128]{1,0:T(8,128)} %get-tuple-element.13.own_pulled_ref) | copy-start | bytes 24580
  32.2 20.8 %copy-start.2 = (f32[16,128]{1,0:T(8,128)S(1)}, f32[16,128]{1,0:T(8,128)}, u32[]{:S(2)}) copy-start(f32[16,128]{1,0:T(8,128)} %get-tuple-element.19.halo_pulled_ref) | copy-start | bytes 24580
  32.2 20.8 %copy-start.3 = (s32[14,7]{0,1:T(8,128)S(1)}, s32[14,7]{0,1:T(8,128)}, u32[]{:S(2)}) copy-start(s32[14,7]{0,1:T(8,128)} %param.19) | copy-start | bytes 1180
  32.3 20.8 %copy-start.4 = (f32[14,7]{0,1:T(8,128)S(1)}, f32[14,7]{0,1:T(8,128)}, u32[]{:S(2)}) copy-start(f32[14,7]{0,1:T(8,128)} %param.14) | copy-start | bytes 1180

commit v5 on v4

--- a/solution.py
+++ b/solution.py
@@ -40,7 +40,9 @@
 
 
 def paired(x, y):
-    return jnp.concatenate([x.astype(F32), y.astype(F32)], axis=0).astype(BF16)
+    x, y = x.astype(F32), y.astype(F32)
+    parts = [x[:PITCH], y[:PITCH], x[PITCH:], y[PITCH:]]
+    return jnp.concatenate(parts, axis=0).astype(BF16)
 
 
 def pack_kernel(
@@ -262,12 +264,17 @@
     diagonal = (row == column).astype(F32)
     shift = diagonal * ((side - 1) / INFLATION)
 
+    rest = members - PITCH
+
     def all_members(pair):
         rows = [table_ref[r, pair].astype(F32) for r in range(ranks)]
-        return [
-            jnp.concatenate([x[k * members : (k + 1) * members] for x in rows], axis=0).astype(BF16)
-            for k in range(2)
-        ]
+        blocks = []
+        for k in range(2):
+            parts = [x[k * PITCH : (k + 1) * PITCH] for x in rows]
+            begin = 2 * PITCH + k * rest
+            parts += [x[begin : begin + rest] for x in rows]
+            blocks.append(jnp.concatenate(parts, axis=0).astype(BF16))
+        return blocks
 
     for t in range(0, tiles, 2):
         for k, block in enumerate(all_members(t // 2)):
@@ -312,8 +319,9 @@
                 root = system_ref[i]
                 system_ref[i] = root + dot3(split(root), change[i])
 
-    start = pl.multiple_of(rank * members // 8 * 8, 8)
-    begins_inside = rank * members > start
+    first = pl.multiple_of(rank * PITCH, 8)
+    last = pl.multiple_of(ranks * PITCH + rank // 2 * (2 * rest), 8)
+    odd = lax.rem(rank, 2) == 1
     ones = jnp.ones((1, side), F32)
     inverses = [split(inverse_ref[i]) for i in range(LIVE)]
     half_way = [
@@ -322,8 +330,9 @@
     mean_weights = [dot3(split(half_way[i]), inverses[i])[0:1, :] for i in range(LIVE)]
     for i in range(LIVE):
         mean_weight = mean_weights[i] * (1.0 / frobenius[i])
-        own = inverse_ref[i, pl.ds(start, PADDED), :]
-        own = jnp.where(begins_inside, own[PADDED - members :], own[:members])
+        ends = inverse_ref[i, pl.ds(last, 2 * rest), :]
+        ends = jnp.where(odd, ends[rest:], ends[:rest])
+        own = jnp.concatenate([inverse_ref[i, pl.ds(first, PITCH), :], ends], axis=0)
         transform = (math.sqrt(side - 1) * lax.rsqrt(frobenius[i])) * own + mean_weight
         transform = transform.astype(BF16).astype(F32)
         keep_share = 1.0 - jnp.sum(transform, axis=1, keepdims=True)
@@ -422,7 +431,7 @@
             pltpu.SemaphoreType.DMA((ranks,)),
             pltpu.SemaphoreType.DMA((2 * MOVE, ranks)),
         ],
-        compiler_params=params(56),
+        compiler_params=params(16),
     )(old_split, new_split, halo_tiles, table, block, *arrived)
     table = lax.all_to_all(table, "mem", 0, 0, tiled=True)
 

time: 61.6 us -> 60.2 us (0.977)
  Pallas kernels: 15.1 us -> 14.1 us
    pallas_call x1, Pallas kernels: 2.71 us -> 1.73 us  [shards(): pl.pallas_call(table_kernel, out_shape=(jax.ShapeDtypeStruct(table_shape,...]
    unnamed x18 -> x14, local copies, waits for them, and re-layouts: 1.37 us -> 1.32 us
where the time goes in v5:
time: 60.2 us; the launch traced here: 59.9 us
  blocking collectives  20.8 us (35%)
  starting transfers between devices  20.7 us (34%)
  Pallas kernels  14.1 us (23%)
  waiting for transfers between devices  2.75 us (5%)
  local copies, waits for them, and re-layouts  1.32 us (2%)
    all_to_all x1, blocking collectives, shards(): table = lax.all_to_all(table, 'mem', 0, 0, tiled=True)  20.8 us
    ppermute x3, starting transfers between devices, shards(): arrived.append(lax.ppermute(value, 'tile', pairs))  17.1 us
    pallas_call x1, Pallas kernels, shards(): pl.pallas_call(analysis_kernel, out_shape=jax.ShapeDtypeStruct((members,...  7.77 us
    all_to_all x1, starting transfers between devices, shards(): lax.all_to_all(block, 'tile', 0, 0, axis_index_groups=groups, tiled=True)  3.66 us
    ppermute x3, waiting for transfers between devices, shards(): arrived.append(lax.ppermute(value, 'tile', pairs))  2.74 us
    pallas_call x1, Pallas kernels, shards(): pl.pallas_call(own_table_kernel, out_shape=jax.ShapeDtypeStruct(table_sha...  2.4 us
    pallas_call x1, Pallas kernels, shards(): pl.pallas_call(pack_kernel, out_shape=(tile_blocks(LIVE), jax.ShapeDtypeS...  2.23 us
    pallas_call x1, Pallas kernels, shards(): pl.pallas_call(table_kernel, out_shape=(jax.ShapeDtypeStruct(table_shape,...  1.73 us
  transfers between devices with their start and end apart: 4, of which 2 were waited for; matrix products, arithmetic and copies ran while one was open for 0% of the time, Pallas kernels for 4%

profile of v5, /device:TPU:56, one launch (start us, length us, event | category | flops | bytes accessed | tf_op | source)
XLA Modules:
  0.0 59.9 jit_solution(11198452225623886969)
XLA Ops:
  0.0 0.0 copy-start.1
  0.0 0.0 copy-start.2
  0.0 0.0 copy-start.3
  0.0 2.2 %shard_map.100 = (bf16[10,24,128]{2,1,0:T(8,128)(2,1)}, f32[16,128]{1,0:T(8,128)}, bf16[4,12,24,128]{3,2,1,0:T(8,128)(2,1)}, bf16[4,24,128]{2,1,0:T(8,128)(2,1)}...) custom-call(s32[14]{0:T(128)} %count_ref.1, s32[129]{0:T(256)} %old_ref.5, s32[129]{0:T(256)} %new_ref.7, ...), custom_call_target="tpu_custom_call" | custom-call | tf_op jit(solution)/shard_map/pallas_call | solution.py:378
  2.2 3.7 %all-to-all-start = ((bf16[4,12,24,128]{3,2,1,0:T(8,128)(2,1)}), bf16[4,12,24,128]{3,2,1,0:T(8,128)(2,1)S(1)}, u32[]{:S(2)}, u32[]{:S(2)}) async-start(bf16[4,12,24,128]{3,2,1,0:T(8,128)(2,1)} %get-tuple-element.15), calls=%async_computation | async-start | bytes 589824 | tf_op jit(solution)/shard_map/all_to_all | solution.py:398
  5.9 11.8 %collective-permute-start.2 = (bf16[12,24,128]{2,1,0:T(8,128)(2,1)}, bf16[12,24,128]{2,1,0:T(8,128)(2,1)S(1)}, u32[]{:S(2)}, u32[]{:S(2)}) collective-permute-start(bf16[12,24,128]{2,1,0:T(8,128)(2,1)} %get-tuple-element.18), channel_id=1, source_target_pairs={{8,20},{12,16},{16,12},{20,8},{24,36},{28,32},{32,28},{36,24},{40,... | collective-permute-start | bytes 221192 | tf_op jit(solution)/shard_map/ppermute | solution.py:403
  17.7 2.4 %collective-permute-start = (bf16[4,24,128]{2,1,0:T(8,128)(2,1)}, bf16[4,24,128]{2,1,0:T(8,128)(2,1)S(1)}, u32[]{:S(2)}, u32[]{:S(2)}) collective-permute-start(bf16[4,24,128]{2,1,0:T(8,128)(2,1)} %get-tuple-element.16), channel_id=1, source_target_pairs={{4,16},{12,24},{16,4},{20,32},{24,12},{28,40},{32,20},{36,48},{40,... | collective-permute-start | bytes 73736 | tf_op jit(solution)/shard_map/ppermute | solution.py:403
  20.1 2.9 %collective-permute-start.1 = (bf16[4,24,128]{2,1,0:T(8,128)(2,1)}, bf16[4,24,128]{2,1,0:T(8,128)(2,1)S(1)}, u32[]{:S(2)}, u32[]{:S(2)}) collective-permute-start(bf16[4,24,128]{2,1,0:T(8,128)(2,1)} %get-tuple-element.17), channel_id=1, source_target_pairs={{8,16},{12,20},{16,8},{20,12},{24,32},{28,36},{32,24},{36,28},{40,... | collective-permute-start | bytes 73736 | tf_op jit(solution)/shard_map/ppermute | solution.py:403
  23.0 2.4 %shard_map.101.table_ref = bf16[4,31,40,128]{3,2,1,0:T(8,128)(2,1)} custom-call(s32[129]{0:T(256)} %old_ref.5, s32[129]{0:T(256)} %new_ref.7, bf16[10,24,128]{2,1,0:T(8,128)(2,1)} %get-tuple-element.14.own_ref, bf16[20,14,512]{2,1,0:T(8,128)(2,1)} %bitcast.11), custom_call_target="tpu_custom_call" | custom-call | flops 1048576 | bytes 4194304 | tf_op jit(solution)/shard_map/pallas_call | solution.py:406
  25.4 0.6 %collective-permute-done.refs_0_ = bf16[4,24,128]{2,1,0:T(8,128)(2,1)S(1)} collective-permute-done((bf16[4,24,128]{2,1,0:T(8,128)(2,1)}, bf16[4,24,128]{2,1,0:T(8,128)(2,1)S(1)}, u32[]{:S(2)}, u32[]{:S(2)}) %collective-permute-start) | collective-permute-done | bytes 24608 | tf_op jit(solution)/shard_map/ppermute | solution.py:403
  26.1 2.1 %collective-permute-done.1.refs_1_ = bf16[4,24,128]{2,1,0:T(8,128)(2,1)S(1)} collective-permute-done((bf16[4,24,128]{2,1,0:T(8,128)(2,1)}, bf16[4,24,128]{2,1,0:T(8,128)(2,1)S(1)}, u32[]{:S(2)}, u32[]{:S(2)}) %collective-permute-start.1) | collective-permute-done | bytes 24608 | tf_op jit(solution)/shard_map/ppermute | solution.py:403
  28.2 0.0 collective-permute-done.2.refs_2_
  28.2 0.0 all-to-all-done.block_ref
  28.2 0.0 copy-done.1
  28.2 0.0 copy-done.2
  28.2 0.0 copy-done.3
  28.2 0.0 copy-start
  28.2 1.3 %copy-done = bf16[4,31,40,128]{3,2,1,0:T(8,128)(2,1)S(1)} copy-done((bf16[4,31,40,128]{3,2,1,0:T(8,128)(2,1)S(1)}, bf16[4,31,40,128]{3,2,1,0:T(8,128)(2,1)}, u32[]{:S(2)}) %copy-start) | copy-done | bytes 1269784
  29.5 1.7 %shard_map.102 = (bf16[4,31,40,128]{3,2,1,0:T(8,128)(2,1)S(1)}, f32[16,128]{1,0:T(8,128)S(1)}) custom-call(s32[129]{0:T(256)S(1)} %copy-done.3, s32[129]{0:T(256)S(1)} %copy-done.2, s32[12,128]{1,0:T(8,128)S(1)} %bitcast.7, bf16[4,31,40,128]{3,2,1,0:T(8,128)(2,1)S(1)} %copy-done, ...), custom_call_target="tpu_custom_call", output_to_operand_aliasing={{0}: (3, {})} | custom-call | tf_op jit(solution)/shard_map/pallas_call | solution.py:419
  31.2 0.0 copy-start.4
  31.2 0.0 copy-start.5
  31.3 0.0 copy-start.6
  31.3 20.8 %all_to_all.10.table_ref = bf16[4,31,40,128]{3,2,1,0:T(8,128)(2,1)S(1)} all-to-all(bf16[4,31,40,128]{3,2,1,0:T(8,128)(2,1)S(1)} %get-tuple-element.20), channel_id=1, replica_groups=mesh['tile'=128,'mem'=4] {'mem'}, dimensions={0} | all-to-all | bytes 2539520 | tf_op jit(solution)/shard_map/all_to_all | solution.py:436
  52.1 0.0 copy-done.4
  52.1 0.0 copy-done.5
  52.1 0.0 copy-done.6
  52.1 7.8 %shard_map.103 = bf16[20,14,512]{2,1,0:T(8,128)(2,1)} custom-call(s32[7,14]{1,0:T(8,128)S(1)} %bitcast.8, f32[7,14]{1,0:T(8,128)S(1)} %bitcast.9, s32[129]{0:T(256)S(1)} %copy-done.2, f32[16,128]{1,0:T(8,128)S(1)} %copy-done.4, f32[16,128]{1,0:T(8,128)S(1)} %get-tuple-element.19.halo_pulled_ref, bf16[4,31,40,128]{3,2,1,0:T(8,128)(2,1)S(1)} %all_to_all.10.table_ref), custom_call_target="tpu_custom_call" | custom-call | tf_op jit(solution)/shard_map/pallas_call | solution.py:439
Async XLA Ops:
  0.0 28.2 %copy-start.1 = (s32[128,12]{0,1:T(8,128)S(1)}, s32[128,12]{0,1:T(8,128)}, u32[]{:S(2)}) copy-start(s32[128,12]{0,1:T(8,128)} %param.18) | copy-start | bytes 18436
  0.0 28.2 %copy-start.2 = (s32[129]{0:T(256)S(1)}, s32[129]{0:T(256)}, u32[]{:S(2)}) copy-start(s32[129]{0:T(256)} %new_ref.7) | copy-start | bytes 1552
  0.0 28.2 %copy-start.3 = (s32[129]{0:T(256)S(1)}, s32[129]{0:T(256)}, u32[]{:S(2)}) copy-start(s32[129]{0:T(256)} %old_ref.5) | copy-start | bytes 1552
  2.2 25.9 %all-to-all-start = ((bf16[4,12,24,128]{3,2,1,0:T(8,128)(2,1)}), bf16[4,12,24,128]{3,2,1,0:T(8,128)(2,1)S(1)}, u32[]{:S(2)}, u32[]{:S(2)}) async-start(bf16[4,12,24,128]{3,2,1,0:T(8,128)(2,1)} %get-tuple-element.15), calls=%async_computation | async-start | bytes 589824 | tf_op jit(solution)/shard_map/all_to_all | solution.py:398
  5.9 22.3 %collective-permute-start.2 = (bf16[12,24,128]{2,1,0:T(8,128)(2,1)}, bf16[12,24,128]{2,1,0:T(8,128)(2,1)S(1)}, u32[]{:S(2)}, u32[]{:S(2)}) collective-permute-start(bf16[12,24,128]{2,1,0:T(8,128)(2,1)} %get-tuple-element.18), channel_id=1, source_target_pairs={{8,20},{12,16},{16,12},{20,8},{24,36},{28,32},{32,28},{36,24},{40,... | collective-permute-start | bytes 221192 | tf_op jit(solution)/shard_map/ppermute | solution.py:403
  17.7 8.4 %collective-permute-start = (bf16[4,24,128]{2,1,0:T(8,128)(2,1)}, bf16[4,24,128]{2,1,0:T(8,128)(2,1)S(1)}, u32[]{:S(2)}, u32[]{:S(2)}) collective-permute-start(bf16[4,24,128]{2,1,0:T(8,128)(2,1)} %get-tuple-element.16), channel_id=1, source_target_pairs={{4,16},{12,24},{16,4},{20,32},{24,12},{28,40},{32,20},{36,48},{40,... | collective-permute-start | bytes 73736 | tf_op jit(solution)/shard_map/ppermute | solution.py:403
  20.1 8.0 %collective-permute-start.1 = (bf16[4,24,128]{2,1,0:T(8,128)(2,1)}, bf16[4,24,128]{2,1,0:T(8,128)(2,1)S(1)}, u32[]{:S(2)}, u32[]{:S(2)}) collective-permute-start(bf16[4,24,128]{2,1,0:T(8,128)(2,1)} %get-tuple-element.17), channel_id=1, source_target_pairs={{8,16},{12,20},{16,8},{20,12},{24,32},{28,36},{32,24},{36,28},{40,... | collective-permute-start | bytes 73736 | tf_op jit(solution)/shard_map/ppermute | solution.py:403
  28.2 1.3 %copy-start = (bf16[4,31,40,128]{3,2,1,0:T(8,128)(2,1)S(1)}, bf16[4,31,40,128]{3,2,1,0:T(8,128)(2,1)}, u32[]{:S(2)}) copy-start(bf16[4,31,40,128]{3,2,1,0:T(8,128)(2,1)} %shard_map.101.table_ref) | copy-start | bytes 3809284
  31.2 20.8 %copy-start.4 = (f32[16,128]{1,0:T(8,128)S(1)}, f32[16,128]{1,0:T(8,128)}, u32[]{:S(2)}) copy-start(f32[16,128]{1,0:T(8,128)} %get-tuple-element.13.own_pulled_ref) | copy-start | bytes 24580
  31.2 20.8 %copy-start.5 = (s32[14,7]{0,1:T(8,128)S(1)}, s32[14,7]{0,1:T(8,128)}, u32[]{:S(2)}) copy-start(s32[14,7]{0,1:T(8,128)} %param.19) | copy-start | bytes 1180
  31.3 20.8 %copy-start.6 = (f32[14,7]{0,1:T(8,128)S(1)}, f32[14,7]{0,1:T(8,128)}, u32[]{:S(2)}) copy-start(f32[14,7]{0,1:T(8,128)} %param.14) | copy-start | bytes 1180

commit v6 on v5

--- a/solution.py
+++ b/solution.py
@@ -112,7 +112,7 @@
 
 
 def own_table_kernel(
-    old_ref, new_ref, own_ref, background_ref, out_ref, table_ref, state_rows, sems
+    old_ref, new_ref, own_ref, background_ref, table_ref, state_rows
 ):
     me = lax.axis_index("tile")
     old_start, old_end, new_start = old_ref[me], old_ref[me + 1], new_ref[me]
@@ -130,18 +130,12 @@
         rows = [state_rows[c, pl.ds(at, members, stride=PITCH), :] for c in range(pieces)]
         for c in range(0, pieces, 2):
             table_ref[(LIVE + HPEER * HCAP + i * pieces + c) // 2] = paired(rows[c], rows[c + 1])
-    copies = [
-        pltpu.make_async_copy(table_ref, out_ref.at[r], sems.at[r])
-        for r in range(out_ref.shape[0])
-    ]
-    for copy in copies:
-        copy.start()
-    for copy in copies:
-        copy.wait()
-
-
-def table_kernel(old_ref, new_ref, halo_ref, table_ref, block_ref, *refs):
-    swap_refs, (out_ref, pulled_ref, halo_rows, moved_rows, halo_sems, moved_sems) = refs[:-6], refs[-6:]
+
+
+def table_kernel(old_ref, new_ref, halo_ref, stays_ref, block_ref, *refs):
+    swap_refs, (out_ref, pulled_ref, table_ref, fetch_sem, sems) = refs[:-5], refs[-5:]
+    fetch = pltpu.make_async_copy(stays_ref, table_ref, fetch_sem)
+    fetch.start()
     devices = new_ref.shape[0] - 1
     me = lax.axis_index("tile")
     place = lax.rem(me, BLOCK)
@@ -152,6 +146,7 @@
     members = pair_rows // 2
     pieces = (block_ref.shape[1] - HCAP) // MOVE
     pulled_ref[...] = jnp.zeros(pulled_ref.shape, F32)
+    fetch.wait()
 
     moves = []
     for j in range(MOVE):
@@ -162,22 +157,14 @@
         tile = old_end + j
         slot = jnp.clip(tile - new_start, 0, LIVE - 1)
         moves.append((tile < new_end, slot, j, place < BLOCK - 1, place + 1))
-    copies = []
-    for n, (comes, slot, index, inside, source) in enumerate(moves):
+    for comes, slot, index, inside, source in moves:
         begin = HCAP + index * pieces
         source = jnp.clip(source, 0, BLOCK - 1)
         at = (LIVE + HPEER * HCAP + slot * pieces) // 2
-        mine = [
-            pltpu.make_async_copy(
-                moved_rows.at[n], out_ref.at[r, pl.ds(at, pieces // 2)], moved_sems.at[n, r]
-            )
-            for r in range(ranks)
-        ]
-        copies.append((comes, mine))
-
-        def put(read, n=n):
+
+        def put(read, at=at):
             for c in range(0, pieces, 2):
-                moved_rows[n, c // 2] = paired(read(c)[:members], read(c + 1)[:members])
+                table_ref[at + c // 2] = paired(read(c)[:members], read(c + 1)[:members])
 
         @pl.when(comes & inside)
         def _():
@@ -186,11 +173,6 @@
         @pl.when(comes & jnp.logical_not(inside))
         def _():
             put(lambda c: swap_refs[-1][begin + c])
-
-        @pl.when(comes)
-        def _():
-            for copy in mine:
-                copy.start()
 
     for g in range(HPEER):
         first = halo_ref[g * HCAP, me]
@@ -204,7 +186,7 @@
                 at = g * HCAP + k
                 pulled_ref[at : at + 1, :] = read(k).astype(F32)[members : members + 1]
             for k in range(0, HCAP, 2):
-                halo_rows[(g * HCAP + k) // 2] = paired(read(k)[:members], read(k + 1)[:members])
+                table_ref[(LIVE + g * HCAP + k) // 2] = paired(read(k)[:members], read(k + 1)[:members])
 
         @pl.when((peer >= base) & (peer < base + BLOCK))
         def _():
@@ -216,20 +198,12 @@
             def _():
                 put(lambda k: swap_ref[k])
 
-    halo = [
-        pltpu.make_async_copy(
-            halo_rows, out_ref.at[r, pl.ds(LIVE // 2, HPEER * HCAP // 2)], halo_sems.at[r]
-        )
-        for r in range(ranks)
+    copies = [
+        pltpu.make_async_copy(table_ref, out_ref.at[r], sems.at[r]) for r in range(ranks)
     ]
-    for copy in halo:
+    for copy in copies:
         copy.start()
-    for comes, mine in copies:
-        @pl.when(comes)
-        def _():
-            for copy in mine:
-                copy.wait()
-    for copy in halo:
+    for copy in copies:
         copy.wait()
 
 
@@ -256,23 +230,32 @@
     members, capacity, width = out_ref.shape
     obs_slots = table_ref.shape[3]
     pieces = width // obs_slots
-    side = ranks * members
+    ensemble = ranks * members
+    side = ensemble + PITCH
     live_count = new_ref[me + 1] - new_ref[me]
 
     row = lax.broadcasted_iota(jnp.int32, (side, side), 0)
     column = lax.broadcasted_iota(jnp.int32, (side, side), 1)
     diagonal = (row == column).astype(F32)
-    shift = diagonal * ((side - 1) / INFLATION)
+    real = (row < ensemble) & (column < ensemble)
+    shift = jnp.where(real, diagonal * ((ensemble - 1) / INFLATION), 0.0)
+    real_lane = lax.broadcasted_iota(jnp.int32, (1, side), 1) < ensemble
 
     rest = members - PITCH
+
+    upper = lax.broadcasted_iota(jnp.int32, (2 * rest, obs_slots), 0) < rest
 
     def all_members(pair):
         rows = [table_ref[r, pair].astype(F32) for r in range(ranks)]
+        ends = [x[2 * PITCH :] for x in rows]
+        turned = [pltpu.roll(x, rest, 0) for x in ends]
         blocks = []
         for k in range(2):
             parts = [x[k * PITCH : (k + 1) * PITCH] for x in rows]
-            begin = 2 * PITCH + k * rest
-            parts += [x[begin : begin + rest] for x in rows]
+            for r in range(0, ranks, 2):
+                above = turned[r] if k else ends[r]
+                below = ends[r + 1] if k else turned[r + 1]
+                parts.append(jnp.where(upper, above, below))
             blocks.append(jnp.concatenate(parts, axis=0).astype(BF16))
         return blocks
 
@@ -281,11 +264,10 @@
             at = t + k
             pulled_ref, where = (own_pulled_ref, at) if at < LIVE else (halo_pulled_ref, at - LIVE)
             pulled = padded_to(pulled_ref[where : where + 1, :], PITCH).astype(BF16)
-            product = lax.dot_general(
-                jnp.concatenate([block, pulled], axis=0), block,
-                (((1,), (1,)), ((), ())), preferred_element_type=F32,
+            block = jnp.concatenate([block, pulled], axis=0)
+            gram_ref[at] = lax.dot_general(
+                block, block, (((1,), (1,)), ((), ())), preferred_element_type=F32
             )
-            gram_ref[at] = product[: side + 8]
 
     frobenius, pull, change = [], [], []
     for i in range(LIVE):
@@ -294,8 +276,8 @@
             r = region_ref[e, i]
             at = jnp.where(r < capacity, jnp.minimum(r, LIVE - 1), r - capacity + LIVE)
             total = total + weight_ref[e, i] * gram_ref[at]
-        pull.append(total[side : side + 1, :])
-        system = total[:side] + shift
+        pull.append(jnp.where(real_lane, total[ensemble : ensemble + 1, :], 0.0))
+        system = jnp.where(real, total, 0.0) + shift
         squared = jnp.sum(jnp.sum(system * system, axis=0, keepdims=True), axis=1, keepdims=True)
         norm = jnp.sqrt(squared)
         frobenius.append(norm)
@@ -322,7 +304,7 @@
     first = pl.multiple_of(rank * PITCH, 8)
     last = pl.multiple_of(ranks * PITCH + rank // 2 * (2 * rest), 8)
     odd = lax.rem(rank, 2) == 1
-    ones = jnp.ones((1, side), F32)
+    ones = jnp.ones((1, ensemble), F32)
     inverses = [split(inverse_ref[i]) for i in range(LIVE)]
     half_way = [
         dot3(split(jnp.broadcast_to(pull[i], (8, side))), inverses[i]) for i in range(LIVE)
@@ -333,14 +315,15 @@
         ends = inverse_ref[i, pl.ds(last, 2 * rest), :]
         ends = jnp.where(odd, ends[rest:], ends[:rest])
         own = jnp.concatenate([inverse_ref[i, pl.ds(first, PITCH), :], ends], axis=0)
-        transform = (math.sqrt(side - 1) * lax.rsqrt(frobenius[i])) * own + mean_weight
+        transform = (math.sqrt(ensemble - 1) * lax.rsqrt(frobenius[i])) * own + mean_weight
+        transform = transform[:, :ensemble]
         transform = transform.astype(BF16).astype(F32)
         keep_share = 1.0 - jnp.sum(transform, axis=1, keepdims=True)
         weights = padded_to(jnp.concatenate([transform, ones], axis=0), 2 * PITCH).astype(BF16)
         state = [x for c in range(0, pieces, 2) for x in all_members((tiles + i * pieces + c) // 2)]
         for c in range(pieces):
             blended = dot(weights, state[c])
-            mean_state = blended[members : members + 1, :] / side
+            mean_state = blended[members : members + 1, :] / ensemble
             analysis = blended[:members] + keep_share * mean_state
             rows_ref[c, pl.ds(i, members, stride=PITCH), :] = jnp.where(i < live_count, analysis, 0.0)
     for i in range(LIVE, capacity):
@@ -402,47 +385,41 @@
         pairs = [(d, e) for d, e in pairs if 0 <= e < devices]
         arrived.append(lax.ppermute(value, "tile", pairs))
 
-    table_shape = (ranks, (tiles + LIVE * pieces) // 2, 2 * members, obs_slots)
-    table = pl.pallas_call(
+    table_shape = ((tiles + LIVE * pieces) // 2, 2 * members, obs_slots)
+    stays = pl.pallas_call(
         own_table_kernel,
         out_shape=jax.ShapeDtypeStruct(table_shape, BF16),
         in_specs=[smem] * 2 + [vmem] * 2,
-        out_specs=pl.BlockSpec(memory_space=pl.ANY),
-        scratch_shapes=[
-            VMEM(table_shape[1:], BF16),
-            VMEM((pieces, members * PITCH, obs_slots), F32),
-            pltpu.SemaphoreType.DMA((ranks,)),
-        ],
+        out_specs=vmem,
+        scratch_shapes=[VMEM((pieces, members * PITCH, obs_slots), F32)],
         compiler_params=params(56),
         cost_estimate=COST,
     )(old_split, new_split, own, background)
     table, halo_pulled = pl.pallas_call(
         table_kernel,
         out_shape=(
-            jax.ShapeDtypeStruct(table_shape, BF16),
+            jax.ShapeDtypeStruct((ranks, *table_shape), BF16),
             jax.ShapeDtypeStruct((PITCH, obs_slots), F32),
         ),
         in_specs=[smem] * 3 + [pl.BlockSpec(memory_space=pl.ANY)] + [vmem] * 4,
         out_specs=(pl.BlockSpec(memory_space=pl.ANY), vmem),
-        input_output_aliases={3: 0},
         scratch_shapes=[
-            VMEM((HPEER * HCAP // 2, 2 * members, obs_slots), BF16),
-            VMEM((2 * MOVE, pieces // 2, 2 * members, obs_slots), BF16),
+            VMEM(table_shape, BF16),
+            pltpu.SemaphoreType.DMA,
             pltpu.SemaphoreType.DMA((ranks,)),
-            pltpu.SemaphoreType.DMA((2 * MOVE, ranks)),
         ],
         compiler_params=params(16),
-    )(old_split, new_split, halo_tiles, table, block, *arrived)
+    )(old_split, new_split, halo_tiles, stays, block, *arrived)
     table = lax.all_to_all(table, "mem", 0, 0, tiled=True)
 
-    side = ranks * members
+    side = ranks * members + PITCH
     analysis = pl.pallas_call(
         analysis_kernel,
         out_shape=jax.ShapeDtypeStruct((members, capacity, width), BF16),
         in_specs=[smem] * 3 + [vmem] * 3,
         out_specs=vmem,
         scratch_shapes=[
-            VMEM((tiles, side + 8, side), F32),
+            VMEM((tiles, side, side), F32),
             VMEM((LIVE, side, side), F32),
             VMEM((LIVE, side, side), F32),
             VMEM((pieces, members * PITCH, obs_slots), F32),

time: 60.2 us -> 58 us (0.963)
  Pallas kernels: 14.1 us -> 11.8 us
    pallas_call x1, Pallas kernels: 7.77 us -> 6.08 us  [shards(): pl.pallas_call(analysis_kernel, out_shape=jax.ShapeDtypeStruct((members,...]
where the time goes in v6:
time: 58 us; the launch traced here: 57.4 us
  starting transfers between devices  20.7 us (36%)
  blocking collectives  20.6 us (36%)
  Pallas kernels  11.8 us (20%)
  waiting for transfers between devices  3.15 us (5%)
  local copies, waits for them, and re-layouts  0.99 us (2%)
    all_to_all x1, blocking collectives, shards(): table = lax.all_to_all(table, 'mem', 0, 0, tiled=True)  20.6 us
    ppermute x3, starting transfers between devices, shards(): arrived.append(lax.ppermute(value, 'tile', pairs))  17.1 us
    pallas_call x1, Pallas kernels, shards(): pl.pallas_call(analysis_kernel, out_shape=jax.ShapeDtypeStruct((members,...  6.08 us
    all_to_all x1, starting transfers between devices, shards(): lax.all_to_all(block, 'tile', 0, 0, axis_index_groups=groups, tiled=True)  3.66 us
    ppermute x3, waiting for transfers between devices, shards(): arrived.append(lax.ppermute(value, 'tile', pairs))  3.15 us
    pallas_call x1, Pallas kernels, shards(): pl.pallas_call(pack_kernel, out_shape=(tile_blocks(LIVE), jax.ShapeDtypeS...  2.25 us
    pallas_call x1, Pallas kernels, shards(): pl.pallas_call(own_table_kernel, out_shape=jax.ShapeDtypeStruct(table_sha...  2.01 us
    pallas_call x1, Pallas kernels, shards(): pl.pallas_call(table_kernel, out_shape=(jax.ShapeDtypeStruct((ranks, *tab...  1.48 us
  transfers between devices with their start and end apart: 4, of which 2 were waited for; matrix products, arithmetic and copies ran while one was open for 0% of the time, Pallas kernels for 4%

profile of v6, /device:TPU:56, one launch (start us, length us, event | category | flops | bytes accessed | tf_op | source)
XLA Modules:
  0.0 57.4 jit_solution(13183884847666498697)
XLA Ops:
  0.0 0.0 copy-start.2
  0.0 0.0 copy-start.3
  0.0 0.0 copy-start.1
  0.0 2.2 %shard_map.100 = (bf16[10,24,128]{2,1,0:T(8,128)(2,1)}, f32[16,128]{1,0:T(8,128)}, bf16[4,12,24,128]{3,2,1,0:T(8,128)(2,1)}, bf16[4,24,128]{2,1,0:T(8,128)(2,1)}...) custom-call(s32[14]{0:T(128)} %count_ref.1, s32[129]{0:T(256)} %old_ref.5, s32[129]{0:T(256)} %new_ref.7, ...), custom_call_target="tpu_custom_call" | custom-call | tf_op jit(solution)/shard_map/pallas_call | solution.py:361
  2.3 3.7 %all-to-all-start = ((bf16[4,12,24,128]{3,2,1,0:T(8,128)(2,1)}), bf16[4,12,24,128]{3,2,1,0:T(8,128)(2,1)S(1)}, u32[]{:S(2)}, u32[]{:S(2)}) async-start(bf16[4,12,24,128]{3,2,1,0:T(8,128)(2,1)} %get-tuple-element.15), calls=%async_computation | async-start | bytes 589824 | tf_op jit(solution)/shard_map/all_to_all | solution.py:381
  5.9 11.8 %collective-permute-start.2 = (bf16[12,24,128]{2,1,0:T(8,128)(2,1)}, bf16[12,24,128]{2,1,0:T(8,128)(2,1)S(1)}, u32[]{:S(2)}, u32[]{:S(2)}) collective-permute-start(bf16[12,24,128]{2,1,0:T(8,128)(2,1)} %get-tuple-element.18), channel_id=1, source_target_pairs={{8,20},{12,16},{16,12},{20,8},{24,36},{28,32},{32,28},{36,24},{40,... | collective-permute-start | bytes 221192 | tf_op jit(solution)/shard_map/ppermute | solution.py:386
  17.7 2.4 %collective-permute-start = (bf16[4,24,128]{2,1,0:T(8,128)(2,1)}, bf16[4,24,128]{2,1,0:T(8,128)(2,1)S(1)}, u32[]{:S(2)}, u32[]{:S(2)}) collective-permute-start(bf16[4,24,128]{2,1,0:T(8,128)(2,1)} %get-tuple-element.16), channel_id=1, source_target_pairs={{4,16},{12,24},{16,4},{20,32},{24,12},{28,40},{32,20},{36,48},{40,... | collective-permute-start | bytes 73736 | tf_op jit(solution)/shard_map/ppermute | solution.py:386
  20.1 2.9 %collective-permute-start.1 = (bf16[4,24,128]{2,1,0:T(8,128)(2,1)}, bf16[4,24,128]{2,1,0:T(8,128)(2,1)S(1)}, u32[]{:S(2)}, u32[]{:S(2)}) collective-permute-start(bf16[4,24,128]{2,1,0:T(8,128)(2,1)} %get-tuple-element.17), channel_id=1, source_target_pairs={{8,16},{12,20},{16,8},{20,12},{24,32},{28,36},{32,24},{36,28},{40,... | collective-permute-start | bytes 73736 | tf_op jit(solution)/shard_map/ppermute | solution.py:386
  23.0 2.0 %shard_map.101.stays_ref = bf16[31,40,128]{2,1,0:T(8,128)(2,1)} custom-call(s32[129]{0:T(256)} %old_ref.5, s32[129]{0:T(256)} %new_ref.7, bf16[10,24,128]{2,1,0:T(8,128)(2,1)} %get-tuple-element.14.own_ref, bf16[20,14,512]{2,1,0:T(8,128)(2,1)} %bitcast.11), custom_call_target="tpu_custom_call" | custom-call | flops 1048576 | bytes 4194304 | tf_op jit(solution)/shard_map/pallas_call | solution.py:389
  25.0 1.0 %collective-permute-done.refs_0_ = bf16[4,24,128]{2,1,0:T(8,128)(2,1)S(1)} collective-permute-done((bf16[4,24,128]{2,1,0:T(8,128)(2,1)}, bf16[4,24,128]{2,1,0:T(8,128)(2,1)S(1)}, u32[]{:S(2)}, u32[]{:S(2)}) %collective-permute-start) | collective-permute-done | bytes 24608 | tf_op jit(solution)/shard_map/ppermute | solution.py:386
  26.1 2.1 %collective-permute-done.1.refs_1_ = bf16[4,24,128]{2,1,0:T(8,128)(2,1)S(1)} collective-permute-done((bf16[4,24,128]{2,1,0:T(8,128)(2,1)}, bf16[4,24,128]{2,1,0:T(8,128)(2,1)S(1)}, u32[]{:S(2)}, u32[]{:S(2)}) %collective-permute-start.1) | collective-permute-done | bytes 24608 | tf_op jit(solution)/shard_map/ppermute | solution.py:386
  28.2 0.0 collective-permute-done.2.refs_2_
  28.2 0.0 all-to-all-done.block_ref
  28.2 0.0 copy-done.2
  28.2 0.0 copy-done.3
  28.2 0.0 copy-done.1
  28.2 0.0 copy-start
  28.2 1.0 %copy-done = bf16[31,40,128]{2,1,0:T(8,128)(2,1)S(1)} copy-done((bf16[31,40,128]{2,1,0:T(8,128)(2,1)S(1)}, bf16[31,40,128]{2,1,0:T(8,128)(2,1)}, u32[]{:S(2)}) %copy-start) | copy-done | bytes 317464
  29.2 1.5 %shard_map.102 = (bf16[4,31,40,128]{3,2,1,0:T(8,128)(2,1)S(1)}, f32[16,128]{1,0:T(8,128)S(1)}) custom-call(s32[129]{0:T(256)S(1)} %copy-done.3, s32[129]{0:T(256)S(1)} %copy-done.2, s32[12,128]{1,0:T(8,128)S(1)} %bitcast.7, bf16[31,40,128]{2,1,0:T(8,128)(2,1)S(1)} %copy-done, bf16[4,12,24,128]{3,2,1,0:T(8,128)(2,1)S(1)} %all-to-all-done.block_ref, ...), custom_call_target="tpu_custom_call" | custom-call | tf_op jit(solution)/shard_map/pallas_call | solution.py:398
  30.7 0.0 copy-start.4
  30.7 0.0 copy-start.5
  30.7 0.0 copy-start.6
  30.7 20.6 %all_to_all.10.table_ref = bf16[4,31,40,128]{3,2,1,0:T(8,128)(2,1)S(1)} all-to-all(bf16[4,31,40,128]{3,2,1,0:T(8,128)(2,1)S(1)} %get-tuple-element.20), channel_id=1, replica_groups=mesh['tile'=128,'mem'=4] {'mem'}, dimensions={0} | all-to-all | bytes 2539520 | tf_op jit(solution)/shard_map/all_to_all | solution.py:413
  51.3 0.0 copy-done.4
  51.3 0.0 copy-done.5
  51.3 0.0 copy-done.6
  51.3 6.1 %shard_map.103 = bf16[20,14,512]{2,1,0:T(8,128)(2,1)} custom-call(s32[7,14]{1,0:T(8,128)S(1)} %bitcast.8, f32[7,14]{1,0:T(8,128)S(1)} %bitcast.9, s32[129]{0:T(256)S(1)} %copy-done.2, f32[16,128]{1,0:T(8,128)S(1)} %copy-done.4, f32[16,128]{1,0:T(8,128)S(1)} %get-tuple-element.19.halo_pulled_ref, bf16[4,31,40,128]{3,2,1,0:T(8,128)(2,1)S(1)} %all_to_all.10.table_ref), custom_call_target="tpu_custom_call" | custom-call | tf_op jit(solution)/shard_map/pallas_call | solution.py:416
Async XLA Ops:
  0.0 28.2 %copy-start.2 = (s32[129]{0:T(256)S(1)}, s32[129]{0:T(256)}, u32[]{:S(2)}) copy-start(s32[129]{0:T(256)} %new_ref.7) | copy-start | bytes 1552
  0.0 28.2 %copy-start.3 = (s32[129]{0:T(256)S(1)}, s32[129]{0:T(256)}, u32[]{:S(2)}) copy-start(s32[129]{0:T(256)} %old_ref.5) | copy-start | bytes 1552
  0.0 28.2 %copy-start.1 = (s32[128,12]{0,1:T(8,128)S(1)}, s32[128,12]{0,1:T(8,128)}, u32[]{:S(2)}) copy-start(s32[128,12]{0,1:T(8,128)} %param.18) | copy-start | bytes 18436
  2.3 25.9 %all-to-all-start = ((bf16[4,12,24,128]{3,2,1,0:T(8,128)(2,1)}), bf16[4,12,24,128]{3,2,1,0:T(8,128)(2,1)S(1)}, u32[]{:S(2)}, u32[]{:S(2)}) async-start(bf16[4,12,24,128]{3,2,1,0:T(8,128)(2,1)} %get-tuple-element.15), calls=%async_computation | async-start | bytes 589824 | tf_op jit(solution)/shard_map/all_to_all | solution.py:381
  5.9 22.3 %collective-permute-start.2 = (bf16[12,24,128]{2,1,0:T(8,128)(2,1)}, bf16[12,24,128]{2,1,0:T(8,128)(2,1)S(1)}, u32[]{:S(2)}, u32[]{:S(2)}) collective-permute-start(bf16[12,24,128]{2,1,0:T(8,128)(2,1)} %get-tuple-element.18), channel_id=1, source_target_pairs={{8,20},{12,16},{16,12},{20,8},{24,36},{28,32},{32,28},{36,24},{40,... | collective-permute-start | bytes 221192 | tf_op jit(solution)/shard_map/ppermute | solution.py:386
  17.7 8.4 %collective-permute-start = (bf16[4,24,128]{2,1,0:T(8,128)(2,1)}, bf16[4,24,128]{2,1,0:T(8,128)(2,1)S(1)}, u32[]{:S(2)}, u32[]{:S(2)}) collective-permute-start(bf16[4,24,128]{2,1,0:T(8,128)(2,1)} %get-tuple-element.16), channel_id=1, source_target_pairs={{4,16},{12,24},{16,4},{20,32},{24,12},{28,40},{32,20},{36,48},{40,... | collective-permute-start | bytes 73736 | tf_op jit(solution)/shard_map/ppermute | solution.py:386
  20.1 8.0 %collective-permute-start.1 = (bf16[4,24,128]{2,1,0:T(8,128)(2,1)}, bf16[4,24,128]{2,1,0:T(8,128)(2,1)S(1)}, u32[]{:S(2)}, u32[]{:S(2)}) collective-permute-start(bf16[4,24,128]{2,1,0:T(8,128)(2,1)} %get-tuple-element.17), channel_id=1, source_target_pairs={{8,16},{12,20},{16,8},{20,12},{24,32},{28,36},{32,24},{36,28},{40,... | collective-permute-start | bytes 73736 | tf_op jit(solution)/shard_map/ppermute | solution.py:386
  28.2 1.0 %copy-start = (bf16[31,40,128]{2,1,0:T(8,128)(2,1)S(1)}, bf16[31,40,128]{2,1,0:T(8,128)(2,1)}, u32[]{:S(2)}) copy-start(bf16[31,40,128]{2,1,0:T(8,128)(2,1)} %shard_map.101.stays_ref) | copy-start | bytes 952324
  30.7 20.6 %copy-start.4 = (f32[16,128]{1,0:T(8,128)S(1)}, f32[16,128]{1,0:T(8,128)}, u32[]{:S(2)}) copy-start(f32[16,128]{1,0:T(8,128)} %get-tuple-element.13.own_pulled_ref) | copy-start | bytes 24580
  30.7 20.6 %copy-start.5 = (s32[14,7]{0,1:T(8,128)S(1)}, s32[14,7]{0,1:T(8,128)}, u32[]{:S(2)}) copy-start(s32[14,7]{0,1:T(8,128)} %param.19) | copy-start | bytes 1180
  30.7 20.6 %copy-start.6 = (f32[14,7]{0,1:T(8,128)S(1)}, f32[14,7]{0,1:T(8,128)}, u32[]{:S(2)}) copy-start(f32[14,7]{0,1:T(8,128)} %param.14) | copy-start | bytes 1180

commit v7 on v6

--- a/solution.py
+++ b/solution.py
@@ -18,6 +18,7 @@
 PADDED = 24
 INFLATION = 1.1
 COST = pl.CostEstimate(flops=1 << 20, bytes_accessed=4 << 20, transcendentals=0)
+ROOM = 40
 PITCH = 16
 
 SWAPS = ((-3, 3, -3, 3), (-2, -2, 2, 2), (-1, -3, 3, 1))
@@ -112,7 +113,7 @@
 
 
 def own_table_kernel(
-    old_ref, new_ref, own_ref, background_ref, table_ref, state_rows
+    old_ref, new_ref, own_ref, background_ref, out_ref, table_ref, state_rows, sem
 ):
     me = lax.axis_index("tile")
     old_start, old_end, new_start = old_ref[me], old_ref[me + 1], new_ref[me]
@@ -130,11 +131,14 @@
         rows = [state_rows[c, pl.ds(at, members, stride=PITCH), :] for c in range(pieces)]
         for c in range(0, pieces, 2):
             table_ref[(LIVE + HPEER * HCAP + i * pieces + c) // 2] = paired(rows[c], rows[c + 1])
+    copy = pltpu.make_async_copy(table_ref, out_ref.at[0], sem)
+    copy.start()
+    copy.wait()
 
 
 def table_kernel(old_ref, new_ref, halo_ref, stays_ref, block_ref, *refs):
     swap_refs, (out_ref, pulled_ref, table_ref, fetch_sem, sems) = refs[:-5], refs[-5:]
-    fetch = pltpu.make_async_copy(stays_ref, table_ref, fetch_sem)
+    fetch = pltpu.make_async_copy(stays_ref.at[0], table_ref, fetch_sem)
     fetch.start()
     devices = new_ref.shape[0] - 1
     me = lax.axis_index("tile")
@@ -217,7 +221,9 @@
 
 
 def dot3(a, b):
-    return dot(a[0], b[0]) + (dot(a[0], b[1]) + dot(a[1], b[0]))
+    rows = a[0].shape[0]
+    both = dot(jnp.concatenate(a, axis=0), b[0])
+    return both[:rows] + (both[rows:] + dot(a[0], b[1]))
 
 
 def analysis_kernel(
@@ -388,10 +394,14 @@
     table_shape = ((tiles + LIVE * pieces) // 2, 2 * members, obs_slots)
     stays = pl.pallas_call(
         own_table_kernel,
-        out_shape=jax.ShapeDtypeStruct(table_shape, BF16),
+        out_shape=jax.ShapeDtypeStruct((ROOM, *table_shape), BF16),
         in_specs=[smem] * 2 + [vmem] * 2,
-        out_specs=vmem,
-        scratch_shapes=[VMEM((pieces, members * PITCH, obs_slots), F32)],
+        out_specs=pl.BlockSpec(memory_space=pl.ANY),
+        scratch_shapes=[
+            VMEM(table_shape, BF16),
+            VMEM((pieces, members * PITCH, obs_slots), F32),
+            pltpu.SemaphoreType.DMA,
+        ],
         compiler_params=params(56),
         cost_estimate=COST,
     )(old_split, new_split, own, background)
@@ -408,7 +418,7 @@
             pltpu.SemaphoreType.DMA,
             pltpu.SemaphoreType.DMA((ranks,)),
         ],
-        compiler_params=params(16),
+        compiler_params=params(50),
     )(old_split, new_split, halo_tiles, stays, block, *arrived)
     table = lax.all_to_all(table, "mem", 0, 0, tiled=True)
 

time: 58 us -> 57.7 us (level)
  local copies, waits for them, and re-layouts: 0.99 us -> 0.04 us
  Pallas kernels: 11.8 us -> 12.4 us
    unnamed x14 -> x12, local copies, waits for them, and re-layouts: 0.99 us -> 0.04 us
    pallas_call x1, Pallas kernels: 1.48 us -> 2.21 us  [shards(): pl.pallas_call(table_kernel, out_shape=(jax.ShapeDtypeStruct((ranks, *tab...]
where the time goes in v7:
time: 57.7 us; the launch traced here: 57.1 us
  starting transfers between devices  20.7 us (36%)
  blocking collectives  20.7 us (36%)
  Pallas kernels  12.4 us (21%)
  waiting for transfers between devices  3.09 us (5%)
    all_to_all x1, blocking collectives, shards(): table = lax.all_to_all(table, 'mem', 0, 0, tiled=True)  20.7 us
    ppermute x3, starting transfers between devices, shards(): arrived.append(lax.ppermute(value, 'tile', pairs))  17.1 us
    pallas_call x1, Pallas kernels, shards(): pl.pallas_call(analysis_kernel, out_shape=jax.ShapeDtypeStruct((members,...  5.95 us
    all_to_all x1, starting transfers between devices, shards(): lax.all_to_all(block, 'tile', 0, 0, axis_index_groups=groups, tiled=True)  3.66 us
    ppermute x3, waiting for transfers between devices, shards(): arrived.append(lax.ppermute(value, 'tile', pairs))  3.09 us
    pallas_call x1, Pallas kernels, shards(): pl.pallas_call(table_kernel, out_shape=(jax.ShapeDtypeStruct((ranks, *tab...  2.21 us
    pallas_call x1, Pallas kernels, shards(): pl.pallas_call(pack_kernel, out_shape=(tile_blocks(LIVE), jax.ShapeDtypeS...  2.21 us
    pallas_call x1, Pallas kernels, shards(): pl.pallas_call(own_table_kernel, out_shape=jax.ShapeDtypeStruct((ROOM, *t...  2.03 us
  transfers between devices with their start and end apart: 4, of which 2 were waited for; matrix products, arithmetic and copies ran while one was open for 0% of the time, Pallas kernels for 4%

profile of v7, /device:TPU:56, one launch (start us, length us, event | category | flops | bytes accessed | tf_op | source)
XLA Modules:
  0.0 57.1 jit_solution(16760698710490171111)
XLA Ops:
  0.0 2.2 %shard_map.100 = (bf16[10,24,128]{2,1,0:T(8,128)(2,1)}, f32[16,128]{1,0:T(8,128)}, bf16[4,12,24,128]{3,2,1,0:T(8,128)(2,1)}, bf16[4,24,128]{2,1,0:T(8,128)(2,1)}...) custom-call(s32[14]{0:T(128)} %count_ref.1, s32[129]{0:T(256)} %old_ref.5, s32[129]{0:T(256)} %new_ref.7, ...), custom_call_target="tpu_custom_call" | custom-call | tf_op jit(solution)/shard_map/pallas_call | solution.py:367
  2.2 3.7 %all-to-all-start = ((bf16[4,12,24,128]{3,2,1,0:T(8,128)(2,1)}), bf16[4,12,24,128]{3,2,1,0:T(8,128)(2,1)S(1)}, u32[]{:S(2)}, u32[]{:S(2)}) async-start(bf16[4,12,24,128]{3,2,1,0:T(8,128)(2,1)} %get-tuple-element.15), calls=%async_computation | async-start | bytes 589824 | tf_op jit(solution)/shard_map/all_to_all | solution.py:387
  5.9 11.8 %collective-permute-start.2 = (bf16[12,24,128]{2,1,0:T(8,128)(2,1)}, bf16[12,24,128]{2,1,0:T(8,128)(2,1)S(1)}, u32[]{:S(2)}, u32[]{:S(2)}) collective-permute-start(bf16[12,24,128]{2,1,0:T(8,128)(2,1)} %get-tuple-element.18), channel_id=1, source_target_pairs={{8,20},{12,16},{16,12},{20,8},{24,36},{28,32},{32,28},{36,24},{40,... | collective-permute-start | bytes 221192 | tf_op jit(solution)/shard_map/ppermute | solution.py:392
  17.7 2.4 %collective-permute-start = (bf16[4,24,128]{2,1,0:T(8,128)(2,1)}, bf16[4,24,128]{2,1,0:T(8,128)(2,1)S(1)}, u32[]{:S(2)}, u32[]{:S(2)}) collective-permute-start(bf16[4,24,128]{2,1,0:T(8,128)(2,1)} %get-tuple-element.16), channel_id=1, source_target_pairs={{4,16},{12,24},{16,4},{20,32},{24,12},{28,40},{32,20},{36,48},{40,... | collective-permute-start | bytes 73736 | tf_op jit(solution)/shard_map/ppermute | solution.py:392
  20.1 2.9 %collective-permute-start.1 = (bf16[4,24,128]{2,1,0:T(8,128)(2,1)}, bf16[4,24,128]{2,1,0:T(8,128)(2,1)S(1)}, u32[]{:S(2)}, u32[]{:S(2)}) collective-permute-start(bf16[4,24,128]{2,1,0:T(8,128)(2,1)} %get-tuple-element.17), channel_id=1, source_target_pairs={{8,16},{12,20},{16,8},{20,12},{24,32},{28,36},{32,24},{36,28},{40,... | collective-permute-start | bytes 73736 | tf_op jit(solution)/shard_map/ppermute | solution.py:392
  23.0 0.0 copy-start
  23.0 0.0 copy-start.1
  23.0 0.0 copy-start.2
  23.0 2.0 %shard_map.101.stays_ref = bf16[40,31,40,128]{3,2,1,0:T(8,128)(2,1)} custom-call(s32[129]{0:T(256)} %old_ref.5, s32[129]{0:T(256)} %new_ref.7, bf16[10,24,128]{2,1,0:T(8,128)(2,1)} %get-tuple-element.14.own_ref, bf16[20,14,512]{2,1,0:T(8,128)(2,1)} %bitcast.11), custom_call_target="tpu_custom_call" | custom-call | flops 1048576 | bytes 4194304 | tf_op jit(solution)/shard_map/pallas_call | solution.py:395
  25.0 1.0 %collective-permute-done.refs_0_ = bf16[4,24,128]{2,1,0:T(8,128)(2,1)S(1)} collective-permute-done((bf16[4,24,128]{2,1,0:T(8,128)(2,1)}, bf16[4,24,128]{2,1,0:T(8,128)(2,1)S(1)}, u32[]{:S(2)}, u32[]{:S(2)}) %collective-permute-start) | collective-permute-done | bytes 24608 | tf_op jit(solution)/shard_map/ppermute | solution.py:392
  26.0 2.1 %collective-permute-done.1.refs_1_ = bf16[4,24,128]{2,1,0:T(8,128)(2,1)S(1)} collective-permute-done((bf16[4,24,128]{2,1,0:T(8,128)(2,1)}, bf16[4,24,128]{2,1,0:T(8,128)(2,1)S(1)}, u32[]{:S(2)}, u32[]{:S(2)}) %collective-permute-start.1) | collective-permute-done | bytes 24608 | tf_op jit(solution)/shard_map/ppermute | solution.py:392
  28.1 0.0 collective-permute-done.2.refs_2_
  28.1 0.0 all-to-all-done.block_ref
  28.1 0.0 copy-done
  28.1 0.0 copy-done.1
  28.2 0.0 copy-done.2
  28.2 2.2 %shard_map.102 = (bf16[4,31,40,128]{3,2,1,0:T(8,128)(2,1)S(1)}, f32[16,128]{1,0:T(8,128)S(1)}) custom-call(s32[129]{0:T(256)S(1)} %copy-done.2, s32[129]{0:T(256)S(1)} %copy-done.1, s32[12,128]{1,0:T(8,128)S(1)} %bitcast.7, bf16[40,31,40,128]{3,2,1,0:T(8,128)(2,1)} %shard_map.101.stays_ref, bf16[4,12,24,128]{3,2,1,0:T(8,128)(2,1)S(1)} %all-to-all-done.block_ref, ...), custom_call_target="tpu_custom_call" | custom-call | tf_op jit(solution)/shard_map/pallas_call | solution.py:408
  30.4 0.0 copy-start.3
  30.4 0.0 copy-start.4
  30.4 0.0 copy-start.5
  30.4 20.7 %all_to_all.10.table_ref = bf16[4,31,40,128]{3,2,1,0:T(8,128)(2,1)S(1)} all-to-all(bf16[4,31,40,128]{3,2,1,0:T(8,128)(2,1)S(1)} %get-tuple-element.20), channel_id=1, replica_groups=mesh['tile'=128,'mem'=4] {'mem'}, dimensions={0} | all-to-all | bytes 2539520 | tf_op jit(solution)/shard_map/all_to_all | solution.py:423
  51.1 0.0 copy-done.3
  51.1 0.0 copy-done.4
  51.1 0.0 copy-done.5
  51.1 6.0 %shard_map.103 = bf16[20,14,512]{2,1,0:T(8,128)(2,1)} custom-call(s32[7,14]{1,0:T(8,128)S(1)} %bitcast.8, f32[7,14]{1,0:T(8,128)S(1)} %bitcast.9, s32[129]{0:T(256)S(1)} %copy-done.1, f32[16,128]{1,0:T(8,128)S(1)} %copy-done.3, f32[16,128]{1,0:T(8,128)S(1)} %get-tuple-element.19.halo_pulled_ref, bf16[4,31,40,128]{3,2,1,0:T(8,128)(2,1)S(1)} %all_to_all.10.table_ref), custom_call_target="tpu_custom_call" | custom-call | tf_op jit(solution)/shard_map/pallas_call | solution.py:426
Async XLA Ops:
  2.2 25.9 %all-to-all-start = ((bf16[4,12,24,128]{3,2,1,0:T(8,128)(2,1)}), bf16[4,12,24,128]{3,2,1,0:T(8,128)(2,1)S(1)}, u32[]{:S(2)}, u32[]{:S(2)}) async-start(bf16[4,12,24,128]{3,2,1,0:T(8,128)(2,1)} %get-tuple-element.15), calls=%async_computation | async-start | bytes 589824 | tf_op jit(solution)/shard_map/all_to_all | solution.py:387
  5.9 22.3 %collective-permute-start.2 = (bf16[12,24,128]{2,1,0:T(8,128)(2,1)}, bf16[12,24,128]{2,1,0:T(8,128)(2,1)S(1)}, u32[]{:S(2)}, u32[]{:S(2)}) collective-permute-start(bf16[12,24,128]{2,1,0:T(8,128)(2,1)} %get-tuple-element.18), channel_id=1, source_target_pairs={{8,20},{12,16},{16,12},{20,8},{24,36},{28,32},{32,28},{36,24},{40,... | collective-permute-start | bytes 221192 | tf_op jit(solution)/shard_map/ppermute | solution.py:392
  17.7 8.4 %collective-permute-start = (bf16[4,24,128]{2,1,0:T(8,128)(2,1)}, bf16[4,24,128]{2,1,0:T(8,128)(2,1)S(1)}, u32[]{:S(2)}, u32[]{:S(2)}) collective-permute-start(bf16[4,24,128]{2,1,0:T(8,128)(2,1)} %get-tuple-element.16), channel_id=1, source_target_pairs={{4,16},{12,24},{16,4},{20,32},{24,12},{28,40},{32,20},{36,48},{40,... | collective-permute-start | bytes 73736 | tf_op jit(solution)/shard_map/ppermute | solution.py:392
  20.1 8.0 %collective-permute-start.1 = (bf16[4,24,128]{2,1,0:T(8,128)(2,1)}, bf16[4,24,128]{2,1,0:T(8,128)(2,1)S(1)}, u32[]{:S(2)}, u32[]{:S(2)}) collective-permute-start(bf16[4,24,128]{2,1,0:T(8,128)(2,1)} %get-tuple-element.17), channel_id=1, source_target_pairs={{8,16},{12,20},{16,8},{20,12},{24,32},{28,36},{32,24},{36,28},{40,... | collective-permute-start | bytes 73736 | tf_op jit(solution)/shard_map/ppermute | solution.py:392
  23.0 5.2 %copy-start = (s32[128,12]{0,1:T(8,128)S(1)}, s32[128,12]{0,1:T(8,128)}, u32[]{:S(2)}) copy-start(s32[128,12]{0,1:T(8,128)} %param.18) | copy-start | bytes 18436
  23.0 5.2 %copy-start.1 = (s32[129]{0:T(256)S(1)}, s32[129]{0:T(256)}, u32[]{:S(2)}) copy-start(s32[129]{0:T(256)} %new_ref.7) | copy-start | bytes 1552
  23.0 5.2 %copy-start.2 = (s32[129]{0:T(256)S(1)}, s32[129]{0:T(256)}, u32[]{:S(2)}) copy-start(s32[129]{0:T(256)} %old_ref.5) | copy-start | bytes 1552
  30.4 20.7 %copy-start.3 = (f32[16,128]{1,0:T(8,128)S(1)}, f32[16,128]{1,0:T(8,128)}, u32[]{:S(2)}) copy-start(f32[16,128]{1,0:T(8,128)} %get-tuple-element.13.own_pulled_ref) | copy-start | bytes 24580
  30.4 20.7 %copy-start.4 = (s32[14,7]{0,1:T(8,128)S(1)}, s32[14,7]{0,1:T(8,128)}, u32[]{:S(2)}) copy-start(s32[14,7]{0,1:T(8,128)} %param.19) | copy-start | bytes 1180
  30.4 20.7 %copy-start.5 = (f32[14,7]{0,1:T(8,128)S(1)}, f32[14,7]{0,1:T(8,128)}, u32[]{:S(2)}) copy-start(f32[14,7]{0,1:T(8,128)} %param.14) | copy-start | bytes 1180

commit v8 on v7

--- a/solution.py
+++ b/solution.py
@@ -291,21 +291,21 @@
         half = 0.5 * (diagonal - root)
         system_ref[i] = root
         inverse_ref[i] = diagonal + half
-        change.append(split(half))
+        change.append(half.astype(BF16))
 
     for step in range(NS_ITERS):
         if step:
             change = []
             for i in range(LIVE):
                 product = dot3(split(inverse_ref[i]), split(system_ref[i]))
-                change.append(split(0.5 * (diagonal - product)))
+                change.append((0.5 * (diagonal - product)).astype(BF16))
         for i in range(LIVE):
             if step:
                 inverse = inverse_ref[i]
-                inverse_ref[i] = inverse + dot3(change[i], split(inverse))
+                inverse_ref[i] = inverse + dot(change[i], inverse.astype(BF16))
             if step < NS_ITERS - 1:
                 root = system_ref[i]
-                system_ref[i] = root + dot3(split(root), change[i])
+                system_ref[i] = root + dot(root.astype(BF16), change[i])
 
     first = pl.multiple_of(rank * PITCH, 8)
     last = pl.multiple_of(ranks * PITCH + rank // 2 * (2 * rest), 8)

time: 57.7 us -> 56.7 us (0.983)
  Pallas kernels: 12.4 us -> 11.4 us
    pallas_call x1, Pallas kernels: 5.95 us -> 4.95 us  [shards(): pl.pallas_call(analysis_kernel, out_shape=jax.ShapeDtypeStruct((members,...]
where the time goes in v8:
time: 56.7 us; the launch traced here: 56 us
  starting transfers between devices  20.7 us (37%)
  blocking collectives  20.7 us (37%)
  Pallas kernels  11.4 us (20%)
  waiting for transfers between devices  3.09 us (5%)
    all_to_all x1, blocking collectives, shards(): table = lax.all_to_all(table, 'mem', 0, 0, tiled=True)  20.7 us
    ppermute x3, starting transfers between devices, shards(): arrived.append(lax.ppermute(value, 'tile', pairs))  17.1 us
    pallas_call x1, Pallas kernels, shards(): pl.pallas_call(analysis_kernel, out_shape=jax.ShapeDtypeStruct((members,...  4.95 us
    all_to_all x1, starting transfers between devices, shards(): lax.all_to_all(block, 'tile', 0, 0, axis_index_groups=groups, tiled=True)  3.66 us
    ppermute x3, waiting for transfers between devices, shards(): arrived.append(lax.ppermute(value, 'tile', pairs))  3.09 us
    pallas_call x1, Pallas kernels, shards(): pl.pallas_call(table_kernel, out_shape=(jax.ShapeDtypeStruct((ranks, *tab...  2.21 us
    pallas_call x1, Pallas kernels, shards(): pl.pallas_call(pack_kernel, out_shape=(tile_blocks(LIVE), jax.ShapeDtypeS...  2.21 us
    pallas_call x1, Pallas kernels, shards(): pl.pallas_call(own_table_kernel, out_shape=jax.ShapeDtypeStruct((ROOM, *t...  2.03 us
  transfers between devices with their start and end apart: 4, of which 2 were waited for; matrix products, arithmetic and copies ran while one was open for 0% of the time, Pallas kernels for 4%

profile of v8, /device:TPU:56, one launch (start us, length us, event | category | flops | bytes accessed | tf_op | source)
XLA Modules:
  0.0 56.0 jit_solution(18272554762254918151)
XLA Ops:
  0.0 2.2 %shard_map.100 = (bf16[10,24,128]{2,1,0:T(8,128)(2,1)}, f32[16,128]{1,0:T(8,128)}, bf16[4,12,24,128]{3,2,1,0:T(8,128)(2,1)}, bf16[4,24,128]{2,1,0:T(8,128)(2,1)}...) custom-call(s32[14]{0:T(128)} %count_ref.1, s32[129]{0:T(256)} %old_ref.5, s32[129]{0:T(256)} %new_ref.7, ...), custom_call_target="tpu_custom_call" | custom-call | tf_op jit(solution)/shard_map/pallas_call | solution.py:367
  2.2 3.7 %all-to-all-start = ((bf16[4,12,24,128]{3,2,1,0:T(8,128)(2,1)}), bf16[4,12,24,128]{3,2,1,0:T(8,128)(2,1)S(1)}, u32[]{:S(2)}, u32[]{:S(2)}) async-start(bf16[4,12,24,128]{3,2,1,0:T(8,128)(2,1)} %get-tuple-element.15), calls=%async_computation | async-start | bytes 589824 | tf_op jit(solution)/shard_map/all_to_all | solution.py:387
  5.9 11.8 %collective-permute-start.2 = (bf16[12,24,128]{2,1,0:T(8,128)(2,1)}, bf16[12,24,128]{2,1,0:T(8,128)(2,1)S(1)}, u32[]{:S(2)}, u32[]{:S(2)}) collective-permute-start(bf16[12,24,128]{2,1,0:T(8,128)(2,1)} %get-tuple-element.18), channel_id=1, source_target_pairs={{8,20},{12,16},{16,12},{20,8},{24,36},{28,32},{32,28},{36,24},{40,... | collective-permute-start | bytes 221192 | tf_op jit(solution)/shard_map/ppermute | solution.py:392
  17.7 2.4 %collective-permute-start = (bf16[4,24,128]{2,1,0:T(8,128)(2,1)}, bf16[4,24,128]{2,1,0:T(8,128)(2,1)S(1)}, u32[]{:S(2)}, u32[]{:S(2)}) collective-permute-start(bf16[4,24,128]{2,1,0:T(8,128)(2,1)} %get-tuple-element.16), channel_id=1, source_target_pairs={{4,16},{12,24},{16,4},{20,32},{24,12},{28,40},{32,20},{36,48},{40,... | collective-permute-start | bytes 73736 | tf_op jit(solution)/shard_map/ppermute | solution.py:392
  20.1 2.9 %collective-permute-start.1 = (bf16[4,24,128]{2,1,0:T(8,128)(2,1)}, bf16[4,24,128]{2,1,0:T(8,128)(2,1)S(1)}, u32[]{:S(2)}, u32[]{:S(2)}) collective-permute-start(bf16[4,24,128]{2,1,0:T(8,128)(2,1)} %get-tuple-element.17), channel_id=1, source_target_pairs={{8,16},{12,20},{16,8},{20,12},{24,32},{28,36},{32,24},{36,28},{40,... | collective-permute-start | bytes 73736 | tf_op jit(solution)/shard_map/ppermute | solution.py:392
  23.0 0.0 copy-start
  23.0 0.0 copy-start.1
  23.0 0.0 copy-start.2
  23.0 2.0 %shard_map.101.stays_ref = bf16[40,31,40,128]{3,2,1,0:T(8,128)(2,1)} custom-call(s32[129]{0:T(256)} %old_ref.5, s32[129]{0:T(256)} %new_ref.7, bf16[10,24,128]{2,1,0:T(8,128)(2,1)} %get-tuple-element.14.own_ref, bf16[20,14,512]{2,1,0:T(8,128)(2,1)} %bitcast.11), custom_call_target="tpu_custom_call" | custom-call | flops 1048576 | bytes 4194304 | tf_op jit(solution)/shard_map/pallas_call | solution.py:395
  25.0 1.0 %collective-permute-done.refs_0_ = bf16[4,24,128]{2,1,0:T(8,128)(2,1)S(1)} collective-permute-done((bf16[4,24,128]{2,1,0:T(8,128)(2,1)}, bf16[4,24,128]{2,1,0:T(8,128)(2,1)S(1)}, u32[]{:S(2)}, u32[]{:S(2)}) %collective-permute-start) | collective-permute-done | bytes 24608 | tf_op jit(solution)/shard_map/ppermute | solution.py:392
  26.0 2.1 %collective-permute-done.1.refs_1_ = bf16[4,24,128]{2,1,0:T(8,128)(2,1)S(1)} collective-permute-done((bf16[4,24,128]{2,1,0:T(8,128)(2,1)}, bf16[4,24,128]{2,1,0:T(8,128)(2,1)S(1)}, u32[]{:S(2)}, u32[]{:S(2)}) %collective-permute-start.1) | collective-permute-done | bytes 24608 | tf_op jit(solution)/shard_map/ppermute | solution.py:392
  28.1 0.0 collective-permute-done.2.refs_2_
  28.1 0.0 all-to-all-done.block_ref
  28.1 0.0 copy-done
  28.1 0.0 copy-done.1
  28.2 0.0 copy-done.2
  28.2 2.2 %shard_map.102 = (bf16[4,31,40,128]{3,2,1,0:T(8,128)(2,1)S(1)}, f32[16,128]{1,0:T(8,128)S(1)}) custom-call(s32[129]{0:T(256)S(1)} %copy-done.2, s32[129]{0:T(256)S(1)} %copy-done.1, s32[12,128]{1,0:T(8,128)S(1)} %bitcast.7, bf16[40,31,40,128]{3,2,1,0:T(8,128)(2,1)} %shard_map.101.stays_ref, bf16[4,12,24,128]{3,2,1,0:T(8,128)(2,1)S(1)} %all-to-all-done.block_ref, ...), custom_call_target="tpu_custom_call" | custom-call | tf_op jit(solution)/shard_map/pallas_call | solution.py:408
  30.4 0.0 copy-start.3
  30.4 0.0 copy-start.4
  30.4 0.0 copy-start.5
  30.4 20.7 %all_to_all.10.table_ref = bf16[4,31,40,128]{3,2,1,0:T(8,128)(2,1)S(1)} all-to-all(bf16[4,31,40,128]{3,2,1,0:T(8,128)(2,1)S(1)} %get-tuple-element.20), channel_id=1, replica_groups=mesh['tile'=128,'mem'=4] {'mem'}, dimensions={0} | all-to-all | bytes 2539520 | tf_op jit(solution)/shard_map/all_to_all | solution.py:423
  51.1 0.0 copy-done.3
  51.1 0.0 copy-done.4
  51.1 0.0 copy-done.5
  51.1 5.0 %shard_map.103 = bf16[20,14,512]{2,1,0:T(8,128)(2,1)} custom-call(s32[7,14]{1,0:T(8,128)S(1)} %bitcast.8, f32[7,14]{1,0:T(8,128)S(1)} %bitcast.9, s32[129]{0:T(256)S(1)} %copy-done.1, f32[16,128]{1,0:T(8,128)S(1)} %copy-done.3, f32[16,128]{1,0:T(8,128)S(1)} %get-tuple-element.19.halo_pulled_ref, bf16[4,31,40,128]{3,2,1,0:T(8,128)(2,1)S(1)} %all_to_all.10.table_ref), custom_call_target="tpu_custom_call" | custom-call | tf_op jit(solution)/shard_map/pallas_call | solution.py:426
Async XLA Ops:
  2.2 25.9 %all-to-all-start = ((bf16[4,12,24,128]{3,2,1,0:T(8,128)(2,1)}), bf16[4,12,24,128]{3,2,1,0:T(8,128)(2,1)S(1)}, u32[]{:S(2)}, u32[]{:S(2)}) async-start(bf16[4,12,24,128]{3,2,1,0:T(8,128)(2,1)} %get-tuple-element.15), calls=%async_computation | async-start | bytes 589824 | tf_op jit(solution)/shard_map/all_to_all | solution.py:387
  5.9 22.3 %collective-permute-start.2 = (bf16[12,24,128]{2,1,0:T(8,128)(2,1)}, bf16[12,24,128]{2,1,0:T(8,128)(2,1)S(1)}, u32[]{:S(2)}, u32[]{:S(2)}) collective-permute-start(bf16[12,24,128]{2,1,0:T(8,128)(2,1)} %get-tuple-element.18), channel_id=1, source_target_pairs={{8,20},{12,16},{16,12},{20,8},{24,36},{28,32},{32,28},{36,24},{40,... | collective-permute-start | bytes 221192 | tf_op jit(solution)/shard_map/ppermute | solution.py:392
  17.7 8.4 %collective-permute-start = (bf16[4,24,128]{2,1,0:T(8,128)(2,1)}, bf16[4,24,128]{2,1,0:T(8,128)(2,1)S(1)}, u32[]{:S(2)}, u32[]{:S(2)}) collective-permute-start(bf16[4,24,128]{2,1,0:T(8,128)(2,1)} %get-tuple-element.16), channel_id=1, source_target_pairs={{4,16},{12,24},{16,4},{20,32},{24,12},{28,40},{32,20},{36,48},{40,... | collective-permute-start | bytes 73736 | tf_op jit(solution)/shard_map/ppermute | solution.py:392
  20.1 8.0 %collective-permute-start.1 = (bf16[4,24,128]{2,1,0:T(8,128)(2,1)}, bf16[4,24,128]{2,1,0:T(8,128)(2,1)S(1)}, u32[]{:S(2)}, u32[]{:S(2)}) collective-permute-start(bf16[4,24,128]{2,1,0:T(8,128)(2,1)} %get-tuple-element.17), channel_id=1, source_target_pairs={{8,16},{12,20},{16,8},{20,12},{24,32},{28,36},{32,24},{36,28},{40,... | collective-permute-start | bytes 73736 | tf_op jit(solution)/shard_map/ppermute | solution.py:392
  23.0 5.2 %copy-start = (s32[128,12]{0,1:T(8,128)S(1)}, s32[128,12]{0,1:T(8,128)}, u32[]{:S(2)}) copy-start(s32[128,12]{0,1:T(8,128)} %param.18) | copy-start | bytes 18436
  23.0 5.2 %copy-start.1 = (s32[129]{0:T(256)S(1)}, s32[129]{0:T(256)}, u32[]{:S(2)}) copy-start(s32[129]{0:T(256)} %new_ref.7) | copy-start | bytes 1552
  23.0 5.2 %copy-start.2 = (s32[129]{0:T(256)S(1)}, s32[129]{0:T(256)}, u32[]{:S(2)}) copy-start(s32[129]{0:T(256)} %old_ref.5) | copy-start | bytes 1552
  30.4 20.7 %copy-start.3 = (f32[16,128]{1,0:T(8,128)S(1)}, f32[16,128]{1,0:T(8,128)}, u32[]{:S(2)}) copy-start(f32[16,128]{1,0:T(8,128)} %get-tuple-element.13.own_pulled_ref) | copy-start | bytes 24580
  30.4 20.7 %copy-start.4 = (s32[14,7]{0,1:T(8,128)S(1)}, s32[14,7]{0,1:T(8,128)}, u32[]{:S(2)}) copy-start(s32[14,7]{0,1:T(8,128)} %param.19) | copy-start | bytes 1180
  30.4 20.7 %copy-start.5 = (f32[14,7]{0,1:T(8,128)S(1)}, f32[14,7]{0,1:T(8,128)}, u32[]{:S(2)}) copy-start(f32[14,7]{0,1:T(8,128)} %param.14) | copy-start | bytes 1180
